TPU v7x, 32 devices: a whole 2x2x4 slice. The times are simulated.
32 devices in a mesh: dp: 8 (over z, y), tensor: 4 (over x, core).
Axes of the slice: x: 2, y: 2, z: 4, core: 2. Of those that a mesh axis runs over, the one named last changes fastest.
Arguments:
- block_input: bfloat16 [8192, 1792], P(('dp', 'tensor')), may hold values from -6 to 6
- cotangent: float32 [8192, 1792], P(('dp', 'tensor')), may hold values from -6 to 6
- teacher: bfloat16 [8192, 1792], P(('dp', 'tensor')), may hold values from -6 to 6
- segments: int32 [8192], P('dp'), may hold values from 0 to 8191, as said below
- valid_mask: int32 [8192], P(('dp', 'tensor')), may hold values from 0 to 1
- query_weight: bfloat16 [1792, 1792], P('dp', 'tensor'), may hold values from -0.125 to 0.125
- key_weight: bfloat16 [1792, 1792], P('dp', 'tensor'), may hold values from -0.125 to 0.125
- value_weight: bfloat16 [1792, 1792], P('dp', 'tensor'), may hold values from -0.125 to 0.125
- mixgate_weight: bfloat16 [1792, 1792], P('dp', 'tensor'), may hold values from -0.125 to 0.125
- output_weight: bfloat16 [1792, 1792], P('tensor', 'dp'), may hold values from -0.125 to 0.125
- conv_weight: float32 [3, 1792], replicated, may hold values from -3 to 3
- gain_mixer: float32 [1792], replicated, may hold values from 0.5 to 1.5
- gain_feed: float32 [1792], replicated, may hold values from 0.5 to 1.5
- gate_weight: bfloat16 [1792, 4864], P('dp', 'tensor'), may hold values from -0.125 to 0.125
- up_weight: bfloat16 [1792, 4864], P('dp', 'tensor'), may hold values from -0.125 to 0.125
- down_weight: bfloat16 [4864, 1792], P('tensor', 'dp'), may hold values from -0.078125 to 0.078125
Outputs:
- mean_loss: float32 [], replicated
- activations: float32 [8192, 1792], P(('dp', 'tensor'))
- input_grad: float32 [8192, 1792], P(('dp', 'tensor'))
- query_grad: float32 [1792, 1792], P('dp', 'tensor')
- key_grad: float32 [1792, 1792], P('dp', 'tensor')
- value_grad: float32 [1792, 1792], P('dp', 'tensor')
- mixgate_grad: float32 [1792, 1792], P('dp', 'tensor')
- output_grad: float32 [1792, 1792], P('tensor', 'dp')
- conv_grad: float32 [3, 1792], replicated
- gainmix_grad: float32 [1792], replicated
- gainfeed_grad: float32 [1792], replicated
- gate_grad: float32 [1792, 4864], P('dp', 'tensor')
- up_grad: float32 [1792, 4864], P('dp', 'tensor')
- down_grad: float32 [4864, 1792], P('tensor', 'dp')
Inputs may be any that keep to these rules, and one draw needn't show every extreme that they name: `segments`: segment ids never fall; each sequence of 1024 tokens begins a new document, and one document of each sequence covers all its tokens but fewer than 128 at each end.
All inputs are finite; a program needn't handle non-finite values.
Results may differ from a plain program's by a relative error of at most 0.02.
Values may be sent and summed in bfloat16 or wider, within the bound.
A program may use at most 192 MiB of HBM per device.

v0:
```python
import jax
import jax.numpy as jnp
from jax import lax
from jax.sharding import PartitionSpec as P

D = 1792
HEAD_DIM = 64
WINDOW = 64
CONV = 3
BLOCK = 512


EPS = 1e-05


def rms_scale(values):
    return lax.rsqrt(jnp.mean(values * values, axis=1, keepdims=True) + EPS)


def rows_inner(matrix_left, matrix_right):
    return lax.dot_general(
        matrix_left, matrix_right, (((0,), (0,)), ((), ())), preferred_element_type=jnp.float32
    )


def cols_inner(matrix_left, matrix_right):
    return lax.dot_general(
        matrix_left, matrix_right, (((1,), (1,)), ((), ())), preferred_element_type=jnp.float32
    )


def shift_down(values, segments, offset):
    if offset == 0:
        return values
    shifted = jnp.concatenate(
        [jnp.zeros((offset, values.shape[1]), values.dtype), values[: values.shape[0] - offset]],
        axis=0,
    )
    same_doc = jnp.concatenate(
        [jnp.zeros((offset,), bool), segments[offset:] == segments[:-offset]]
    )
    return jnp.where(same_doc[:, None], shifted, 0.0)


def shift_up(values, segments, offset):
    if offset == 0:
        return values
    shifted = jnp.concatenate(
        [values[offset:], jnp.zeros((offset, values.shape[1]), values.dtype)], axis=0
    )
    same_doc = jnp.concatenate(
        [segments[:-offset] == segments[offset:], jnp.zeros((offset,), bool)]
    )
    return jnp.where(same_doc[:, None], shifted, 0.0)


def pad_front(array, fill_value):
    front = jnp.full((WINDOW,) + array.shape[1:], fill_value, array.dtype)
    return jnp.concatenate([front, array], axis=0)


def block_setup(queries, key_pad, seg_pad, segments, row_start, head_count):
    score_scale = HEAD_DIM ** (-0.5)
    query_rows = lax.dynamic_slice_in_dim(queries, row_start, BLOCK, 0).reshape(
        BLOCK, head_count, HEAD_DIM
    )
    key_block = lax.dynamic_slice_in_dim(key_pad, row_start, BLOCK + WINDOW, 0).reshape(
        BLOCK + WINDOW, head_count, HEAD_DIM
    )
    seg_rows = lax.dynamic_slice_in_dim(segments, row_start, BLOCK, 0)
    seg_keys = lax.dynamic_slice_in_dim(seg_pad, row_start, BLOCK + WINDOW, 0)
    distance = (
        jnp.arange(BLOCK, dtype=jnp.int32)[:, None]
        + WINDOW
        - jnp.arange(BLOCK + WINDOW, dtype=jnp.int32)[None, :]
    )
    allowed = (distance >= 0) & (distance < WINDOW) & (seg_rows[:, None] == seg_keys[None, :])
    scores = (
        jnp.einsum("qhd,khd->hqk", query_rows, key_block, preferred_element_type=jnp.float32)
        * score_scale
    )
    return (query_rows, key_block, jnp.where(allowed[None], scores, -1e30))


def attend_forward(queries, key_rows, value_rows, segments):
    group_rows, local_width = queries.shape
    head_count = local_width // HEAD_DIM
    key_pad = pad_front(key_rows, 0)
    value_pad = pad_front(value_rows, 0)
    seg_pad = pad_front(segments, -1)

    def one_block(block_index):
        row_start = block_index * BLOCK
        query_rows, key_block, scores = block_setup(
            queries, key_pad, seg_pad, segments, row_start, head_count
        )
        row_max = jnp.max(scores, axis=-1, keepdims=True)
        exponent = jnp.exp(scores - row_max)
        row_total = jnp.sum(exponent, axis=-1, keepdims=True)
        attention = (exponent / row_total).astype(jnp.bfloat16)
        value_block = lax.dynamic_slice_in_dim(value_pad, row_start, BLOCK + WINDOW, 0).reshape(
            BLOCK + WINDOW, head_count, HEAD_DIM
        )
        mixed_rows = jnp.einsum(
            "hqk,khd->qhd", attention, value_block, preferred_element_type=jnp.float32
        )
        return (
            mixed_rows.reshape(BLOCK, local_width),
            row_max[..., 0] + jnp.log(row_total[..., 0]),
        )

    blocks_out, log_totals = lax.map(one_block, jnp.arange(group_rows // BLOCK, dtype=jnp.int32))
    return (blocks_out.reshape(group_rows, local_width), log_totals)


def attend_backward(queries, key_rows, value_rows, segments, log_totals, grad_mixed):
    group_rows, local_width = queries.shape
    head_count = local_width // HEAD_DIM
    score_scale = HEAD_DIM ** (-0.5)
    key_pad = pad_front(key_rows, 0)
    value_pad = pad_front(value_rows, 0)
    seg_pad = pad_front(segments, -1)

    def one_block(accumulated, block_pair):
        block_index, log_block = block_pair
        row_start = block_index * BLOCK
        query_rows, key_block, scores = block_setup(
            queries, key_pad, seg_pad, segments, row_start, head_count
        )
        attention = jnp.exp(scores - log_block[..., None])
        value_block = lax.dynamic_slice_in_dim(value_pad, row_start, BLOCK + WINDOW, 0).reshape(
            BLOCK + WINDOW, head_count, HEAD_DIM
        )
        grad_block = lax.dynamic_slice_in_dim(grad_mixed, row_start, BLOCK, 0).reshape(
            BLOCK, head_count, HEAD_DIM
        )
        grad_attention = jnp.einsum(
            "qhd,khd->hqk", grad_block, value_block, preferred_element_type=jnp.float32
        )
        row_inner = jnp.sum(attention * grad_attention, axis=-1, keepdims=True)
        grad_scores = (attention * (grad_attention - row_inner)).astype(jnp.bfloat16)
        grad_query = (
            jnp.einsum("hqk,khd->qhd", grad_scores, key_block, preferred_element_type=jnp.float32)
            * score_scale
        )
        grad_key = (
            jnp.einsum("hqk,qhd->khd", grad_scores, query_rows, preferred_element_type=jnp.float32)
            * score_scale
        )
        grad_value = jnp.einsum(
            "hqk,qhd->khd",
            attention.astype(jnp.bfloat16),
            grad_block,
            preferred_element_type=jnp.float32,
        )
        key_acc, value_acc = accumulated
        key_acc = lax.dynamic_update_slice_in_dim(
            key_acc,
            lax.dynamic_slice_in_dim(key_acc, row_start, BLOCK + WINDOW, 0)
            + grad_key.reshape(BLOCK + WINDOW, local_width),
            row_start,
            0,
        )
        value_acc = lax.dynamic_update_slice_in_dim(
            value_acc,
            lax.dynamic_slice_in_dim(value_acc, row_start, BLOCK + WINDOW, 0)
            + grad_value.reshape(BLOCK + WINDOW, local_width),
            row_start,
            0,
        )
        return ((key_acc, value_acc), grad_query.astype(jnp.bfloat16).reshape(BLOCK, local_width))

    zeros_pad = jnp.zeros((group_rows + WINDOW, local_width), jnp.float32)
    block_ids = jnp.arange(group_rows // BLOCK, dtype=jnp.int32)
    (key_acc, value_acc), query_blocks = lax.scan(
        one_block, (zeros_pad, zeros_pad), (block_ids, log_totals)
    )
    return (query_blocks.reshape(group_rows, local_width), key_acc[WINDOW:], value_acc[WINDOW:])


def on_device(
    block_input,
    cotangent,
    teacher,
    segments,
    valid_mask,
    query_weight,
    key_weight,
    value_weight,
    mixgate_weight,
    output_weight,
    conv_weight,
    gain_mixer,
    gain_feed,
    gate_weight,
    up_weight,
    down_weight,
):
    gathered = (
        lax.all_gather(query_weight, "dp", axis=0, tiled=True),
        lax.all_gather(key_weight, "dp", axis=0, tiled=True),
        lax.all_gather(value_weight, "dp", axis=0, tiled=True),
        lax.all_gather(mixgate_weight, "dp", axis=0, tiled=True),
        lax.all_gather(output_weight, "dp", axis=1, tiled=True),
        lax.all_gather(gate_weight, "dp", axis=0, tiled=True),
        lax.all_gather(up_weight, "dp", axis=0, tiled=True),
        lax.all_gather(down_weight, "dp", axis=1, tiled=True),
    )
    (
        full_query,
        full_key,
        full_value,
        full_mixgate,
        full_output,
        full_gate,
        full_upward,
        full_down,
    ) = gathered
    local_width = full_query.shape[1]
    column = lax.axis_index("tensor") * local_width
    conv_local = lax.dynamic_slice_in_dim(conv_weight, column, local_width, 1)
    inputs = block_input.astype(jnp.float32)
    scale_one = rms_scale(inputs)
    normed_one = inputs * scale_one
    group_one = lax.all_gather(
        (normed_one * gain_mixer).astype(jnp.bfloat16), "tensor", axis=0, tiled=True
    )
    queries = jnp.dot(group_one, full_query, preferred_element_type=jnp.float32).astype(
        jnp.bfloat16
    )
    key_rows = jnp.dot(group_one, full_key, preferred_element_type=jnp.float32).astype(jnp.bfloat16)
    value_rows = jnp.dot(group_one, full_value, preferred_element_type=jnp.float32).astype(
        jnp.bfloat16
    )
    mix_gate = jnp.dot(group_one, full_mixgate, preferred_element_type=jnp.float32).astype(
        jnp.bfloat16
    )
    attended, log_totals = attend_forward(queries, key_rows, value_rows, segments)
    value_float = value_rows.astype(jnp.float32)
    convolved = jnp.zeros_like(value_float)
    for offset in range(CONV):
        convolved = convolved + conv_local[offset] * shift_down(value_float, segments, offset)
    gate_float = mix_gate.astype(jnp.float32)
    mixer_out = (attended + convolved * gate_float).astype(jnp.bfloat16)
    mixer_part = jnp.dot(mixer_out, full_output, preferred_element_type=jnp.float32)
    hidden = inputs + lax.psum_scatter(mixer_part, "tensor", scatter_dimension=0, tiled=True)
    scale_two = rms_scale(hidden)
    normed_two = hidden * scale_two
    group_two = lax.all_gather(
        (normed_two * gain_feed).astype(jnp.bfloat16), "tensor", axis=0, tiled=True
    )
    gate_value = jnp.dot(group_two, full_gate, preferred_element_type=jnp.float32)
    up_value = jnp.dot(group_two, full_upward, preferred_element_type=jnp.float32)
    sigmoid_gate = jax.nn.sigmoid(gate_value)
    silu_gate = gate_value * sigmoid_gate
    active = (silu_gate * up_value).astype(jnp.bfloat16)
    feed_part = jnp.dot(active, full_down, preferred_element_type=jnp.float32)
    outputs = hidden + lax.psum_scatter(
        feed_part.astype(jnp.bfloat16), "tensor", scatter_dimension=0, tiled=True
    ).astype(jnp.float32)
    target = teacher.astype(jnp.float32)
    valid_rows = valid_mask.astype(jnp.float32)
    deviation = outputs - target
    valid_total, squares = lax.psum(
        (jnp.sum(valid_rows), jnp.sum(valid_rows[:, None] * deviation * deviation)),
        ("dp", "tensor"),
    )
    all_tokens = block_input.shape[0] * lax.axis_size("dp") * lax.axis_size("tensor")
    mean_loss = squares / (valid_total * D)
    grad_out = cotangent + valid_rows[:, None] * deviation * (all_tokens / valid_total)
    (
        back_query,
        back_key,
        back_value,
        back_mixgate,
        back_output,
        back_gate,
        back_upward,
        back_down,
    ) = gathered
    grad_feed = lax.all_gather(grad_out.astype(jnp.bfloat16), "tensor", axis=0, tiled=True)
    down_part = rows_inner(active, grad_feed)
    grad_active = cols_inner(grad_feed, back_down)
    silu_slope = sigmoid_gate * (1.0 + gate_value * (1.0 - sigmoid_gate))
    grad_gate = (grad_active * up_value * silu_slope).astype(jnp.bfloat16)
    grad_upward = (grad_active * silu_gate).astype(jnp.bfloat16)
    gate_part = rows_inner(group_two, grad_gate)
    up_part = rows_inner(group_two, grad_upward)
    grad_normed_two = cols_inner(grad_gate, back_gate) + cols_inner(grad_upward, back_upward)
    grad_rows_two = lax.psum_scatter(
        grad_normed_two.astype(jnp.bfloat16), "tensor", scatter_dimension=0, tiled=True
    ).astype(jnp.float32)
    gainfeed_part = jnp.sum(grad_rows_two * normed_two, axis=0)
    scaled_two = grad_rows_two * gain_feed
    grad_hidden = grad_out + scale_two * (
        scaled_two - normed_two * jnp.mean(scaled_two * normed_two, axis=1, keepdims=True)
    )
    grad_mixer = lax.all_gather(grad_hidden.astype(jnp.bfloat16), "tensor", axis=0, tiled=True)
    output_part = rows_inner(mixer_out, grad_mixer)
    grad_mixed = cols_inner(grad_mixer, back_output).astype(jnp.bfloat16)
    grad_mixed_float = grad_mixed.astype(jnp.float32)
    grad_mixgate = (grad_mixed_float * convolved).astype(jnp.bfloat16)
    grad_conv_out = grad_mixed_float * gate_float
    conv_rows = []
    value_from_conv = jnp.zeros_like(value_float)
    for offset in range(CONV):
        conv_rows.append(jnp.sum(grad_conv_out * shift_down(value_float, segments, offset), axis=0))
        value_from_conv = value_from_conv + conv_local[offset] * shift_up(
            grad_conv_out, segments, offset
        )
    grad_queries, key_float, value_attn = attend_backward(
        queries, key_rows, value_rows, segments, log_totals, grad_mixed
    )
    grad_keys = key_float.astype(jnp.bfloat16)
    grad_values = (value_attn + value_from_conv).astype(jnp.bfloat16)
    query_part = rows_inner(group_one, grad_queries)
    key_part = rows_inner(group_one, grad_keys)
    value_part = rows_inner(group_one, grad_values)
    mixgate_part = rows_inner(group_one, grad_mixgate)
    grad_normed_one = (
        cols_inner(grad_queries, back_query)
        + cols_inner(grad_keys, back_key)
        + cols_inner(grad_values, back_value)
        + cols_inner(grad_mixgate, back_mixgate)
    )
    grad_rows_one = lax.psum_scatter(
        grad_normed_one.astype(jnp.bfloat16), "tensor", scatter_dimension=0, tiled=True
    ).astype(jnp.float32)
    gainmix_part = jnp.sum(grad_rows_one * normed_one, axis=0)
    scaled_one = grad_rows_one * gain_mixer
    input_grad = grad_hidden + scale_one * (
        scaled_one - normed_one * jnp.mean(scaled_one * normed_one, axis=1, keepdims=True)
    )
    query_grad, key_grad, value_grad, mixgate_grad, output_grad, gate_grad, up_grad, down_grad = (
        lax.psum_scatter(
            query_part.astype(jnp.bfloat16), "dp", scatter_dimension=0, tiled=True
        ).astype(jnp.float32),
        lax.psum_scatter(
            key_part.astype(jnp.bfloat16), "dp", scatter_dimension=0, tiled=True
        ).astype(jnp.float32),
        lax.psum_scatter(
            value_part.astype(jnp.bfloat16), "dp", scatter_dimension=0, tiled=True
        ).astype(jnp.float32),
        lax.psum_scatter(
            mixgate_part.astype(jnp.bfloat16), "dp", scatter_dimension=0, tiled=True
        ).astype(jnp.float32),
        lax.psum_scatter(
            output_part.astype(jnp.bfloat16), "dp", scatter_dimension=1, tiled=True
        ).astype(jnp.float32),
        lax.psum_scatter(
            gate_part.astype(jnp.bfloat16), "dp", scatter_dimension=0, tiled=True
        ).astype(jnp.float32),
        lax.psum_scatter(
            up_part.astype(jnp.bfloat16), "dp", scatter_dimension=0, tiled=True
        ).astype(jnp.float32),
        lax.psum_scatter(
            down_part.astype(jnp.bfloat16), "dp", scatter_dimension=1, tiled=True
        ).astype(jnp.float32),
    )
    conv_full = lax.dynamic_update_slice_in_dim(
        jnp.zeros((CONV, D), jnp.float32), jnp.stack(conv_rows), column, 1
    )
    gainmix_grad, gainfeed_grad, conv_grad = lax.psum(
        (gainmix_part, gainfeed_part, conv_full), ("dp", "tensor")
    )
    return (
        mean_loss,
        outputs,
        input_grad,
        query_grad,
        key_grad,
        value_grad,
        mixgate_grad,
        output_grad,
        conv_grad,
        gainmix_grad,
        gainfeed_grad,
        gate_grad,
        up_grad,
        down_grad,
    )


def solution(mesh):
    return jax.shard_map(
        on_device,
        mesh=mesh,
        in_specs=(
            P(("dp", "tensor"), None),
            P(("dp", "tensor"), None),
            P(("dp", "tensor"), None),
            P("dp"),
            P(("dp", "tensor")),
            P("dp", "tensor"),
            P("dp", "tensor"),
            P("dp", "tensor"),
            P("dp", "tensor"),
            P("tensor", "dp"),
            P(),
            P(),
            P(),
            P("dp", "tensor"),
            P("dp", "tensor"),
            P("tensor", "dp"),
        ),
        out_specs=(
            P(),
            P(("dp", "tensor"), None),
            P(("dp", "tensor"), None),
            P("dp", "tensor"),
            P("dp", "tensor"),
            P("dp", "tensor"),
            P("dp", "tensor"),
            P("tensor", "dp"),
            P(),
            P(),
            P(),
            P("dp", "tensor"),
            P("dp", "tensor"),
            P("tensor", "dp"),
        ),
        check_vma=False,
    )
```

profile of v0, /device:TPU:0, one launch (start us, length us, event | category | flops | bytes accessed | tf_op | source)
XLA Modules:
  0.0 1560.1 jit_solution(9206048574327260512)
XLA Ops:
  17.2 42.0 %all-gather.19.cloned.1.call-done = bf16[1792,448]{1,0:T(8,128)(2,1)} async-done(((bf16[224,448]{1,0:T(8,128)(2,1)}), bf16[1792,448]{1,0:T(8,128)(2,1)}) %all-gather.19.cloned.1.call-update) | async-done | bytes 1605648 | tf_op jit(solution)/shard_map/all_gather | solution.py:201
  59.2 32.7 %all-gather.13.cloned.1.call-done = bf16[1024,1792]{1,0:T(8,128)(2,1)} async-done(((bf16[256,1792]{1,0:T(8,128)(2,1)}), bf16[1024,1792]{1,0:T(8,128)(2,1)}) %all-gather.13.cloned.1.call-update) | async-done | bytes 3670032 | tf_op jit(solution)/shard_map/all_gather | solution.py:225
  96.8 43.5 %all-gather.15.cloned.1.call-done = bf16[1792,448]{1,0:T(8,128)(2,1)} async-done(((bf16[224,448]{1,0:T(8,128)(2,1)}), bf16[1792,448]{1,0:T(8,128)(2,1)}) %all-gather.15.cloned.1.call-update) | async-done | bytes 1605648 | tf_op jit(solution)/shard_map/all_gather | solution.py:202
  146.3 41.4 %all-gather.17.cloned.1.call-done = bf16[1792,448]{1,0:T(8,128)(2,1)} async-done(((bf16[224,448]{1,0:T(8,128)(2,1)}), bf16[1792,448]{1,0:T(8,128)(2,1)}) %all-gather.17.cloned.1.call-update) | async-done | bytes 1605648 | tf_op jit(solution)/shard_map/all_gather | solution.py:200
  187.7 5.4 convolution_convert_fusion.12
  193.1 57.2 %while.26 = (s32[]{:T(128)}, f32[2,512,448]{1,0,2:T(2,128)}, f32[2,7,512]{2,1,0:T(8,128)S(1)}, s32[2]{0:T(128)S(1)}, bf16[1088,448]{0,1:T(8,128)(2,1)}, /*index=...) while((s32[]{:T(128)}, f32[2,512,448]{1,0,2:T(2,128)}, ...), condition=%wide.region_4.5_spmd, body=%wide.region_1.4_spmd.sunk | while | flops 555021312 | bytes 35150840 | solution.py:112
  204.6 17.2 %dynamic_update_slice.30 = f32[2,512,448]{1,0,2:T(2,128)} dynamic-update-slice(f32[2,512,448]{1,0,2:T(2,128)} %get-tuple-element.375, f32[1,512,448]{1,0,2:T(1,128)S(1)} %copy.58, s32[]{:T(128)S(6)} %copy.67, s32[]{:T(128)} %constant.56.clone.1..sunk, s32[]{:T(128)} %constant.56.clone.1..sunk) | dynamic-update-slice | bytes 1835012 | tf_op jit(solution)/shard_map/while/body/jit(dynamic_update_index_in_dim)/dynamic_update_slice | solution.py:112
  233.1 17.2 %dynamic_update_slice.30 = f32[2,512,448]{1,0,2:T(2,128)} dynamic-update-slice(f32[2,512,448]{1,0,2:T(2,128)} %get-tuple-element.375, f32[1,512,448]{1,0,2:T(1,128)S(1)} %copy.58, s32[]{:T(128)S(6)} %copy.67, s32[]{:T(128)} %constant.56.clone.1..sunk, s32[]{:T(128)} %constant.56.clone.1..sunk) | dynamic-update-slice | bytes 1835012 | tf_op jit(solution)/shard_map/while/body/jit(dynamic_update_index_in_dim)/dynamic_update_slice | solution.py:112
  255.6 7.5 fusion.34
  263.1 19.9 %all-gather.23.cloned.1.call-done = bf16[448,1792]{0,1:T(8,128)(2,1)} async-done(((bf16[448,224]{0,1:T(8,128)(2,1)}), bf16[448,1792]{0,1:T(8,128)(2,1)}) %all-gather.23.cloned.1.call-update) | async-done | bytes 1605648 | tf_op jit(solution)/shard_map/all_gather | solution.py:204
  283.0 6.6 fusion.50
  290.5 63.8 %reduce-scatter.15.cloned.1.call-done = f32[256,1792]{1,0:T(8,128)} async-done(((f32[1024,1792]{1,0:T(8,128)}), f32[256,1792]{1,0:T(8,128)}) %reduce-scatter.15.cloned.1.call-update) | async-done | bytes 1835024 | tf_op jit(solution)/shard_map/reduce_scatter | solution.py:246
  359.4 75.7 %all-gather.27.cloned.1.call-done = bf16[1792,1216]{1,0:T(8,128)(2,1)} async-done(((bf16[224,1216]{1,0:T(8,128)(2,1)}), bf16[1792,1216]{1,0:T(8,128)(2,1)}) %all-gather.27.cloned.1.call-update) | async-done | bytes 4358160 | tf_op jit(solution)/shard_map/all_gather | solution.py:205
  435.0 31.9 %all-gather.25.cloned.1.call-done = bf16[1024,1792]{1,0:T(8,128)(2,1)} async-done(((bf16[256,1792]{1,0:T(8,128)(2,1)}), bf16[1024,1792]{1,0:T(8,128)(2,1)}) %all-gather.25.cloned.1.call-update) | async-done | bytes 3670032 | tf_op jit(solution)/shard_map/all_gather | solution.py:249
  466.9 10.4 fusion.51
  477.3 70.2 %all-gather.29.cloned.1.call-done = bf16[1792,1216]{1,0:T(8,128)(2,1)} async-done(((bf16[224,1216]{1,0:T(8,128)(2,1)}), bf16[1792,1216]{1,0:T(8,128)(2,1)}) %all-gather.29.cloned.1.call-update) | async-done | bytes 4358160 | tf_op jit(solution)/shard_map/all_gather | solution.py:206
  547.5 13.3 multiply_convert_fusion.3
  560.8 65.6 %all-gather.31.cloned.1.call-done = bf16[1216,1792]{0,1:T(8,128)(2,1)} async-done(((bf16[1216,224]{0,1:T(8,128)(2,1)}), bf16[1216,1792]{0,1:T(8,128)(2,1)}) %all-gather.31.cloned.1.call-update) | async-done | bytes 4358160 | tf_op jit(solution)/shard_map/all_gather | solution.py:207
  626.4 10.2 convolution_convert_fusion.3
  637.9 38.7 %psum.36 = f32[]{:T(128)} all-reduce(f32[]{:T(128)} %convert_reduce_fusion), channel_id=1, replica_groups=mesh['dp'=8,'tensor'=4] {'dp','tensor'}, use_global_device_ids=true, to_apply=%region_11.12 | all-reduce | flops 1 | bytes 8 | tf_op jit(solution)/shard_map/psum | solution.py:264
  681.5 32.6 %all-gather.33.cloned.1.call-done = bf16[1024,1792]{1,0:T(8,128)(2,1)} async-done(((bf16[256,1792]{1,0:T(8,128)(2,1)}), bf16[1024,1792]{1,0:T(8,128)(2,1)}) %all-gather.33.cloned.1.call-update) | async-done | bytes 3670032 | tf_op jit(solution)/shard_map/all_gather | solution.py:281
  714.0 13.1 multiply_convert_fusion.1
  727.2 9.2 fusion.52
  736.3 9.2 add_convert_fusion.1
  745.6 41.3 %reduce-scatter.19.cloned.1.call-done = bf16[256,1792]{1,0:T(8,128)(2,1)} async-done(((bf16[1024,1792]{1,0:T(8,128)(2,1)}), bf16[256,1792]{1,0:T(8,128)(2,1)}) %reduce-scatter.19.cloned.1.call-update) | async-done | bytes 917520 | tf_op jit(solution)/shard_map/reduce_scatter | solution.py:290
  794.7 9.9 convolution_convert_fusion
  806.3 10.0 convolution_convert_fusion.1
  818.0 9.6 convolution_convert_fusion.2
  835.2 6.3 convert_multiply_fusion.4
  844.5 64.3 %while.27 = (s32[]{:T(128)}, f32[1088,448]{0,1:T(8,128)}, f32[1088,448]{0,1:T(8,128)}, bf16[2,512,448]{1,2,0:T(8,128)(2,1)}, s32[2]{0:T(128)S(1)}, /*index=5*/bf...) while((s32[]{:T(128)}, f32[1088,448]{0,1:T(8,128)}, ...), condition=%wide.region_16.17_spmd, body=%wide.region_14.16_spmd.sunk | while | flops 1355170816 | bytes 99871824 | solution.py:175
  863.9 6.7 dynamic_update_slice.32
  870.7 6.7 dynamic_update_slice.33
  896.7 6.1 dynamic_update_slice.32
  902.7 6.0 dynamic_update_slice.33
  910.1 5.9 convolution_convert_fusion.7
  916.3 5.8 convolution_convert_fusion.6
  935.6 6.3 convolution_convert_fusion.4
  942.2 6.8 fusion.54
  956.8 9.7 add_convert_fusion
  969.3 51.5 %reduce-scatter.33.cloned.1.call-done = bf16[224,1216]{1,0:T(8,128)(2,1)} async-done(((bf16[1792,1216]{1,0:T(8,128)(2,1)}), bf16[224,1216]{1,0:T(8,128)(2,1)}) %reduce-scatter.33.cloned.1.call-update) | async-done | bytes 544784 | tf_op jit(solution)/shard_map/reduce_scatter | solution.py:353
  1023.0 95.0 %reduce-scatter.31.cloned.1.call-done = bf16[224,1216]{1,0:T(8,128)(2,1)} async-done(((bf16[1792,1216]{1,0:T(8,128)(2,1)}), bf16[224,1216]{1,0:T(8,128)(2,1)}) %reduce-scatter.31.cloned.1.call-update) | async-done | bytes 544784 | tf_op jit(solution)/shard_map/reduce_scatter | solution.py:350
  1120.5 67.5 %reduce-scatter.37.cloned.1.call-done = bf16[224,448]{1,0:T(8,128)(2,1)} async-done(((bf16[1792,448]{1,0:T(8,128)(2,1)}), bf16[224,448]{1,0:T(8,128)(2,1)}) %reduce-scatter.37.cloned.1.call-update) | async-done | bytes 200720
  1189.9 66.6 %reduce-scatter.23.cloned.1.call-done = bf16[224,448]{1,0:T(8,128)(2,1)} async-done(((bf16[1792,448]{1,0:T(8,128)(2,1)}), bf16[224,448]{1,0:T(8,128)(2,1)}) %reduce-scatter.23.cloned.1.call-update) | async-done | bytes 200720 | tf_op jit(solution)/shard_map/reduce_scatter | solution.py:335
  1258.2 67.1 %reduce-scatter.25.cloned.1.call-done = bf16[224,448]{1,0:T(8,128)(2,1)} async-done(((bf16[1792,448]{1,0:T(8,128)(2,1)}), bf16[224,448]{1,0:T(8,128)(2,1)}) %reduce-scatter.25.cloned.1.call-update) | async-done | bytes 200720 | tf_op jit(solution)/shard_map/reduce_scatter | solution.py:338
  1327.1 66.8 %reduce-scatter.27.cloned.1.call-done = bf16[224,448]{1,0:T(8,128)(2,1)} async-done(((bf16[1792,448]{1,0:T(8,128)(2,1)}), bf16[224,448]{1,0:T(8,128)(2,1)}) %reduce-scatter.27.cloned.1.call-update) | async-done | bytes 200720 | tf_op jit(solution)/shard_map/reduce_scatter | solution.py:341
  1395.7 67.2 %reduce-scatter.29.cloned.1.call-done = bf16[224,448]{1,0:T(8,128)(2,1)} async-done(((bf16[1792,448]{1,0:T(8,128)(2,1)}), bf16[224,448]{1,0:T(8,128)(2,1)}) %reduce-scatter.29.cloned.1.call-update) | async-done | bytes 200720 | tf_op jit(solution)/shard_map/reduce_scatter | solution.py:344
  1464.7 40.8 %reduce-scatter.21.cloned.1.call-done = bf16[256,1792]{1,0:T(8,128)(2,1)} async-done(((bf16[1024,1792]{1,0:T(8,128)(2,1)}), bf16[256,1792]{1,0:T(8,128)(2,1)}) %reduce-scatter.21.cloned.1.call-update) | async-done | bytes 917520 | tf_op jit(solution)/shard_map/reduce_scatter | solution.py:326
  1507.4 40.7 %all-reduce.9 = (f32[]{:T(128)}, f32[3,1792]{1,0:T(4,128)}, f32[1792]{0:T(1024)}, f32[1792]{0:T(1024)}) all-reduce(f32[]{:T(128)} %get-tuple-element.202, f32[3,1792]{1,0:T(4,128)S(1)} %dynamic_update_slice.21, f32[1792]{0:T(1024)S(1)} %get-tuple-element.133, f32[1792]{0:T(1024)S(1)} %copy-done.33), channel_id=1, replica_groups=mesh['dp'=8,'tensor'=4] {'dp','tensor'}, use_global_device_ids=true, to_apply=%region_9.10 | all-reduce | flops 8961 | bytes 71688 | tf_op jit(solution)/shard_map/psum | solution.py:264
  (283 shorter events, 160.5 us)
Async XLA Ops:
  7.2 52.0 %all-gather.19.cloned.1.call-start = ((), (), s32[]{:S(2)}) async-start(), calls=%async_computation.15 | async-start | bytes 2064384 | tf_op jit(solution)/shard_map/all_gather | solution.py:201
  7.9 5.9 copy-start.28
  7.9 84.0 %all-gather.13.cloned.1.call-start = ((), (), s32[]{:S(2)}) async-start(), calls=%async_computation.12 | async-start | bytes 4587520 | tf_op jit(solution)/shard_map/all_gather | solution.py:225
  9.5 5.3 copy-start.24
  11.9 128.5 %all-gather.15.cloned.1.call-start = ((), (), s32[]{:S(2)}) async-start(), calls=%async_computation.13 | async-start | bytes 2064384 | tf_op jit(solution)/shard_map/all_gather | solution.py:202
  12.6 175.1 %all-gather.17.cloned.1.call-start = ((), (), s32[]{:S(2)}) async-start(), calls=%async_computation.14 | async-start | bytes 2064384 | tf_op jit(solution)/shard_map/all_gather | solution.py:200
  13.2 242.3 %all-gather.21.cloned.1.call-start = ((), (), s32[]{:S(2)}) async-start(), calls=%async_computation.16 | async-start | bytes 2064384 | tf_op jit(solution)/shard_map/all_gather | solution.py:203
  13.8 269.2 %all-gather.23.cloned.1.call-start = ((), (), s32[]{:S(2)}) async-start(), calls=%async_computation.17 | async-start | bytes 2064384 | tf_op jit(solution)/shard_map/all_gather | solution.py:204
  14.7 339.6 %reduce-scatter.15.cloned.1.call-start = ((), (), s32[]{:S(2)}) async-start(), calls=%async_computation.18 | async-start | bytes 9175040 | tf_op jit(solution)/shard_map/reduce_scatter | solution.py:246
  16.2 239.3 %copy-start.42 = (pred[1024]{0:T(1024)(128)(4,1)}, pred[1024]{0:T(1024)(128)(4,1)S(1)}, u32[]{:S(2)}) copy-start(pred[1024]{0:T(1024)(128)(4,1)S(1)} %pad_add_fusion) | copy-start | bytes 3076
  16.3 239.2 %copy-start.44 = (pred[1024]{0:T(1024)(128)(4,1)}, pred[1024]{0:T(1024)(128)(4,1)S(1)}, u32[]{:S(2)}) copy-start(pred[1024]{0:T(1024)(128)(4,1)S(1)} %concatenate.45) | copy-start | bytes 3076
  17.2 238.4 %copy-start.34 = (f32[1,448]{1,0:T(1,128)}, f32[1,448]{1,0:T(1,128)S(1)}, u32[]{:S(2)}) copy-start(f32[1,448]{1,0:T(1,128)S(1)} %get-tuple-element.204) | copy-start | bytes 5380
  17.2 238.4 %copy-start.36 = (f32[1,448]{1,0:T(1,128)}, f32[1,448]{1,0:T(1,128)S(1)}, u32[]{:S(2)}) copy-start(f32[1,448]{1,0:T(1,128)S(1)} %get-tuple-element.205) | copy-start | bytes 5380
  17.2 238.4 %copy-start.38 = (f32[1,448]{1,0:T(1,128)}, f32[1,448]{1,0:T(1,128)S(1)}, u32[]{:S(2)}) copy-start(f32[1,448]{1,0:T(1,128)S(1)} %get-tuple-element.206) | copy-start | bytes 5380
  144.8 110.7 %copy-start.2 = (bf16[1024,448]{0,1:T(8,128)(2,1)}, bf16[1024,448]{0,1:T(8,128)(2,1)S(1)}, u32[]{:S(2)}) copy-start(bf16[1024,448]{0,1:T(8,128)(2,1)S(1)} %convolution_convert_fusion.13) | copy-start | bytes 2752516
  263.1 26.5 %copy-start.22 = (bf16[1024,448]{0,1:T(8,128)(2,1)}, bf16[1024,448]{0,1:T(8,128)(2,1)S(1)}, u32[]{:S(2)}) copy-start(bf16[1024,448]{0,1:T(8,128)(2,1)S(1)} %get-tuple-element.190) | copy-start | bytes 2752516
  289.7 145.4 %all-gather.27.cloned.1.call-start = ((), (), s32[]{:S(2)}) async-start(), calls=%async_computation.20 | async-start | bytes 5160960 | tf_op jit(solution)/shard_map/all_gather | solution.py:205
  290.4 66.0 %copy-start.32 = (f32[1792]{0:T(1024)S(1)}, f32[1792]{0:T(1024)}, u32[]{:S(2)}) copy-start(f32[1792]{0:T(1024)} %param.32) | copy-start | bytes 21508
  290.4 176.5 %all-gather.25.cloned.1.call-start = ((), (), s32[]{:S(2)}) async-start(), calls=%async_computation.19 | async-start | bytes 4587520 | tf_op jit(solution)/shard_map/all_gather | solution.py:249
  357.5 190.0 %all-gather.29.cloned.1.call-start = ((), (), s32[]{:S(2)}) async-start(), calls=%async_computation.21 | async-start | bytes 5160960 | tf_op jit(solution)/shard_map/all_gather | solution.py:206
  358.1 268.3 %all-gather.31.cloned.1.call-start = ((), (), s32[]{:S(2)}) async-start(), calls=%async_computation.22 | async-start | bytes 5160960 | tf_op jit(solution)/shard_map/all_gather | solution.py:207
  358.9 318.5 %reduce-scatter.17.cloned.1.call-start = ((), (), s32[]{:S(2)}) async-start(), calls=%async_computation.23 | async-start | bytes 4587520 | tf_op jit(solution)/shard_map/reduce_scatter | solution.py:258
  636.7 77.4 %all-gather.33.cloned.1.call-start = ((), (), s32[]{:S(2)}) async-start(), calls=%async_computation.24 | async-start | bytes 4587520 | tf_op jit(solution)/shard_map/all_gather | solution.py:281
  681.4 105.5 %reduce-scatter.19.cloned.1.call-start = ((), (), s32[]{:S(2)}) async-start(), calls=%async_computation.25 | async-start | bytes 4587520 | tf_op jit(solution)/shard_map/reduce_scatter | solution.py:290
  727.1 9.2 copy-start.50
  727.1 9.2 copy-start.52
  745.5 82.2 %all-gather.35.cloned.1.call-start = ((), (), s32[]{:S(2)}) async-start(), calls=%async_computation.26 | async-start | bytes 4587520 | tf_op jit(solution)/shard_map/all_gather | solution.py:298
  794.7 172.5 %reduce-scatter.35.cloned.1.call-start = ((), (), s32[]{:S(2)}) async-start(), calls=%async_computation.34 | async-start | bytes 5160960 | tf_op jit(solution)/shard_map/reduce_scatter | solution.py:356
  804.6 216.3 %reduce-scatter.33.cloned.1.call-start = ((), (), s32[]{:S(2)}) async-start(), calls=%async_computation.33 | async-start | bytes 5160960 | tf_op jit(solution)/shard_map/reduce_scatter | solution.py:353
  816.3 301.7 %reduce-scatter.31.cloned.1.call-start = ((), (), s32[]{:S(2)}) async-start(), calls=%async_computation.32 | async-start | bytes 5160960 | tf_op jit(solution)/shard_map/reduce_scatter | solution.py:350
  827.7 360.3 %reduce-scatter.37.cloned.1.call-start = ((), (), s32[]{:S(2)}) async-start(), calls=%async_computation.35 | async-start | bytes 2064384
  835.1 421.4 %reduce-scatter.23.cloned.1.call-start = ((), (), s32[]{:S(2)}) async-start(), calls=%async_computation.28 | async-start | bytes 2064384 | tf_op jit(solution)/shard_map/reduce_scatter | solution.py:335
  910.1 5.9 copy-start.20
  910.1 6.2 copy-start.1
  916.0 409.4 %reduce-scatter.25.cloned.1.call-start = ((), (), s32[]{:S(2)}) async-start(), calls=%async_computation.29 | async-start | bytes 2064384 | tf_op jit(solution)/shard_map/reduce_scatter | solution.py:338
  916.3 5.9 copy-start.47
  916.3 5.9 copy-start.46
  922.1 471.8 %reduce-scatter.27.cloned.1.call-start = ((), (), s32[]{:S(2)}) async-start(), calls=%async_computation.30 | async-start | bytes 2064384 | tf_op jit(solution)/shard_map/reduce_scatter | solution.py:341
  935.5 527.5 %reduce-scatter.29.cloned.1.call-start = ((), (), s32[]{:S(2)}) async-start(), calls=%async_computation.31 | async-start | bytes 2064384 | tf_op jit(solution)/shard_map/reduce_scatter | solution.py:344
  935.5 6.6 copy-start.19
  941.8 563.6 %reduce-scatter.21.cloned.1.call-start = ((), (), s32[]{:S(2)}) async-start(), calls=%async_computation.27 | async-start | bytes 4587520 | tf_op jit(solution)/shard_map/reduce_scatter | solution.py:326
  942.2 6.8 copy-start.21
  942.2 6.8 copy-start.49
  1120.1 385.3 %copy-start.6 = (bf16[256,1792]{1,0:T(8,128)(2,1)S(1)}, bf16[256,1792]{1,0:T(8,128)(2,1)}, u32[]{:S(2)}) copy-start(bf16[256,1792]{1,0:T(8,128)(2,1)} %param.20) | copy-start | bytes 2752516
  1120.1 385.3 %copy-start.31 = (f32[1792]{0:T(1024)S(1)}, f32[1792]{0:T(1024)}, u32[]{:S(2)}) copy-start(f32[1792]{0:T(1024)} %param.31) | copy-start | bytes 21508
  1120.1 385.3 %copy-start.41 = (f32[256]{0:T(256)S(1)}, f32[256]{0:T(256)}, u32[]{:S(2)}) copy-start(f32[256]{0:T(256)} %copy-done.40) | copy-start | bytes 3076
  1258.2 249.2 %copy-start.33 = (f32[1792]{0:T(1024)S(1)}, f32[1792]{0:T(1024)}, u32[]{:S(2)}) copy-start(f32[1792]{0:T(1024)} %get-tuple-element.131) | copy-start | bytes 21508
  1258.2 290.5 %copy-start.10 = (f32[256,1792]{1,0:T(8,128)S(1)}, f32[256,1792]{1,0:T(8,128)}, u32[]{:S(2)}) copy-start(f32[256,1792]{1,0:T(8,128)} %get-tuple-element.185) | copy-start | bytes 5505028
  (32 other events, 85.3 us)
Sparse Core Ops, SparseCore 0:
  10.2 48.9 all-gather.18
  61.3 30.5 all-gather.12
  94.1 46.2 all-gather.14
  142.4 45.2 all-gather.16
  189.7 45.3 all-gather.20
  237.7 45.2 all-gather.22
  289.8 64.4 reduce-scatter.14
  356.7 78.2 all-gather.26
  437.3 29.6 all-gather.24
  469.2 78.2 all-gather.28
  549.9 76.4 all-gather.30
  636.8 39.8 reduce-scatter.16
  681.5 32.4 all-gather.32
  745.7 41.2 reduce-scatter.18
  794.8 31.5 all-gather.34
  830.3 93.4 reduce-scatter.34
  927.6 93.1 reduce-scatter.32
  1024.8 93.1 reduce-scatter.30
  1121.9 66.0 reduce-scatter.36
  1191.3 65.1 reduce-scatter.22
  1260.3 64.9 reduce-scatter.24
  1328.8 65.0 reduce-scatter.26
  1397.8 65.0 reduce-scatter.28
  1465.3 40.0 reduce-scatter.20
where the time goes:
time: 1570 us; the launch traced here: 1560 us
  waiting for transfers between devices  1090 us (69%)
  matrix products  205 us (13%)
  local copies, waits for them, and re-layouts  109 us (7%)
  blocking collectives  79.4 us (5%)
  other arithmetic  55.8 us (4%)
  between operations  18.6 us (1%)
    reduce_scatter x1, waiting for transfers between devices, on_device(): lax.psum_scatter(gate_part.astype(jnp.bfloat16), 'dp', scatter_dimension=...  95 us
    psum x2, blocking collectives, on_device(): lax.psum((jnp.sum(valid_rows), jnp.sum(valid_rows[:, None] * deviation *...  79.4 us
    all_gather x1, waiting for transfers between devices, on_device(): lax.all_gather(gate_weight, 'dp', axis=0, tiled=True)  75.7 us
    unnamed x25, waiting for transfers between devices  72.1 us
    all_gather x1, waiting for transfers between devices, on_device(): lax.all_gather(up_weight, 'dp', axis=0, tiled=True)  70.2 us
    reduce_scatter x1, waiting for transfers between devices, on_device(): lax.psum_scatter(mixgate_part.astype(jnp.bfloat16), 'dp', scatter_dimensi...  67.2 us
    reduce_scatter x1, waiting for transfers between devices, on_device(): lax.psum_scatter(key_part.astype(jnp.bfloat16), 'dp', scatter_dimension=0...  67.1 us
    reduce_scatter x1, waiting for transfers between devices, on_device(): lax.psum_scatter(value_part.astype(jnp.bfloat16), 'dp', scatter_dimension...  66.8 us
  transfers between devices with their start and end apart: 24, of which 20 were waited for; matrix products, arithmetic and copies ran while one was open for 19% of the time, Pallas kernels for 0%

commit v1 on v0

--- a/solution.py
+++ b/solution.py
@@ -176,6 +176,134 @@
         one_block, (zeros_pad, zeros_pad), (block_ids, log_totals)
     )
     return (query_blocks.reshape(group_rows, local_width), key_acc[WINDOW:], value_acc[WINDOW:])
+
+
+def pairs_xor(size, mask):
+    return [(i, i ^ mask) for i in range(size)]
+
+
+def pairs_shift(size, step):
+    return [(i, (i + step) % size) for i in range(size)]
+
+
+def put(buffer, block, index):
+    return lax.dynamic_update_slice_in_dim(buffer, block[None], index, 0)
+
+
+def pick(blocks, index):
+    return lax.dynamic_index_in_dim(blocks, index, 0, keepdims=False)
+
+
+def gather_dp(own):
+    size = lax.axis_size("dp")
+    if size != 8:
+        return lax.all_gather(own, "dp", axis=0)
+    me = lax.axis_index("dp")
+    over_y = pairs_xor(size, 1)
+    up, down = pairs_shift(size, 2), pairs_shift(size, -2)
+    mate = lax.ppermute(own, "dp", over_y)
+    own_below = lax.ppermute(own, "dp", up)
+    own_above = lax.ppermute(own, "dp", down)
+    mate_below = lax.ppermute(mate, "dp", up)
+    mate_above = lax.ppermute(mate, "dp", down)
+    own_far = lax.ppermute(own_below, "dp", up)
+    mate_far = lax.ppermute(mate_above, "dp", down)
+    below, above, far = (me + 6) % size, (me + 2) % size, (me + 4) % size
+    full = jnp.zeros((size,) + own.shape, own.dtype)
+    for block, index in (
+        (own, me),
+        (mate, me ^ 1),
+        (own_below, below),
+        (own_above, above),
+        (mate_below, below ^ 1),
+        (mate_above, above ^ 1),
+        (own_far, far),
+        (mate_far, far ^ 1),
+    ):
+        full = put(full, block, index)
+    return full
+
+
+def scatter_dp(parts):
+    size = lax.axis_size("dp")
+    if size != 8:
+        return lax.psum_scatter(parts, "dp", scatter_dimension=0).astype(jnp.float32)
+    me = lax.axis_index("dp")
+    over_y = pairs_xor(size, 1)
+    up, down = pairs_shift(size, 2), pairs_shift(size, -2)
+    below, above, far = (me + 6) % size, (me + 2) % size, (me + 4) % size
+
+    def part(index):
+        return pick(parts, index).astype(jnp.float32)
+
+    low = jnp.bfloat16
+    own_first = lax.ppermute(pick(parts, far), "dp", up)
+    mate_first = lax.ppermute(pick(parts, far ^ 1), "dp", down)
+    mate_from_below = lax.ppermute(pick(parts, above ^ 1), "dp", up)
+    own_from_above = lax.ppermute(pick(parts, below), "dp", down)
+    mate_from_above = lax.ppermute(
+        (part(below ^ 1) + mate_first.astype(jnp.float32)).astype(low), "dp", down
+    )
+    own_from_below = lax.ppermute(
+        (part(above) + own_first.astype(jnp.float32)).astype(low), "dp", up
+    )
+    mate_sum = (
+        part(me ^ 1)
+        + mate_from_below.astype(jnp.float32)
+        + mate_from_above.astype(jnp.float32)
+    )
+    from_mate = lax.ppermute(mate_sum.astype(low), "dp", over_y)
+    own_sum = part(me) + own_from_below.astype(jnp.float32) + own_from_above.astype(jnp.float32)
+    return own_sum + from_mate.astype(jnp.float32)
+
+
+def gather_tensor(own):
+    size = lax.axis_size("tensor")
+    if size != 4:
+        return lax.all_gather(own, "tensor", axis=0, tiled=True)
+    me = lax.axis_index("tensor")
+    across = lax.ppermute(own, "tensor", pairs_xor(size, 2))
+    beside = lax.ppermute(own, "tensor", pairs_xor(size, 1))
+    beside_across = lax.ppermute(across, "tensor", pairs_xor(size, 1))
+    full = jnp.zeros((size,) + own.shape, own.dtype)
+    for block, index in ((own, me), (beside, me ^ 1), (across, me ^ 2), (beside_across, me ^ 3)):
+        full = put(full, block, index)
+    return full.reshape(size * own.shape[0], own.shape[1])
+
+
+def scatter_tensor(parts):
+    size = lax.axis_size("tensor")
+    if size != 4:
+        return lax.psum_scatter(
+            parts.astype(jnp.bfloat16), "tensor", scatter_dimension=0, tiled=True
+        ).astype(jnp.float32)
+    me = lax.axis_index("tensor")
+    low = jnp.bfloat16
+    parts = parts.reshape(size, -1, parts.shape[1])
+    beside = lax.ppermute(pick(parts, me ^ 3).astype(low), "tensor", pairs_xor(size, 1))
+    sent = (pick(parts, me ^ 2).astype(jnp.float32) + beside.astype(jnp.float32)).astype(low)
+    across = lax.ppermute(sent, "tensor", pairs_xor(size, 2))
+    beside_own = lax.ppermute(pick(parts, me ^ 1).astype(low), "tensor", pairs_xor(size, 1))
+    return (
+        pick(parts, me).astype(jnp.float32)
+        + beside_own.astype(jnp.float32)
+        + across.astype(jnp.float32)
+    )
+
+
+def sum_all(values):
+    dp_size, tensor_size = lax.axis_size("dp"), lax.axis_size("tensor")
+    if dp_size != 8 or tensor_size != 4:
+        return lax.psum(values, ("dp", "tensor"))
+    for axis, size, mask in (
+        ("tensor", tensor_size, 1),
+        ("tensor", tensor_size, 2),
+        ("dp", dp_size, 1),
+        ("dp", dp_size, 2),
+        ("dp", dp_size, 6),
+    ):
+        values = values + lax.ppermute(values, axis, pairs_xor(size, mask))
+    return values
 
 
 def on_device(
@@ -196,35 +324,26 @@
     up_weight,
     down_weight,
 ):
-    gathered = (
-        lax.all_gather(query_weight, "dp", axis=0, tiled=True),
-        lax.all_gather(key_weight, "dp", axis=0, tiled=True),
-        lax.all_gather(value_weight, "dp", axis=0, tiled=True),
-        lax.all_gather(mixgate_weight, "dp", axis=0, tiled=True),
-        lax.all_gather(output_weight, "dp", axis=1, tiled=True),
-        lax.all_gather(gate_weight, "dp", axis=0, tiled=True),
-        lax.all_gather(up_weight, "dp", axis=0, tiled=True),
-        lax.all_gather(down_weight, "dp", axis=1, tiled=True),
-    )
-    (
-        full_query,
-        full_key,
-        full_value,
-        full_mixgate,
-        full_output,
-        full_gate,
-        full_upward,
-        full_down,
-    ) = gathered
-    local_width = full_query.shape[1]
+    rows = block_input.shape[0]
+    valid_rows = valid_mask.astype(jnp.float32)
+    valid_total = sum_all(jnp.full((8, 128), jnp.sum(valid_rows), jnp.float32))[0, 0]
+    local_width = query_weight.shape[1]
+    local_hidden = gate_weight.shape[1]
+    mixer_own = jnp.concatenate(
+        [query_weight, key_weight, value_weight, mixgate_weight, output_weight.T], axis=1
+    )
+    feed_own = jnp.concatenate([gate_weight, up_weight], axis=1)
+    mixer_all = gather_dp(mixer_own).reshape(D, -1)
+    feed_all = gather_dp(feed_own).reshape(D, -1)
+    full_down = gather_dp(down_weight.T).reshape(D, -1)
+    full_query, full_key, full_value, full_mixgate, full_output = jnp.split(mixer_all, 5, axis=1)
+    full_gate, full_upward = jnp.split(feed_all, 2, axis=1)
     column = lax.axis_index("tensor") * local_width
     conv_local = lax.dynamic_slice_in_dim(conv_weight, column, local_width, 1)
     inputs = block_input.astype(jnp.float32)
     scale_one = rms_scale(inputs)
     normed_one = inputs * scale_one
-    group_one = lax.all_gather(
-        (normed_one * gain_mixer).astype(jnp.bfloat16), "tensor", axis=0, tiled=True
-    )
+    group_one = gather_tensor((normed_one * gain_mixer).astype(jnp.bfloat16))
     queries = jnp.dot(group_one, full_query, preferred_element_type=jnp.float32).astype(
         jnp.bfloat16
     )
@@ -242,62 +361,46 @@
         convolved = convolved + conv_local[offset] * shift_down(value_float, segments, offset)
     gate_float = mix_gate.astype(jnp.float32)
     mixer_out = (attended + convolved * gate_float).astype(jnp.bfloat16)
-    mixer_part = jnp.dot(mixer_out, full_output, preferred_element_type=jnp.float32)
-    hidden = inputs + lax.psum_scatter(mixer_part, "tensor", scatter_dimension=0, tiled=True)
+    mixer_part = cols_inner(mixer_out, full_output)
+    hidden = inputs + scatter_tensor(mixer_part)
     scale_two = rms_scale(hidden)
     normed_two = hidden * scale_two
-    group_two = lax.all_gather(
-        (normed_two * gain_feed).astype(jnp.bfloat16), "tensor", axis=0, tiled=True
-    )
+    group_two = gather_tensor((normed_two * gain_feed).astype(jnp.bfloat16))
     gate_value = jnp.dot(group_two, full_gate, preferred_element_type=jnp.float32)
     up_value = jnp.dot(group_two, full_upward, preferred_element_type=jnp.float32)
     sigmoid_gate = jax.nn.sigmoid(gate_value)
     silu_gate = gate_value * sigmoid_gate
     active = (silu_gate * up_value).astype(jnp.bfloat16)
-    feed_part = jnp.dot(active, full_down, preferred_element_type=jnp.float32)
-    outputs = hidden + lax.psum_scatter(
-        feed_part.astype(jnp.bfloat16), "tensor", scatter_dimension=0, tiled=True
-    ).astype(jnp.float32)
+    feed_part = cols_inner(active, full_down)
+    outputs = hidden + scatter_tensor(feed_part)
     target = teacher.astype(jnp.float32)
-    valid_rows = valid_mask.astype(jnp.float32)
     deviation = outputs - target
-    valid_total, squares = lax.psum(
-        (jnp.sum(valid_rows), jnp.sum(valid_rows[:, None] * deviation * deviation)),
-        ("dp", "tensor"),
-    )
-    all_tokens = block_input.shape[0] * lax.axis_size("dp") * lax.axis_size("tensor")
-    mean_loss = squares / (valid_total * D)
+    squares = jnp.sum(valid_rows[:, None] * deviation * deviation)
+    all_tokens = rows * lax.axis_size("dp") * lax.axis_size("tensor")
     grad_out = cotangent + valid_rows[:, None] * deviation * (all_tokens / valid_total)
-    (
-        back_query,
-        back_key,
-        back_value,
-        back_mixgate,
-        back_output,
-        back_gate,
-        back_upward,
-        back_down,
-    ) = gathered
-    grad_feed = lax.all_gather(grad_out.astype(jnp.bfloat16), "tensor", axis=0, tiled=True)
-    down_part = rows_inner(active, grad_feed)
-    grad_active = cols_inner(grad_feed, back_down)
+    grad_feed = gather_tensor(grad_out.astype(jnp.bfloat16))
+    down_part = rows_inner(grad_feed, active)
+    down_grad = scatter_dp(down_part.astype(jnp.bfloat16).reshape(-1, down_weight.shape[1], local_hidden)).T
+    grad_active = jnp.dot(grad_feed, full_down, preferred_element_type=jnp.float32)
     silu_slope = sigmoid_gate * (1.0 + gate_value * (1.0 - sigmoid_gate))
     grad_gate = (grad_active * up_value * silu_slope).astype(jnp.bfloat16)
     grad_upward = (grad_active * silu_gate).astype(jnp.bfloat16)
+    grad_normed_two = cols_inner(grad_gate, full_gate) + cols_inner(grad_upward, full_upward)
+    grad_rows_two = scatter_tensor(grad_normed_two)
     gate_part = rows_inner(group_two, grad_gate)
     up_part = rows_inner(group_two, grad_upward)
-    grad_normed_two = cols_inner(grad_gate, back_gate) + cols_inner(grad_upward, back_upward)
-    grad_rows_two = lax.psum_scatter(
-        grad_normed_two.astype(jnp.bfloat16), "tensor", scatter_dimension=0, tiled=True
-    ).astype(jnp.float32)
+    shard = gate_weight.shape[0]
+    gate_grad = scatter_dp(gate_part.astype(jnp.bfloat16).reshape(-1, shard, local_hidden))
+    up_grad = scatter_dp(up_part.astype(jnp.bfloat16).reshape(-1, shard, local_hidden))
     gainfeed_part = jnp.sum(grad_rows_two * normed_two, axis=0)
     scaled_two = grad_rows_two * gain_feed
     grad_hidden = grad_out + scale_two * (
         scaled_two - normed_two * jnp.mean(scaled_two * normed_two, axis=1, keepdims=True)
     )
-    grad_mixer = lax.all_gather(grad_hidden.astype(jnp.bfloat16), "tensor", axis=0, tiled=True)
-    output_part = rows_inner(mixer_out, grad_mixer)
-    grad_mixed = cols_inner(grad_mixer, back_output).astype(jnp.bfloat16)
+    grad_mixer = gather_tensor(grad_hidden.astype(jnp.bfloat16))
+    output_part = rows_inner(grad_mixer, mixer_out)
+    output_grad = scatter_dp(output_part.astype(jnp.bfloat16).reshape(-1, shard, local_width)).T
+    grad_mixed = jnp.dot(grad_mixer, full_output, preferred_element_type=jnp.float32).astype(jnp.bfloat16)
     grad_mixed_float = grad_mixed.astype(jnp.float32)
     grad_mixgate = (grad_mixed_float * convolved).astype(jnp.bfloat16)
     grad_conv_out = grad_mixed_float * gate_float
@@ -313,56 +416,42 @@
     )
     grad_keys = key_float.astype(jnp.bfloat16)
     grad_values = (value_attn + value_from_conv).astype(jnp.bfloat16)
-    query_part = rows_inner(group_one, grad_queries)
-    key_part = rows_inner(group_one, grad_keys)
-    value_part = rows_inner(group_one, grad_values)
-    mixgate_part = rows_inner(group_one, grad_mixgate)
+
+    def project_grad(grads):
+        part = rows_inner(group_one, grads).astype(jnp.bfloat16)
+        return scatter_dp(part.reshape(-1, shard, local_width))
+
+    query_grad = project_grad(grad_queries)
+    key_grad = project_grad(grad_keys)
+    value_grad = project_grad(grad_values)
+    mixgate_grad = project_grad(grad_mixgate)
     grad_normed_one = (
-        cols_inner(grad_queries, back_query)
-        + cols_inner(grad_keys, back_key)
-        + cols_inner(grad_values, back_value)
-        + cols_inner(grad_mixgate, back_mixgate)
-    )
-    grad_rows_one = lax.psum_scatter(
-        grad_normed_one.astype(jnp.bfloat16), "tensor", scatter_dimension=0, tiled=True
-    ).astype(jnp.float32)
+        cols_inner(grad_queries, full_query)
+        + cols_inner(grad_keys, full_key)
+        + cols_inner(grad_values, full_value)
+        + cols_inner(grad_mixgate, full_mixgate)
+    )
+    grad_rows_one = scatter_tensor(grad_normed_one)
     gainmix_part = jnp.sum(grad_rows_one * normed_one, axis=0)
     scaled_one = grad_rows_one * gain_mixer
     input_grad = grad_hidden + scale_one * (
         scaled_one - normed_one * jnp.mean(scaled_one * normed_one, axis=1, keepdims=True)
     )
-    query_grad, key_grad, value_grad, mixgate_grad, output_grad, gate_grad, up_grad, down_grad = (
-        lax.psum_scatter(
-            query_part.astype(jnp.bfloat16), "dp", scatter_dimension=0, tiled=True
-        ).astype(jnp.float32),
-        lax.psum_scatter(
-            key_part.astype(jnp.bfloat16), "dp", scatter_dimension=0, tiled=True
-        ).astype(jnp.float32),
-        lax.psum_scatter(
-            value_part.astype(jnp.bfloat16), "dp", scatter_dimension=0, tiled=True
-        ).astype(jnp.float32),
-        lax.psum_scatter(
-            mixgate_part.astype(jnp.bfloat16), "dp", scatter_dimension=0, tiled=True
-        ).astype(jnp.float32),
-        lax.psum_scatter(
-            output_part.astype(jnp.bfloat16), "dp", scatter_dimension=1, tiled=True
-        ).astype(jnp.float32),
-        lax.psum_scatter(
-            gate_part.astype(jnp.bfloat16), "dp", scatter_dimension=0, tiled=True
-        ).astype(jnp.float32),
-        lax.psum_scatter(
-            up_part.astype(jnp.bfloat16), "dp", scatter_dimension=0, tiled=True
-        ).astype(jnp.float32),
-        lax.psum_scatter(
-            down_part.astype(jnp.bfloat16), "dp", scatter_dimension=1, tiled=True
-        ).astype(jnp.float32),
-    )
     conv_full = lax.dynamic_update_slice_in_dim(
         jnp.zeros((CONV, D), jnp.float32), jnp.stack(conv_rows), column, 1
     )
-    gainmix_grad, gainfeed_grad, conv_grad = lax.psum(
-        (gainmix_part, gainfeed_part, conv_full), ("dp", "tensor")
-    )
+    small = sum_all(
+        jnp.concatenate(
+            [
+                conv_full,
+                gainmix_part[None],
+                gainfeed_part[None],
+                jnp.full((1, D), squares, jnp.float32),
+            ]
+        )
+    )
+    conv_grad, gainmix_grad, gainfeed_grad = small[:CONV], small[CONV], small[CONV + 1]
+    mean_loss = small[CONV + 2, 0] / (valid_total * D)
     return (
         mean_loss,
         outputs,

time: 1570 us -> 1290 us (0.82)
  waiting for transfers between devices: 1090 us -> 517 us
  local copies, waits for them, and re-layouts: 109 us -> 308 us
  starting transfers between devices: 1.9 us -> 186 us
  blocking collectives: 79.4 us -> 0 us
    reduce_scatter x11 -> x0, waiting for transfers between devices: 560 us -> none  [the longest x1 95 us: on_device(): lax.psum_scatter(gate_part.astype(jnp.bfloat16), 'dp', scatter_dimension=...]
    ppermute x0 -> x111, waiting for transfers between devices: none -> 517 us  [the longest x3 93.3 us: gather_dp(): mate_above = lax.ppermute(mate, 'dp', down)]
    all_gather x12 -> x0, waiting for transfers between devices: 456 us -> none  [the longest x1 75.7 us: on_device(): lax.all_gather(gate_weight, 'dp', axis=0, tiled=True)]
    ppermute x0 -> x111, starting transfers between devices: none -> 186 us  [the longest x8 33.9 us: scatter_dp(): own_from_above = lax.ppermute(pick(parts, below), 'dp', down)]
    psum x2 -> x0, blocking collectives: 79.4 us -> none  [on_device(): lax.psum((jnp.sum(valid_rows), jnp.sum(valid_rows[:, None] * deviation *...]
    unnamed x25 -> x0, waiting for transfers between devices: 72.1 us -> none
    dynamic_slice x0 -> x18, local copies, waits for them, and re-layouts: none -> 56 us  [pick(): return lax.dynamic_index_in_dim(blocks, index, 0, keepdims=False)]
    dynamic_update_slice x0 -> x35, local copies, waits for them, and re-layouts: none -> 43.8 us  [put(): return lax.dynamic_update_slice_in_dim(buffer, block[None], index, 0)]
  transfers between devices with their start and end apart: 24 -> 111, of which waited for: 20 -> 56; matrix products, arithmetic and copies ran while one was open for 19% -> 26% of each run, Pallas kernels for 0% -> 0%
where the time goes in v1:
time: 1290 us; the launch traced here: 1280 us
  waiting for transfers between devices  517 us (40%)
  local copies, waits for them, and re-layouts  308 us (24%)
  matrix products  202 us (16%)
  starting transfers between devices  186 us (14%)
  other arithmetic  58.6 us (5%)
    ppermute x3, waiting for transfers between devices, gather_dp(): mate_above = lax.ppermute(mate, 'dp', down)  93.3 us
    ppermute x8, waiting for transfers between devices, scatter_dp(): lax.ppermute((part(below ^ 1) + mate_first.astype(jnp.float32)).astype(lo...  70.5 us
    dot_general x8, matrix products, cols_inner(): lax.dot_general(matrix_left, matrix_right, (((1,), (1,)), ((), ())), pref...  67.6 us
    ppermute x4, waiting for transfers between devices, gather_tensor(): across = lax.ppermute(own, 'tensor', pairs_xor(size, 2))  59.5 us
    dynamic_slice x18, local copies, waits for them, and re-layouts, pick(): return lax.dynamic_index_in_dim(blocks, index, 0, keepdims=False)  56 us
    dot_general x8, matrix products, rows_inner(): lax.dot_general(matrix_left, matrix_right, (((0,), (0,)), ((), ())), pref...  46.5 us
    ppermute x3, waiting for transfers between devices, gather_dp(): mate_far = lax.ppermute(mate_above, 'dp', down)  45.4 us
    dynamic_update_slice x35, local copies, waits for them, and re-layouts, put(): return lax.dynamic_update_slice_in_dim(buffer, block[None], index, 0)  43.8 us
  transfers between devices with their start and end apart: 111, of which 56 were waited for; matrix products, arithmetic and copies ran while one was open for 26% of the time, Pallas kernels for 0%

profile of v1, /device:TPU:0, one launch (start us, length us, event | category | flops | bytes accessed | tf_op | source)
XLA Modules:
  0.0 1281.2 jit_solution(15516445401020684834)
XLA Ops:
  35.7 10.6 collective-permute-done.23
  68.5 13.4 %collective-permute-done.1 = bf16[256,1792]{1,0:T(8,128)(2,1)S(1)} collective-permute-done((bf16[256,1792]{1,0:T(8,128)(2,1)S(1)}, bf16[256,1792]{1,0:T(8,128)(2,1)S(1)}, u32[]{:S(2)}, u32[]{:S(2)}) %collective-permute-start.1) | collective-permute-done | bytes 917536 | tf_op jit(solution)/shard_map/ppermute | solution.py:265
  89.0 25.6 %collective-permute-done.4 = bf16[224,2240]{1,0:T(8,128)(2,1)S(1)} collective-permute-done((bf16[224,2240]{1,0:T(8,128)(2,1)S(1)}, bf16[224,2240]{1,0:T(8,128)(2,1)S(1)}, u32[]{:S(2)}, u32[]{:S(2)}) %collective-permute-start.4) | collective-permute-done | bytes 1003552 | tf_op jit(solution)/shard_map/ppermute | solution.py:205
  117.7 23.7 %collective-permute-done.5 = bf16[224,2240]{1,0:T(8,128)(2,1)S(1)} collective-permute-done((bf16[224,2240]{1,0:T(8,128)(2,1)S(1)}, bf16[224,2240]{1,0:T(8,128)(2,1)S(1)}, u32[]{:S(2)}, u32[]{:S(2)}) %collective-permute-start.5) | collective-permute-done | bytes 1003552 | tf_op jit(solution)/shard_map/ppermute | solution.py:206
  155.0 35.3 %collective-permute-done.27 = bf16[224,1216]{1,0:T(8,128)(2,1)} collective-permute-done((bf16[224,1216]{1,0:T(8,128)(2,1)}, bf16[224,1216]{1,0:T(8,128)(2,1)}, u32[]{:S(2)}, u32[]{:S(2)}) %collective-permute-start.27) | collective-permute-done | bytes 544800 | tf_op jit(solution)/shard_map/ppermute | solution.py:208
  199.7 58.1 %collective-permute-done.7 = bf16[224,2240]{1,0:T(8,128)(2,1)S(1)} collective-permute-done((bf16[224,2240]{1,0:T(8,128)(2,1)}, bf16[224,2240]{1,0:T(8,128)(2,1)S(1)}, u32[]{:S(2)}, u32[]{:S(2)}) %collective-permute-start.7) | collective-permute-done | bytes 1003552 | tf_op jit(solution)/shard_map/ppermute | solution.py:208
  263.1 45.4 %collective-permute-done.9 = bf16[224,2240]{1,0:T(8,128)(2,1)S(1)} collective-permute-done((bf16[224,2240]{1,0:T(8,128)(2,1)S(1)}, bf16[224,2240]{1,0:T(8,128)(2,1)S(1)}, u32[]{:S(2)}, u32[]{:S(2)}) %collective-permute-start.9) | collective-permute-done | bytes 1003552 | tf_op jit(solution)/shard_map/ppermute | solution.py:210
  330.1 60.5 %while.26 = (s32[]{:T(128)}, f32[2,512,448]{1,0,2:T(2,128)}, f32[2,7,512]{2,1,0:T(8,128)}, s32[2]{0:T(128)}, bf16[1088,448]{0,1:T(8,128)(2,1)S(1)}, /*index=5*/s...) while((s32[]{:T(128)}, f32[2,512,448]{1,0,2:T(2,128)}, ...), condition=%wide.region_4.5_spmd, body=%wide.region_1.0_spmd.sunk | while | flops 555021312 | bytes 35147244 | solution.py:112
  343.1 17.2 %dynamic_update_slice.230 = f32[2,512,448]{1,0,2:T(2,128)} dynamic-update-slice(f32[2,512,448]{1,0,2:T(2,128)} %get-tuple-element.491, f32[1,512,448]{1,0,2:T(1,128)S(1)} %copy.255, s32[]{:T(128)} %get-tuple-element.490, s32[]{:T(128)} %constant.345.clone.1..sunk, s32[]{:T(128)} %constant.345.clone.1..sunk) | dynamic-update-slice | bytes 1835012 | tf_op jit(solution)/shard_map/while/body/jit(dynamic_update_index_in_dim)/dynamic_update_slice | solution.py:112
  373.1 17.2 %dynamic_update_slice.230 = f32[2,512,448]{1,0,2:T(2,128)} dynamic-update-slice(f32[2,512,448]{1,0,2:T(2,128)} %get-tuple-element.491, f32[1,512,448]{1,0,2:T(1,128)S(1)} %copy.255, s32[]{:T(128)} %get-tuple-element.490, s32[]{:T(128)} %constant.345.clone.1..sunk, s32[]{:T(128)} %constant.345.clone.1..sunk) | dynamic-update-slice | bytes 1835012 | tf_op jit(solution)/shard_map/while/body/jit(dynamic_update_index_in_dim)/dynamic_update_slice | solution.py:112
  393.8 7.5 fusion.40
  409.8 13.0 %collective-permute-start.12 = (bf16[256,1792]{1,0:T(8,128)(2,1)S(1)}, bf16[256,1792]{1,0:T(8,128)(2,1)S(1)}, u32[]{:S(2)}, u32[]{:S(2)}) collective-permute-start(bf16[256,1792]{1,0:T(8,128)(2,1)S(1)} %fusion.58), channel_id=1, source_target_pairs={{0,2},{1,3},{2,0},{3,1},{4,6},{5,7},{6,4},{7,5},{8,10},{9,11},{10,... | collective-permute-start | bytes 2752520 | tf_op jit(solution)/shard_map/ppermute | solution.py:285
  427.4 15.9 %collective-permute-done.12 = bf16[256,1792]{1,0:T(8,128)(2,1)S(1)} collective-permute-done((bf16[256,1792]{1,0:T(8,128)(2,1)S(1)}, bf16[256,1792]{1,0:T(8,128)(2,1)S(1)}, u32[]{:S(2)}, u32[]{:S(2)}) %collective-permute-start.12) | collective-permute-done | bytes 917536 | tf_op jit(solution)/shard_map/ppermute | solution.py:285
  450.2 17.5 %collective-permute-done.14 = bf16[256,1792]{1,0:T(8,128)(2,1)S(1)} collective-permute-done((bf16[256,1792]{1,0:T(8,128)(2,1)S(1)}, bf16[256,1792]{1,0:T(8,128)(2,1)S(1)}, u32[]{:S(2)}, u32[]{:S(2)}) %collective-permute-start.14) | collective-permute-done | bytes 917536 | tf_op jit(solution)/shard_map/ppermute | solution.py:265
  470.3 8.6 fusion.27
  478.9 14.3 %multiply_convert_fusion.3 = (bf16[1024,1216]{0,1:T(8,128)(2,1)S(1)}, f32[1024,1216]{0,1:T(8,128)}) fusion(f32[1024,1216]{0,1:T(8,128)S(1)} %fusion.27, bf16[1024,1792]{1,0:T(8,128)(2,1)S(1)} %bitcast.498, bf16[1792,2432]{1,0:T(8,128)(2,1)} %bitcast.55), kind=kOutput, calls=%fused_computation.49 | convolution fusion | flops 4470210560 | bytes 20709376 | tf_op jit(solution)/shard_map/dot_general | solution.py:370
  493.2 8.3 fusion.36
  509.7 17.3 %collective-permute-done.34 = f32[8,128]{1,0:T(8,128)S(1)} collective-permute-done((f32[8,128]{1,0:T(8,128)S(1)}, f32[8,128]{1,0:T(8,128)S(1)}, u32[]{:S(2)}, u32[]{:S(2)}) %collective-permute-start.34) | collective-permute-done | bytes 4128 | tf_op jit(solution)/shard_map/ppermute | solution.py:305
  553.1 13.8 %collective-permute-done.39 = bf16[256,1792]{1,0:T(8,128)(2,1)} collective-permute-done((bf16[256,1792]{1,0:T(8,128)(2,1)}, bf16[256,1792]{1,0:T(8,128)(2,1)}, u32[]{:S(2)}, u32[]{:S(2)}) %collective-permute-start.39) | collective-permute-done | bytes 917536 | tf_op jit(solution)/shard_map/ppermute | solution.py:265
  572.5 8.6 convolution_convert_fusion
  581.1 12.1 multiply_convert_fusion.2
  593.2 8.8 convolution_convert_fusion.1
  602.1 12.1 fusion.21
  628.6 7.2 copy.208
  642.8 8.6 convolution_convert_fusion.2
  658.5 10.4 fusion.29
  679.3 12.3 collective-permute-done.97
  693.5 10.2 collective-permute-done.90
  703.7 10.4 collective-permute-done.94
  714.1 15.0 %collective-permute-start.109 = (bf16[224,1216]{1,0:T(8,128)(2,1)S(1)}, bf16[224,1216]{1,0:T(8,128)(2,1)S(1)}, u32[]{:S(2)}, u32[]{:S(2)}) collective-permute-start(bf16[224,1216]{1,0:T(8,128)(2,1)S(1)} %get-tuple-element.248), channel_id=1, source_target_pairs={{0,24},{4,28},{8,0},{12,4},{16,8},{20,12},{24,16},{28,20},{1,25},{... | collective-permute-start | bytes 1634312 | tf_op jit(solution)/shard_map/ppermute | solution.py:244
  731.7 21.0 %collective-permute-done.109 = bf16[224,1216]{1,0:T(8,128)(2,1)S(1)} collective-permute-done((bf16[224,1216]{1,0:T(8,128)(2,1)S(1)}, bf16[224,1216]{1,0:T(8,128)(2,1)S(1)}, u32[]{:S(2)}, u32[]{:S(2)}) %collective-permute-start.109) | collective-permute-done | bytes 544800 | tf_op jit(solution)/shard_map/ppermute | solution.py:244
  756.1 9.5 collective-permute-start.105
  765.6 9.1 collective-permute-done.102
  779.8 8.3 collective-permute-done.95
  796.1 8.4 collective-permute-done.105
  804.5 16.6 %collective-permute-start.92 = (bf16[224,1216]{1,0:T(8,128)(2,1)}, bf16[224,1216]{1,0:T(8,128)(2,1)S(1)}, u32[]{:S(2)}, u32[]{:S(2)}) collective-permute-start(bf16[224,1216]{1,0:T(8,128)(2,1)} %get-tuple-element.264), channel_id=1, source_target_pairs={{0,24},{4,28},{8,0},{12,4},{16,8},{20,12},{24,16},{28,20},{1,25},{... | collective-permute-start | bytes 1634312 | tf_op jit(solution)/shard_map/ppermute | solution.py:243
  830.7 14.1 %collective-permute-done.98 = bf16[224,1216]{1,0:T(8,128)(2,1)S(1)} collective-permute-done((bf16[224,1216]{1,0:T(8,128)(2,1)S(1)}, bf16[224,1216]{1,0:T(8,128)(2,1)S(1)}, u32[]{:S(2)}, u32[]{:S(2)}) %collective-permute-start.98) | collective-permute-done | bytes 544800 | tf_op jit(solution)/shard_map/ppermute | solution.py:247
  852.9 14.8 %collective-permute-done.45 = bf16[256,1792]{1,0:T(8,128)(2,1)S(1)} collective-permute-done((bf16[256,1792]{1,0:T(8,128)(2,1)S(1)}, bf16[256,1792]{1,0:T(8,128)(2,1)S(1)}, u32[]{:S(2)}, u32[]{:S(2)}) %collective-permute-start.45) | collective-permute-done | bytes 917536 | tf_op jit(solution)/shard_map/ppermute | solution.py:265
  883.0 74.2 %while.27 = (s32[]{:T(128)}, f32[1088,448]{0,1:T(8,128)}, f32[1088,448]{0,1:T(8,128)}, bf16[2,512,448]{1,2,0:T(8,128)(2,1)}, s32[2]{0:T(128)S(1)}, /*index=5*/bf...) while((s32[]{:T(128)}, f32[1088,448]{0,1:T(8,128)}, ...), condition=%wide.region_13.14_spmd, body=%wide.region_11.13_spmd.sunk | while | flops 1355170816 | bytes 131067112 | solution.py:175
  963.1 7.8 fusion.67
  1015.6 15.9 %constant_dynamic-slice_fusion.15 = (bf16[1,224,448]{1,0,2:T(2,128)(2,1)}, bf16[1,224,448]{1,0,2:T(2,128)(2,1)}, bf16[1,224,448]{1,0,2:T(2,128)(2,1)}, bf16[1,22...) fusion(bf16[8,224,448]{1,0,2:T(8,128)(2,1)S(1)} %reshape.379, ...), kind=kLoop, calls=%fused_computation.313 | loop fusion | bytes 6422560 | tf_op jit(solution)/shard_map/jit(dynamic_index_in_dim)/dynamic_slice | solution.py:194
  1068.4 15.9 %constant_dynamic-slice_fusion.31 = (bf16[1,224,448]{1,0,2:T(2,128)(2,1)}, bf16[1,224,448]{1,0,2:T(2,128)(2,1)}, bf16[1,224,448]{1,0,2:T(2,128)(2,1)}, bf16[1,22...) fusion(bf16[8,224,448]{1,0,2:T(8,128)(2,1)} %reshape.377, ...), kind=kLoop, calls=%fused_computation.329 | loop fusion | bytes 6422560 | tf_op jit(solution)/shard_map/jit(dynamic_index_in_dim)/dynamic_slice | solution.py:194
  1108.1 11.4 add_add_fusion
  1131.5 9.2 collective-permute-done.69
  1164.0 7.7 collective-permute-done.81
  1187.5 8.2 collective-permute-done.67
  1196.2 8.0 collective-permute-done.60
  1235.8 9.1 collective-permute-done.63
  (720 shorter events, 597.7 us)
Async XLA Ops:
  6.0 136.5 %collective-permute-start.16 = (bf16[224,2432]{1,0:T(8,128)(2,1)S(1)}, bf16[224,2432]{1,0:T(8,128)(2,1)}, u32[]{:S(2)}, u32[]{:S(2)}) collective-permute-start(bf16[224,2432]{1,0:T(8,128)(2,1)S(1)} %get-tuple-element.220), channel_id=1, source_target_pairs={{0,4},{4,0},{8,12},{12,8},{16,20},{20,16},{24,28},{28,24},{1,5},{5... | collective-permute-start | bytes 3268616 | tf_op jit(solution)/shard_map/ppermute | solution.py:204
  9.1 137.9 %collective-permute-start.17 = (bf16[224,2432]{1,0:T(8,128)(2,1)S(1)}, bf16[224,2432]{1,0:T(8,128)(2,1)}, u32[]{:S(2)}, u32[]{:S(2)}) collective-permute-start(bf16[224,2432]{1,0:T(8,128)(2,1)S(1)} %get-tuple-element.220), channel_id=1, source_target_pairs={{0,8},{4,12},{8,16},{12,20},{16,24},{20,28},{24,0},{28,4},{1,9},{5... | collective-permute-start | bytes 3268616 | tf_op jit(solution)/shard_map/ppermute | solution.py:205
  10.6 35.7 %collective-permute-start.23 = (bf16[224,1216]{1,0:T(8,128)(2,1)}, bf16[224,1216]{1,0:T(8,128)(2,1)}, u32[]{:S(2)}, u32[]{:S(2)}) collective-permute-start(bf16[224,1216]{1,0:T(8,128)(2,1)} %bitcast.56), channel_id=1, source_target_pairs={{0,4},{4,0},{8,12},{12,8},{16,20},{20,16},{24,28},{28,24},{1,5},{5... | collective-permute-start | bytes 1634312 | tf_op jit(solution)/shard_map/ppermute | solution.py:204
  11.1 41.2 %collective-permute-start.24 = (bf16[224,1216]{1,0:T(8,128)(2,1)}, bf16[224,1216]{1,0:T(8,128)(2,1)}, u32[]{:S(2)}, u32[]{:S(2)}) collective-permute-start(bf16[224,1216]{1,0:T(8,128)(2,1)} %bitcast.56), channel_id=1, source_target_pairs={{0,8},{4,12},{8,16},{12,20},{16,24},{20,28},{24,0},{28,4},{1,9},{5... | collective-permute-start | bytes 1634312 | tf_op jit(solution)/shard_map/ppermute | solution.py:205
  14.0 68.9 %collective-permute-start.3 = (bf16[224,2240]{1,0:T(8,128)(2,1)S(1)}, bf16[224,2240]{1,0:T(8,128)(2,1)}, u32[]{:S(2)}, u32[]{:S(2)}) collective-permute-start(bf16[224,2240]{1,0:T(8,128)(2,1)S(1)} %concatenate.49), channel_id=1, source_target_pairs={{0,4},{4,0},{8,12},{12,8},{16,20},{20,16},{24,28},{28,24},{1,5},{5... | collective-permute-start | bytes 3010568 | tf_op jit(solution)/shard_map/ppermute | solution.py:204
  63.3 86.0 %collective-permute-start.18 = (bf16[224,2432]{1,0:T(8,128)(2,1)S(1)}, bf16[224,2432]{1,0:T(8,128)(2,1)S(1)}, u32[]{:S(2)}, u32[]{:S(2)}) collective-permute-start(bf16[224,2432]{1,0:T(8,128)(2,1)S(1)} %get-tuple-element.220), channel_id=1, source_target_pairs={{0,24},{4,28},{8,0},{12,4},{16,8},{20,12},{24,16},{28,20},{1,25},{... | collective-permute-start | bytes 3268616 | tf_op jit(solution)/shard_map/ppermute | solution.py:206
  82.9 58.5 %collective-permute-start.5 = (bf16[224,2240]{1,0:T(8,128)(2,1)S(1)}, bf16[224,2240]{1,0:T(8,128)(2,1)S(1)}, u32[]{:S(2)}, u32[]{:S(2)}) collective-permute-start(bf16[224,2240]{1,0:T(8,128)(2,1)S(1)} %concatenate.49), channel_id=1, source_target_pairs={{0,24},{4,28},{8,0},{12,4},{16,8},{20,12},{24,16},{28,20},{1,25},{... | collective-permute-start | bytes 3010568 | tf_op jit(solution)/shard_map/ppermute | solution.py:206
  114.6 35.8 %collective-permute-start.26 = (bf16[224,1216]{1,0:T(8,128)(2,1)}, bf16[224,1216]{1,0:T(8,128)(2,1)S(1)}, u32[]{:S(2)}, u32[]{:S(2)}) collective-permute-start(bf16[224,1216]{1,0:T(8,128)(2,1)} %collective-permute-done.23), channel_id=1, source_target_pairs={{0,8},{4,12},{8,16},{12,20},{16,24},{20,28},{24,0},{28,4},{1,9},{5... | collective-permute-start | bytes 1634312 | tf_op jit(solution)/shard_map/ppermute | solution.py:207
  141.4 48.9 %collective-permute-start.27 = (bf16[224,1216]{1,0:T(8,128)(2,1)}, bf16[224,1216]{1,0:T(8,128)(2,1)}, u32[]{:S(2)}, u32[]{:S(2)}) collective-permute-start(bf16[224,1216]{1,0:T(8,128)(2,1)} %collective-permute-done.23), channel_id=1, source_target_pairs={{0,24},{4,28},{8,0},{12,4},{16,8},{20,12},{24,16},{28,20},{1,25},{... | collective-permute-start | bytes 1634312 | tf_op jit(solution)/shard_map/ppermute | solution.py:208
  142.5 263.1 %collective-permute-start.28 = (bf16[224,1216]{1,0:T(8,128)(2,1)}, bf16[224,1216]{1,0:T(8,128)(2,1)}, u32[]{:S(2)}, u32[]{:S(2)}) collective-permute-start(bf16[224,1216]{1,0:T(8,128)(2,1)} %collective-permute-done.24), channel_id=1, source_target_pairs={{0,8},{4,12},{8,16},{12,20},{16,24},{20,28},{24,0},{28,4},{1,9},{5... | collective-permute-start | bytes 1634312 | tf_op jit(solution)/shard_map/ppermute | solution.py:209
  147.0 45.3 %collective-permute-start.2 = (bf16[256,1792]{1,0:T(8,128)(2,1)S(1)}, bf16[256,1792]{1,0:T(8,128)(2,1)S(1)}, u32[]{:S(2)}, u32[]{:S(2)}) collective-permute-start(bf16[256,1792]{1,0:T(8,128)(2,1)S(1)} %collective-permute-done.1), channel_id=1, source_target_pairs={{0,1},{1,0},{2,3},{3,2},{4,5},{5,4},{6,7},{7,6},{8,9},{9,8},{10,11... | collective-permute-start | bytes 2752520 | tf_op jit(solution)/shard_map/ppermute | solution.py:267
  149.3 46.5 %collective-permute-start.6 = (bf16[224,2240]{1,0:T(8,128)(2,1)}, bf16[224,2240]{1,0:T(8,128)(2,1)S(1)}, u32[]{:S(2)}, u32[]{:S(2)}) collective-permute-start(bf16[224,2240]{1,0:T(8,128)(2,1)} %collective-permute-done.3), channel_id=1, source_target_pairs={{0,8},{4,12},{8,16},{12,20},{16,24},{20,28},{24,0},{28,4},{1,9},{5... | collective-permute-start | bytes 3010568 | tf_op jit(solution)/shard_map/ppermute | solution.py:207
  150.4 107.4 %collective-permute-start.7 = (bf16[224,2240]{1,0:T(8,128)(2,1)}, bf16[224,2240]{1,0:T(8,128)(2,1)S(1)}, u32[]{:S(2)}, u32[]{:S(2)}) collective-permute-start(bf16[224,2240]{1,0:T(8,128)(2,1)} %collective-permute-done.3), channel_id=1, source_target_pairs={{0,24},{4,28},{8,0},{12,4},{16,8},{20,12},{24,16},{28,20},{1,25},{... | collective-permute-start | bytes 3010568 | tf_op jit(solution)/shard_map/ppermute | solution.py:208
  190.3 69.5 %collective-permute-start.8 = (bf16[224,2240]{1,0:T(8,128)(2,1)S(1)}, bf16[224,2240]{1,0:T(8,128)(2,1)S(1)}, u32[]{:S(2)}, u32[]{:S(2)}) collective-permute-start(bf16[224,2240]{1,0:T(8,128)(2,1)S(1)} %collective-permute-done.4), channel_id=1, source_target_pairs={{0,8},{4,12},{8,16},{12,20},{16,24},{20,28},{24,0},{28,4},{1,9},{5... | collective-permute-start | bytes 3010568 | tf_op jit(solution)/shard_map/ppermute | solution.py:209
  192.2 230.5 %collective-permute-start.19 = (bf16[224,2432]{1,0:T(8,128)(2,1)}, bf16[224,2432]{1,0:T(8,128)(2,1)}, u32[]{:S(2)}, u32[]{:S(2)}) collective-permute-start(bf16[224,2432]{1,0:T(8,128)(2,1)} %collective-permute-done.16), channel_id=1, source_target_pairs={{0,8},{4,12},{8,16},{12,20},{16,24},{20,28},{24,0},{28,4},{1,9},{5... | collective-permute-start | bytes 3268616 | tf_op jit(solution)/shard_map/ppermute | solution.py:207
  195.8 212.7 %collective-permute-start.20 = (bf16[224,2432]{1,0:T(8,128)(2,1)}, bf16[224,2432]{1,0:T(8,128)(2,1)}, u32[]{:S(2)}, u32[]{:S(2)}) collective-permute-start(bf16[224,2432]{1,0:T(8,128)(2,1)} %collective-permute-done.16), channel_id=1, source_target_pairs={{0,24},{4,28},{8,0},{12,4},{16,8},{20,12},{24,16},{28,20},{1,25},{... | collective-permute-start | bytes 3268616 | tf_op jit(solution)/shard_map/ppermute | solution.py:208
  257.7 50.8 %collective-permute-start.9 = (bf16[224,2240]{1,0:T(8,128)(2,1)S(1)}, bf16[224,2240]{1,0:T(8,128)(2,1)S(1)}, u32[]{:S(2)}, u32[]{:S(2)}) collective-permute-start(bf16[224,2240]{1,0:T(8,128)(2,1)S(1)} %collective-permute-done.7), channel_id=1, source_target_pairs={{0,24},{4,28},{8,0},{12,4},{16,8},{20,12},{24,16},{28,20},{1,25},{... | collective-permute-start | bytes 3010568 | tf_op jit(solution)/shard_map/ppermute | solution.py:210
  259.8 187.0 %collective-permute-start.21 = (bf16[224,2432]{1,0:T(8,128)(2,1)}, bf16[224,2432]{1,0:T(8,128)(2,1)}, u32[]{:S(2)}, u32[]{:S(2)}) collective-permute-start(bf16[224,2432]{1,0:T(8,128)(2,1)} %collective-permute-done.17), channel_id=1, source_target_pairs={{0,8},{4,12},{8,16},{12,20},{16,24},{20,28},{24,0},{28,4},{1,9},{5... | collective-permute-start | bytes 3268616 | tf_op jit(solution)/shard_map/ppermute | solution.py:209
  308.5 99.1 %collective-permute-start.29 = (bf16[224,1216]{1,0:T(8,128)(2,1)}, bf16[224,1216]{1,0:T(8,128)(2,1)S(1)}, u32[]{:S(2)}, u32[]{:S(2)}) collective-permute-start(bf16[224,1216]{1,0:T(8,128)(2,1)} %collective-permute-done.27), channel_id=1, source_target_pairs={{0,24},{4,28},{8,0},{12,4},{16,8},{20,12},{24,16},{28,20},{1,25},{... | collective-permute-start | bytes 1634312 | tf_op jit(solution)/shard_map/ppermute | solution.py:210
  408.5 40.6 %collective-permute-start.22 = (bf16[224,2432]{1,0:T(8,128)(2,1)}, bf16[224,2432]{1,0:T(8,128)(2,1)S(1)}, u32[]{:S(2)}, u32[]{:S(2)}) collective-permute-start(bf16[224,2432]{1,0:T(8,128)(2,1)} %collective-permute-done.20), channel_id=1, source_target_pairs={{0,24},{4,28},{8,0},{12,4},{16,8},{20,12},{24,16},{28,20},{1,25},{... | collective-permute-start | bytes 3268616 | tf_op jit(solution)/shard_map/ppermute | solution.py:210
  501.9 39.6 %collective-permute-start.30 = (bf16[256,1792]{1,0:T(8,128)(2,1)S(1)}, bf16[256,1792]{1,0:T(8,128)(2,1)S(1)}, u32[]{:S(2)}, u32[]{:S(2)}) collective-permute-start(bf16[256,1792]{1,0:T(8,128)(2,1)S(1)} %get-tuple-element.243), channel_id=1, source_target_pairs={{0,1},{1,0},{2,3},{3,2},{4,5},{5,4},{6,7},{7,6},{8,9},{9,8},{10,11... | collective-permute-start | bytes 2752520 | tf_op jit(solution)/shard_map/ppermute | solution.py:286
  504.4 37.1 %collective-permute-start.32 = (bf16[256,1792]{1,0:T(8,128)(2,1)S(1)}, bf16[256,1792]{1,0:T(8,128)(2,1)S(1)}, u32[]{:S(2)}, u32[]{:S(2)}) collective-permute-start(bf16[256,1792]{1,0:T(8,128)(2,1)S(1)} %fusion.55), channel_id=1, source_target_pairs={{0,2},{1,3},{2,0},{3,1},{4,6},{5,7},{6,4},{7,5},{8,10},{9,11},{10,... | collective-permute-start | bytes 2752520 | tf_op jit(solution)/shard_map/ppermute | solution.py:285
  624.3 45.7 %collective-permute-start.104 = (bf16[224,1216]{1,0:T(8,128)(2,1)}, bf16[224,1216]{1,0:T(8,128)(2,1)}, u32[]{:S(2)}, u32[]{:S(2)}) collective-permute-start(bf16[224,1216]{1,0:T(8,128)(2,1)} %get-tuple-element.249), channel_id=1, source_target_pairs={{0,8},{4,12},{8,16},{12,20},{16,24},{20,28},{24,0},{28,4},{1,9},{5... | collective-permute-start | bytes 1634312 | tf_op jit(solution)/shard_map/ppermute | solution.py:240
  624.4 45.7 %collective-permute-start.108 = (bf16[224,1216]{1,0:T(8,128)(2,1)}, bf16[224,1216]{1,0:T(8,128)(2,1)}, u32[]{:S(2)}, u32[]{:S(2)}) collective-permute-start(bf16[224,1216]{1,0:T(8,128)(2,1)} %get-tuple-element.250), channel_id=1, source_target_pairs={{0,24},{4,28},{8,0},{12,4},{16,8},{20,12},{24,16},{28,20},{1,25},{... | collective-permute-start | bytes 1634312 | tf_op jit(solution)/shard_map/ppermute | solution.py:241
  628.2 103.4 %collective-permute-start.107 = (bf16[224,1216]{1,0:T(8,128)(2,1)}, bf16[224,1216]{1,0:T(8,128)(2,1)S(1)}, u32[]{:S(2)}, u32[]{:S(2)}) collective-permute-start(bf16[224,1216]{1,0:T(8,128)(2,1)} %get-tuple-element.251), channel_id=1, source_target_pairs={{0,8},{4,12},{8,16},{12,20},{16,24},{20,28},{24,0},{28,4},{1,9},{5... | collective-permute-start | bytes 1634312 | tf_op jit(solution)/shard_map/ppermute | solution.py:242
  638.9 38.4 %collective-permute-start.101 = (bf16[224,1216]{1,0:T(8,128)(2,1)}, bf16[224,1216]{1,0:T(8,128)(2,1)}, u32[]{:S(2)}, u32[]{:S(2)}) collective-permute-start(bf16[224,1216]{1,0:T(8,128)(2,1)} %get-tuple-element.256), channel_id=1, source_target_pairs={{0,24},{4,28},{8,0},{12,4},{16,8},{20,12},{24,16},{28,20},{1,25},{... | collective-permute-start | bytes 1634312 | tf_op jit(solution)/shard_map/ppermute | solution.py:241
  642.7 48.9 %collective-permute-start.97 = (bf16[224,1216]{1,0:T(8,128)(2,1)}, bf16[224,1216]{1,0:T(8,128)(2,1)}, u32[]{:S(2)}, u32[]{:S(2)}) collective-permute-start(bf16[224,1216]{1,0:T(8,128)(2,1)} %get-tuple-element.255), channel_id=1, source_target_pairs={{0,8},{4,12},{8,16},{12,20},{16,24},{20,28},{24,0},{28,4},{1,9},{5... | collective-permute-start | bytes 1634312 | tf_op jit(solution)/shard_map/ppermute | solution.py:240
  670.2 44.0 %collective-permute-start.94 = (bf16[224,1216]{1,0:T(8,128)(2,1)S(1)}, bf16[224,1216]{1,0:T(8,128)(2,1)S(1)}, u32[]{:S(2)}, u32[]{:S(2)}) collective-permute-start(bf16[224,1216]{1,0:T(8,128)(2,1)S(1)} %get-tuple-element.262), channel_id=1, source_target_pairs={{0,24},{4,28},{8,0},{12,4},{16,8},{20,12},{24,16},{28,20},{1,25},{... | collective-permute-start | bytes 1634312 | tf_op jit(solution)/shard_map/ppermute | solution.py:241
  677.4 112.7 %collective-permute-start.106 = (bf16[224,1216]{1,0:T(8,128)(2,1)S(1)}, bf16[224,1216]{1,0:T(8,128)(2,1)S(1)}, u32[]{:S(2)}, u32[]{:S(2)}) collective-permute-start(bf16[224,1216]{1,0:T(8,128)(2,1)S(1)} %copy-done.74), channel_id=1, source_target_pairs={{0,24},{4,28},{8,0},{12,4},{16,8},{20,12},{24,16},{28,20},{1,25},{... | collective-permute-start | bytes 1634312 | tf_op jit(solution)/shard_map/ppermute | solution.py:243
  691.6 37.7 %collective-permute-start.42 = (bf16[256,1792]{1,0:T(8,128)(2,1)S(1)}, bf16[256,1792]{1,0:T(8,128)(2,1)S(1)}, u32[]{:S(2)}, u32[]{:S(2)}) collective-permute-start(bf16[256,1792]{1,0:T(8,128)(2,1)S(1)} %get-tuple-element.242), channel_id=1, source_target_pairs={{0,1},{1,0},{2,3},{3,2},{4,5},{5,4},{6,7},{7,6},{8,9},{9,8},{10,11... | collective-permute-start | bytes 2752520 | tf_op jit(solution)/shard_map/ppermute | solution.py:283
  703.7 52.3 %collective-permute-start.100 = (bf16[224,1216]{1,0:T(8,128)(2,1)S(1)}, bf16[224,1216]{1,0:T(8,128)(2,1)S(1)}, u32[]{:S(2)}, u32[]{:S(2)}) collective-permute-start(bf16[224,1216]{1,0:T(8,128)(2,1)S(1)} %copy-done.75), channel_id=1, source_target_pairs={{0,8},{4,12},{8,16},{12,20},{16,24},{20,28},{24,0},{28,4},{1,9},{5... | collective-permute-start | bytes 1634312 | tf_op jit(solution)/shard_map/ppermute | solution.py:242
  714.1 38.5 %collective-permute-start.109 = (bf16[224,1216]{1,0:T(8,128)(2,1)S(1)}, bf16[224,1216]{1,0:T(8,128)(2,1)S(1)}, u32[]{:S(2)}, u32[]{:S(2)}) collective-permute-start(bf16[224,1216]{1,0:T(8,128)(2,1)S(1)} %get-tuple-element.248), channel_id=1, source_target_pairs={{0,24},{4,28},{8,0},{12,4},{16,8},{20,12},{24,16},{28,20},{1,25},{... | collective-permute-start | bytes 1634312 | tf_op jit(solution)/shard_map/ppermute | solution.py:244
  729.4 45.3 %collective-permute-start.102 = (bf16[224,1216]{1,0:T(8,128)(2,1)S(1)}, bf16[224,1216]{1,0:T(8,128)(2,1)S(1)}, u32[]{:S(2)}, u32[]{:S(2)}) collective-permute-start(bf16[224,1216]{1,0:T(8,128)(2,1)S(1)} %get-tuple-element.254), channel_id=1, source_target_pairs={{0,24},{4,28},{8,0},{12,4},{16,8},{20,12},{24,16},{28,20},{1,25},{... | collective-permute-start | bytes 1634312 | tf_op jit(solution)/shard_map/ppermute | solution.py:244
  731.6 48.3 %collective-permute-start.93 = (bf16[224,1216]{1,0:T(8,128)(2,1)S(1)}, bf16[224,1216]{1,0:T(8,128)(2,1)S(1)}, u32[]{:S(2)}, u32[]{:S(2)}) collective-permute-start(bf16[224,1216]{1,0:T(8,128)(2,1)S(1)} %get-tuple-element.263), channel_id=1, source_target_pairs={{0,8},{4,12},{8,16},{12,20},{16,24},{20,28},{24,0},{28,4},{1,9},{5... | collective-permute-start | bytes 1634312 | tf_op jit(solution)/shard_map/ppermute | solution.py:242
  756.1 48.5 %collective-permute-start.105 = (bf16[224,1216]{1,0:T(8,128)(2,1)S(1)}, bf16[224,1216]{1,0:T(8,128)(2,1)S(1)}, u32[]{:S(2)}, u32[]{:S(2)}) collective-permute-start(bf16[224,1216]{1,0:T(8,128)(2,1)S(1)} %get-tuple-element.247), channel_id=1, source_target_pairs={{0,8},{4,12},{8,16},{12,20},{16,24},{20,28},{24,0},{28,4},{1,9},{5... | collective-permute-start | bytes 1634312 | tf_op jit(solution)/shard_map/ppermute | solution.py:247
  774.6 46.5 %collective-permute-start.110 = (bf16[224,1216]{1,0:T(8,128)(2,1)S(1)}, bf16[224,1216]{1,0:T(8,128)(2,1)S(1)}, u32[]{:S(2)}, u32[]{:S(2)}) collective-permute-start(bf16[224,1216]{1,0:T(8,128)(2,1)S(1)} %fusion.96), channel_id=1, source_target_pairs={{0,4},{4,0},{8,12},{12,8},{16,20},{20,16},{24,28},{28,24},{1,5},{5... | collective-permute-start | bytes 1634312 | tf_op jit(solution)/shard_map/ppermute | solution.py:255
  779.8 43.6 %collective-permute-start.41 = (bf16[256,1792]{1,0:T(8,128)(2,1)S(1)}, bf16[256,1792]{1,0:T(8,128)(2,1)S(1)}, u32[]{:S(2)}, u32[]{:S(2)}) collective-permute-start(bf16[256,1792]{1,0:T(8,128)(2,1)S(1)} %get-tuple-element.241), channel_id=1, source_target_pairs={{0,1},{1,0},{2,3},{3,2},{4,5},{5,4},{6,7},{7,6},{8,9},{9,8},{10,11... | collective-permute-start | bytes 2752520 | tf_op jit(solution)/shard_map/ppermute | solution.py:286
  788.1 35.5 %collective-permute-start.43 = (bf16[256,1792]{1,0:T(8,128)(2,1)S(1)}, bf16[256,1792]{1,0:T(8,128)(2,1)S(1)}, u32[]{:S(2)}, u32[]{:S(2)}) collective-permute-start(bf16[256,1792]{1,0:T(8,128)(2,1)S(1)} %fusion.53), channel_id=1, source_target_pairs={{0,2},{1,3},{2,0},{3,1},{4,6},{5,7},{6,4},{7,5},{8,10},{9,11},{10,... | collective-permute-start | bytes 2752520 | tf_op jit(solution)/shard_map/ppermute | solution.py:285
  790.1 38.9 %collective-permute-start.99 = (bf16[224,1216]{1,0:T(8,128)(2,1)S(1)}, bf16[224,1216]{1,0:T(8,128)(2,1)S(1)}, u32[]{:S(2)}, u32[]{:S(2)}) collective-permute-start(bf16[224,1216]{1,0:T(8,128)(2,1)S(1)} %copy-done.73), channel_id=1, source_target_pairs={{0,24},{4,28},{8,0},{12,4},{16,8},{20,12},{24,16},{28,20},{1,25},{... | collective-permute-start | bytes 1634312 | tf_op jit(solution)/shard_map/ppermute | solution.py:243
  804.5 44.4 %collective-permute-start.92 = (bf16[224,1216]{1,0:T(8,128)(2,1)}, bf16[224,1216]{1,0:T(8,128)(2,1)S(1)}, u32[]{:S(2)}, u32[]{:S(2)}) collective-permute-start(bf16[224,1216]{1,0:T(8,128)(2,1)} %get-tuple-element.264), channel_id=1, source_target_pairs={{0,24},{4,28},{8,0},{12,4},{16,8},{20,12},{24,16},{28,20},{1,25},{... | collective-permute-start | bytes 1634312 | tf_op jit(solution)/shard_map/ppermute | solution.py:243
  997.2 122.7 %collective-permute-start.83 = (bf16[224,448]{1,0:T(8,128)(2,1)}, bf16[224,448]{1,0:T(8,128)(2,1)}, u32[]{:S(2)}, u32[]{:S(2)}) collective-permute-start(bf16[224,448]{1,0:T(8,128)(2,1)} %get-tuple-element.267), channel_id=1, source_target_pairs={{0,8},{4,12},{8,16},{12,20},{16,24},{20,28},{24,0},{28,4},{1,9},{5... | collective-permute-start | bytes 602120 | tf_op jit(solution)/shard_map/ppermute | solution.py:240
  997.2 123.2 %collective-permute-start.87 = (bf16[224,448]{1,0:T(8,128)(2,1)}, bf16[224,448]{1,0:T(8,128)(2,1)}, u32[]{:S(2)}, u32[]{:S(2)}) collective-permute-start(bf16[224,448]{1,0:T(8,128)(2,1)} %get-tuple-element.268), channel_id=1, source_target_pairs={{0,24},{4,28},{8,0},{12,4},{16,8},{20,12},{24,16},{28,20},{1,25},{... | collective-permute-start | bytes 602120 | tf_op jit(solution)/shard_map/ppermute | solution.py:241
  1001.1 204.9 %collective-permute-start.86 = (bf16[224,448]{1,0:T(8,128)(2,1)}, bf16[224,448]{1,0:T(8,128)(2,1)}, u32[]{:S(2)}, u32[]{:S(2)}) collective-permute-start(bf16[224,448]{1,0:T(8,128)(2,1)} %get-tuple-element.269), channel_id=1, source_target_pairs={{0,8},{4,12},{8,16},{12,20},{16,24},{20,28},{24,0},{28,4},{1,9},{5... | collective-permute-start | bytes 602120 | tf_op jit(solution)/shard_map/ppermute | solution.py:242
  1033.6 91.9 %collective-permute-start.76 = (bf16[224,448]{1,0:T(8,128)(2,1)}, bf16[224,448]{1,0:T(8,128)(2,1)}, u32[]{:S(2)}, u32[]{:S(2)}) collective-permute-start(bf16[224,448]{1,0:T(8,128)(2,1)} %bitcast.122), channel_id=1, source_target_pairs={{0,8},{4,12},{8,16},{12,20},{16,24},{20,28},{24,0},{28,4},{1,9},{5... | collective-permute-start | bytes 602120 | tf_op jit(solution)/shard_map/ppermute | solution.py:240
  1037.3 89.4 %collective-permute-start.80 = (bf16[224,448]{1,0:T(8,128)(2,1)}, bf16[224,448]{1,0:T(8,128)(2,1)}, u32[]{:S(2)}, u32[]{:S(2)}) collective-permute-start(bf16[224,448]{1,0:T(8,128)(2,1)} %bitcast.127), channel_id=1, source_target_pairs={{0,24},{4,28},{8,0},{12,4},{16,8},{20,12},{24,16},{28,20},{1,25},{... | collective-permute-start | bytes 602120 | tf_op jit(solution)/shard_map/ppermute | solution.py:241
  1120.5 43.4 %collective-permute-start.79 = (bf16[224,448]{1,0:T(8,128)(2,1)S(1)}, bf16[224,448]{1,0:T(8,128)(2,1)S(1)}, u32[]{:S(2)}, u32[]{:S(2)}) collective-permute-start(bf16[224,448]{1,0:T(8,128)(2,1)S(1)} %bitcast.514), channel_id=1, source_target_pairs={{0,8},{4,12},{8,16},{12,20},{16,24},{20,28},{24,0},{28,4},{1,9},{5... | collective-permute-start | bytes 602120 | tf_op jit(solution)/shard_map/ppermute | solution.py:242
  1120.6 89.5 %collective-permute-start.78 = (bf16[224,448]{1,0:T(8,128)(2,1)S(1)}, bf16[224,448]{1,0:T(8,128)(2,1)S(1)}, u32[]{:S(2)}, u32[]{:S(2)}) collective-permute-start(bf16[224,448]{1,0:T(8,128)(2,1)S(1)} %bitcast.512), channel_id=1, source_target_pairs={{0,24},{4,28},{8,0},{12,4},{16,8},{20,12},{24,16},{28,20},{1,25},{... | collective-permute-start | bytes 602120 | tf_op jit(solution)/shard_map/ppermute | solution.py:243
  1221.0 41.9 %collective-permute-start.85 = (bf16[224,448]{1,0:T(8,128)(2,1)S(1)}, bf16[224,448]{1,0:T(8,128)(2,1)S(1)}, u32[]{:S(2)}, u32[]{:S(2)}) collective-permute-start(bf16[224,448]{1,0:T(8,128)(2,1)S(1)} %copy-done.82), channel_id=1, source_target_pairs={{0,24},{4,28},{8,0},{12,4},{16,8},{20,12},{24,16},{28,20},{1,25},{... | collective-permute-start | bytes 602120 | tf_op jit(solution)/shard_map/ppermute | solution.py:243
  (195 other events, 2801.9 us)

commit v2 on v1

--- a/solution.py
+++ b/solution.py
@@ -1,6 +1,8 @@
 import jax
 import jax.numpy as jnp
 from jax import lax
+from jax.experimental import pallas as pl
+from jax.experimental.pallas import tpu as pltpu
 from jax.sharding import PartitionSpec as P
 
 D = 1792
@@ -8,9 +10,9 @@
 WINDOW = 64
 CONV = 3
 BLOCK = 512
-
-
 EPS = 1e-05
+MESH = pl.DeviceIdType.MESH
+VMEM_LIMIT = 62 * 2**20
 
 
 def rms_scale(values):
@@ -306,7 +308,1166 @@
     return values
 
 
-def on_device(
+TILE = 64
+LANES = 128
+
+
+def neighbours():
+    d, t = lax.axis_index("dp"), lax.axis_index("tensor")
+    z, y = d // 2, lax.rem(d, 2)
+    core = t + 1 - 2 * lax.rem(t, 2)
+    place = z + y * (7 - 2 * z)
+
+    def ring(offset):
+        position = lax.rem(place + offset + 16, 8)
+        side = position // 4
+        return 2 * (position + side * (7 - 2 * position)) + side
+
+    return dict(
+        d=d,
+        t=t,
+        ring=ring,
+        core=core,
+        cross=lax.rem(t + 2, 4),
+        cross_core=lax.rem(core + 2, 4),
+        mate=d + 1 - 2 * y,
+        z_pair=2 * (z + 1 - 2 * lax.rem(z, 2)) + y,
+        z_mirror=2 * (3 - z) + y,
+    )
+
+
+def greet(at, everyone=False):
+    d, t = at["d"], at["t"]
+    devices = [(at["ring"](1), t), (at["ring"](-1), t), (d, at["core"]), (d, at["cross"])]
+    if everyone:
+        devices += [(at["mate"], t), (at["z_pair"], t), (at["z_mirror"], t)]
+    barrier = pltpu.get_barrier_semaphore()
+    for device in devices:
+        pl.semaphore_signal(barrier, inc=1, device_id=device, device_id_type=MESH)
+    pl.semaphore_wait(barrier, len(devices))
+
+
+def remote(source, target, sems, index, device):
+    return pltpu.make_async_remote_copy(
+        src_ref=source,
+        dst_ref=target,
+        send_sem=sems[0].at[index],
+        recv_sem=sems[1].at[index],
+        device_id=device,
+        device_id_type=MESH,
+    )
+
+
+class RingGather:
+    def __init__(self, at, owns, slots, sems, base, local_sem):
+        half = owns[0].shape[0] // 2
+        ring, t = at["ring"], at["t"]
+        self.local = [
+            pltpu.make_async_copy(own, slot(at["d"], 0, 2 * half), local_sem.at[n])
+            for n, (own, slot) in enumerate(zip(owns, slots))
+        ]
+        self.sends, self.receives, self.s = [], [], 0
+        for s in range(7):
+            sends, receives = [], []
+            for way, sign in ((0, 1), (1, -1)):
+                to = (ring(sign), t)
+                for n, (own, slot) in enumerate(zip(owns, slots)):
+                    index = base + (2 * s + way) * len(owns) + n
+                    here = slot(ring(-sign * s), way * half, half)
+                    there = slot(ring(-sign * (s + 1)), way * half, half)
+                    source = own.at[pl.ds(way * half, half)] if s == 0 else here
+                    sends.append(remote(source, here, sems, index, to))
+                    receives.append(remote(there, there, sems, index, to))
+            self.sends.append(sends)
+            self.receives.append(receives)
+
+    def start(self):
+        for copy in self.sends[0] + self.local:
+            copy.start()
+
+    def step(self):
+        for k, copy in enumerate(self.receives[self.s]):
+            copy.wait_recv()
+            if self.s < 6:
+                self.sends[self.s + 1][k].start()
+        self.s += 1
+
+    def finish(self):
+        while self.s < 7:
+            self.step()
+        for copy in self.local:
+            copy.wait()
+
+    def drain(self):
+        for sends in self.sends:
+            for copy in sends:
+                copy.wait_send()
+
+
+class RingScatter:
+    def __init__(self, at, left, right, slots, term, out, sems, base):
+        self.ring, self.left, self.right = at["ring"], left, right
+        self.slots, self.term, self.out = slots, term, out
+        self.half, self.columns = slots.shape[2], slots.shape[3]
+        self.s = 0
+        self.sends = [
+            [
+                remote(
+                    slots.at[way, s], slots.at[way, s + 1], sems, base + 2 * s + way,
+                    (at["ring"](sign), at["t"]),
+                )
+                for way, sign in ((0, 1), (1, -1))
+            ]
+            for s in range(7)
+        ]
+
+    def compute(self, away):
+        half = self.half
+        first = pl.multiple_of(self.ring(-away) * 2 * half, half)
+        second = pl.multiple_of(self.ring(away) * 2 * half + half, half)
+        width = 512
+        whole = self.columns // width * width
+
+        def block(lanes):
+            left = jnp.concatenate(
+                [self.left[pl.ds(first, half)], self.left[pl.ds(second, half)]], axis=0
+            )
+            self.term[:, lanes] = nn_dot(left, self.right[:, lanes])
+
+        @pl.loop(0, whole // width)
+        def _(i):
+            block(pl.ds(pl.multiple_of(i * width, width), width))
+
+        if whole < self.columns:
+            block(pl.ds(whole, self.columns - whole))
+
+    def start(self):
+        self.compute(1)
+        for way in range(2):
+            rows = pl.ds(way * self.half, self.half)
+            self.slots[way, 0] = self.term[rows, pl.ds(0, self.columns)].astype(jnp.bfloat16)
+            self.sends[0][way].start()
+
+    def step(self):
+        s, half = self.s, self.half
+        self.compute(s + 2)
+        for way in range(2):
+            rows = pl.ds(way * half, half)
+            self.sends[s][way].wait_recv()
+            total = self.slots[way, s + 1].astype(jnp.float32) + self.term[rows, pl.ds(0, self.columns)]
+            if s < 6:
+                self.slots[way, s + 1] = total.astype(jnp.bfloat16)
+                self.sends[s + 1][way].start()
+            else:
+                self.out[rows] = total
+        self.s += 1
+
+    def finish(self):
+        while self.s < 7:
+            self.step()
+        for sends in self.sends:
+            for copy in sends:
+                copy.wait_send()
+
+
+class GatherTensor:
+    def __init__(self, at, full, rows, sems, base):
+        def block(index):
+            return full.at[pl.ds(pl.multiple_of(index * rows, rows), rows)]
+
+        mine, across = block(at["t"]), block(at["cross"])
+        self.to_core = remote(mine, mine, sems, base, (at["d"], at["core"]))
+        self.to_cross = remote(mine, mine, sems, base + 1, (at["d"], at["cross"]))
+        self.relay_core = remote(across, across, sems, base + 2, (at["d"], at["core"]))
+        places = (block(at["core"]), across, block(at["cross_core"]))
+        self.receives = [
+            remote(place, place, sems, base + k, (at["d"], at["core"]))
+            for k, place in enumerate(places)
+        ]
+
+    def start(self):
+        self.to_cross.start()
+        self.to_core.start()
+
+    def relay(self):
+        self.receives[1].wait_recv()
+        self.relay_core.start()
+
+    def drain(self):
+        for send in (self.to_core, self.to_cross, self.relay_core):
+            send.wait_send()
+
+    def finish(self):
+        self.receives[0].wait_recv()
+        self.receives[2].wait_recv()
+        self.drain()
+
+
+def sum_rows(at, block_part, send, receive, total, sems, base, idle=None):
+    to_core, to_cross = (at["d"], at["core"]), (at["d"], at["cross"])
+    low = jnp.bfloat16
+    first = remote(send.at[0], receive.at[0], sems, base, to_core)
+    second = remote(send.at[1], receive.at[1], sems, base + 1, to_cross)
+    third = remote(send.at[2], receive.at[2], sems, base + 2, to_core)
+    send[0] = block_part(at["cross_core"]).astype(low)
+    first.start()
+    total[...] = block_part(at["cross"])
+    first.wait_recv()
+    send[1] = (total[...] + receive[0].astype(jnp.float32)).astype(low)
+    second.start()
+    send[2] = block_part(at["core"]).astype(low)
+    third.start()
+    total[...] = block_part(at["t"])
+    if idle is not None:
+        idle()
+    third.wait_recv()
+    second.wait_recv()
+    total[...] += receive[2].astype(jnp.float32) + receive[1].astype(jnp.float32)
+    for copy in (first, second, third):
+        copy.wait_send()
+
+
+class SumAll:
+    def __init__(self, at, value, received, sems, base):
+        d, t = at["d"], at["t"]
+        partners = ((d, at["core"]), (d, at["cross"]), (at["mate"], t), (at["z_pair"], t), (at["z_mirror"], t))
+        self.value, self.received, self.s = value, received, 0
+        self.copies = [
+            remote(value.at[k], received.at[k], sems, base + k, partner)
+            for k, partner in enumerate(partners)
+        ]
+
+    def start(self):
+        self.copies[0].start()
+
+    def step(self):
+        s = self.s
+        self.copies[s].wait_recv()
+        self.value[s + 1] = self.value[s] + self.received[s]
+        if s < 4:
+            self.copies[s + 1].start()
+        self.s += 1
+
+    def finish(self):
+        while self.s < 5:
+            self.step()
+        for copy in self.copies:
+            copy.wait_send()
+
+
+def nt_dot(left, right):
+    return lax.dot_general(
+        left, right, (((1,), (1,)), ((), ())), preferred_element_type=jnp.float32
+    )
+
+
+def nn_dot(left, right):
+    return lax.dot_general(
+        left, right, (((1,), (0,)), ((), ())), preferred_element_type=jnp.float32
+    )
+
+
+def tn_dot(left, right):
+    return lax.dot_general(
+        left, right, (((0,), (0,)), ((), ())), preferred_element_type=jnp.float32
+    )
+
+
+def head_groups(width):
+    heads = width // HEAD_DIM
+    return [(2 * HEAD_DIM * j, min(2, heads - 2 * j)) for j in range((heads + 1) // 2)]
+
+
+def split_heads(tile, heads):
+    if heads == 1:
+        return tile
+    lane = lax.broadcasted_iota(jnp.int32, tile.shape, 1)
+    zero = jnp.zeros_like(tile)
+    return jnp.concatenate(
+        [jnp.where(lane < HEAD_DIM, tile, zero), jnp.where(lane < HEAD_DIM, zero, tile)], axis=0
+    )
+
+
+def join_heads(stacked, heads):
+    if heads == 1:
+        return stacked
+    half = stacked.shape[0] // 2
+    lane = lax.broadcasted_iota(jnp.int32, (half, stacked.shape[1]), 1)
+    return jnp.where(lane < HEAD_DIM, stacked[:half], stacked[half:])
+
+
+def convolve(window, taps, lanes, same_one, same_two):
+    one = pltpu.roll(window, 1, axis=0)[TILE:] * same_one
+    two = pltpu.roll(window, 2, axis=0)[TILE:] * same_two
+    rows = (window[TILE:], one, two)
+    return sum(taps[m : m + 1, lanes] * rows[m] for m in range(CONV)), rows
+
+
+def attend_tile(i, q, k_pad, v_pad, u, seg_q, seg_k, same, taps, p_out, o):
+    row = pl.multiple_of(i * TILE, TILE)
+    at_row, at_window = pl.ds(row, TILE), pl.ds(row, 2 * TILE)
+    distance = (
+        lax.broadcasted_iota(jnp.int32, (TILE, 2 * TILE), 0)
+        + TILE
+        - lax.broadcasted_iota(jnp.int32, (TILE, 2 * TILE), 1)
+    )
+    allowed = (seg_q[at_row] == seg_k[i]) & (distance >= 0) & (distance < WINDOW)
+    same_one, same_two = same[at_row, 0:1], same[at_row, 1:2]
+    for lane, heads in head_groups(q.shape[1]):
+        lanes = pl.ds(lane, heads * HEAD_DIM)
+        values = v_pad[at_window, lanes]
+        allow = jnp.concatenate([allowed] * heads, axis=0) if heads > 1 else allowed
+        scores = nt_dot(split_heads(q[at_row, lanes], heads), k_pad[at_window, lanes])
+        scores = jnp.where(allow, scores * (HEAD_DIM**-0.5), -1e30)
+        exponent = jnp.exp(scores - jnp.max(scores, axis=1, keepdims=True))
+        chance = exponent * (1.0 / jnp.sum(exponent, axis=1, keepdims=True))
+        chance = chance.astype(jnp.bfloat16)
+        p_out[i, pl.ds((lane // HEAD_DIM) * TILE, heads * TILE), :] = chance
+        mixed = join_heads(nn_dot(chance, values), heads)
+        convolved, _ = convolve(values.astype(jnp.float32), taps, lanes, same_one, same_two)
+        o[at_row, lanes] = (mixed + convolved * u[at_row, lanes].astype(jnp.float32)).astype(
+            jnp.bfloat16
+        )
+
+
+def attend_back_tile(
+    i, q, k_pad, v_pad, u, p, same, taps, do, dq, du, dk, dv, conv_sum
+):
+    row = pl.multiple_of(i * TILE, TILE)
+    at_row, at_window = pl.ds(row, TILE), pl.ds(row, 2 * TILE)
+    same_one, same_two = same[at_row, 0:1], same[at_row, 1:2]
+    for lane, heads in head_groups(q.shape[1]):
+        lanes = pl.ds(lane, heads * HEAD_DIM)
+        keys, values = k_pad[at_window, lanes], v_pad[at_window, lanes]
+        grad = do[at_row, lanes]
+        grad_heads = split_heads(grad, heads)
+        chance_low = p[i, pl.ds((lane // HEAD_DIM) * TILE, heads * TILE), :]
+        chance = chance_low.astype(jnp.float32)
+        weighted = chance * nt_dot(grad_heads, values)
+        slope = weighted - chance * jnp.sum(weighted, axis=1, keepdims=True)
+        slope = (slope * (HEAD_DIM**-0.5)).astype(jnp.bfloat16)
+        dq[at_row, lanes] = join_heads(nn_dot(slope, keys), heads).astype(jnp.bfloat16)
+        dk[at_window, lanes] += tn_dot(slope, split_heads(q[at_row, lanes], heads))
+        convolved, rows = convolve(values.astype(jnp.float32), taps, lanes, same_one, same_two)
+        grad = grad.astype(jnp.float32)
+        du[at_row, lanes] = (grad * convolved).astype(jnp.bfloat16)
+        grad_conv = grad * u[at_row, lanes].astype(jnp.float32)
+        back = tn_dot(chance_low, grad_heads)
+        zero = jnp.zeros_like(grad_conv)
+        for m, same_m in enumerate((None, same_one, same_two)):
+            conv_sum[m : m + 1, lanes] += jnp.sum(grad_conv * rows[m], axis=0, keepdims=True)
+            term = taps[m : m + 1, lanes] * grad_conv
+            term = term if m == 0 else term * same_m
+            term = jnp.concatenate([zero, term], axis=0)
+            back = back + (term if m == 0 else pltpu.roll(term, 2 * TILE - m, axis=0))
+        dv[at_window, lanes] += back
+
+
+def norm_rows(values, gain):
+    scale = lax.rsqrt(jnp.mean(values * values, axis=1, keepdims=True) + EPS)
+    return (values * scale * gain).astype(jnp.bfloat16)
+
+
+def norm_back(values, grad, gain):
+    scale = lax.rsqrt(jnp.mean(values * values, axis=1, keepdims=True) + EPS)
+    normed = values * scale
+    scaled = grad * gain
+    through = scale * (scaled - normed * jnp.mean(scaled * normed, axis=1, keepdims=True))
+    return through, jnp.sum(grad * normed, axis=0, keepdims=True)
+
+
+def chunks_of(rows, size=64):
+    def run(body):
+        @pl.loop(0, rows // size)
+        def _(i):
+            body(pl.multiple_of(i * size, size), size)
+
+    return run
+
+
+def mixer_forward_kernel(
+    x, valid, gain_one, gain_two, seg_q, seg_k, same, taps, mix_own, out_own, feed_own,
+    mix_out, last_out, feed, h1t_out, q_out, k_out, v_out, u_out, p_out, o_out, x1_out, h2_out, count_out,
+    mix, last, h1, h1t, h2, q, k_pad, v_pad, u, p, o, send, receive, total, count, count_in,
+    send_sems, recv_sems, local_sems, out_sems,
+):
+    at = neighbours()
+    sems = (send_sems, recv_sems)
+    rows, shard = x.shape[0], mix_own.shape[0]
+    greet(at, everyone=True)
+
+    def slot_of(full):
+        return lambda i, first, size: full.at[pl.ds(pl.multiple_of(i * shard + first, 16), size)]
+
+    early = RingGather(
+        at, [mix_own, out_own], [slot_of(mix), slot_of(last)], sems, 0, local_sems.at[pl.ds(0, 2)]
+    )
+    late = RingGather(at, [feed_own], [slot_of(feed)], sems, 28, local_sems.at[pl.ds(2, 1)])
+    group_one = GatherTensor(at, h1, rows, sems, 42)
+    group_two = GatherTensor(at, h2, rows, sems, 45)
+    counting = SumAll(at, count, count_in, sems, 51)
+    local = q.shape[1]
+    main = local // LANES * LANES
+    tail = local - main
+    keeps = []
+
+    def keep(source, target):
+        copy = pltpu.make_async_copy(source, target, out_sems.at[len(keeps)])
+        copy.start()
+        keeps.append(copy)
+
+    early.start()
+
+    @chunks_of(rows)
+    def _(row, size):
+        h1[pl.ds(pl.multiple_of(at["t"] * rows + row, size), size)] = norm_rows(
+            x[pl.ds(row, size)].astype(jnp.float32), gain_one[...]
+        )
+
+    group_one.start()
+    count[0] = jnp.full(count.shape[1:], jnp.sum(valid[...]), jnp.float32)
+    counting.start()
+    k_pad[pl.ds(0, TILE)] = jnp.zeros((TILE, local), k_pad.dtype)
+    v_pad[pl.ds(0, TILE)] = jnp.zeros((TILE, local), v_pad.dtype)
+    early.step()
+    counting.step()
+    early.step()
+    counting.step()
+    group_one.relay()
+    early.step()
+    counting.step()
+    early.step()
+    counting.step()
+    group_one.finish()
+    early.step()
+
+    @pl.loop(0, 4)
+    def _(j):
+        here = pl.multiple_of(j * rows, rows)
+        h1t[:, pl.ds(here, rows)] = h1[pl.ds(here, rows)].T
+
+    keep(h1t, h1t_out)
+    counting.finish()
+    keep(count.at[5], count_out)
+    early.step()
+    late.start()
+    early.finish()
+    keep(mix, mix_out)
+    keep(last, last_out)
+
+    def project(j):
+        here = pl.ds(pl.multiple_of(j * rows, rows), rows)
+        there = pl.ds(pl.multiple_of(j * rows + TILE, TILE), rows)
+        left = h1[here]
+        low = jnp.bfloat16
+        pair = nn_dot(left, mix[:, pl.ds(0, 2 * main)]).astype(low)
+        q[here, pl.ds(0, main)] = pair[:, :main]
+        k_pad[there, pl.ds(0, main)] = pair[:, main:]
+        pair = nn_dot(left, mix[:, pl.ds(2 * main, 2 * main)]).astype(low)
+        v_pad[there, pl.ds(0, main)] = pair[:, :main]
+        u[here, pl.ds(0, main)] = pair[:, main:]
+        ends = nn_dot(left, mix[:, pl.ds(4 * main, 4 * tail)])
+        q[here, pl.ds(main, tail)] = ends[:, :tail].astype(low)
+        k_pad[there, pl.ds(main, tail)] = ends[:, tail : 2 * tail].astype(low)
+        v_pad[there, pl.ds(main, tail)] = ends[:, 2 * tail : 3 * tail].astype(low)
+        u[here, pl.ds(main, tail)] = ends[:, 3 * tail :].astype(low)
+
+    @pl.loop(0, h1.shape[0] // rows)
+    def _(j):
+        project(j)
+
+    for source, target in ((q, q_out), (k_pad, k_out), (v_pad, v_out), (u, u_out)):
+        keep(source, target)
+    late.step()
+    tiles = q.shape[0] // TILE
+
+    def attend(first, last_tile):
+        @pl.loop(first, last_tile)
+        def _(i):
+            attend_tile(i, q, k_pad, v_pad, u, seg_q, seg_k, same, taps, p, o)
+
+    attend(0, tiles // 2)
+    late.step()
+    attend(tiles // 2, tiles)
+    keep(p, p_out)
+    keep(o, o_out)
+
+    def part(block):
+        return nt_dot(o[pl.ds(pl.multiple_of(block * rows, rows), rows)], last[...])
+
+    def idle():
+        late.step()
+
+    sum_rows(at, part, send, receive, total, sems, 48, idle=idle)
+
+    @chunks_of(rows)
+    def _(row, size):
+        here = pl.ds(row, size)
+        hidden = total[here] + x[here].astype(jnp.float32)
+        total[here] = hidden
+        h2[pl.ds(pl.multiple_of(at["t"] * rows + row, size), size)] = norm_rows(hidden, gain_two[...])
+
+    group_two.start()
+    keep(total, x1_out)
+    late.step()
+    late.step()
+    group_two.relay()
+    group_two.finish()
+    keep(h2, h2_out)
+    late.finish()
+    early.drain()
+    late.drain()
+    for copy in keeps:
+        copy.wait()
+
+
+def specs():
+    return pl.BlockSpec(memory_space=pltpu.VMEM), pl.BlockSpec(memory_space=pl.ANY)
+
+
+def shape(*dims, kind=jnp.bfloat16):
+    return jax.ShapeDtypeStruct(dims, kind)
+
+
+def params(identity):
+    return pltpu.CompilerParams(
+        collective_id=identity, has_side_effects=True, vmem_limit_bytes=VMEM_LIMIT
+    )
+
+
+def dma(count):
+    return pltpu.SemaphoreType.DMA((count,))
+
+
+def mixer_forward(x, valid, gain_one, gain_two, seg_q, seg_k, same, taps, mix_own, out_own, feed_own):
+    rows, width = x.shape
+    shard, local = out_own.shape
+    everyone, depth = 4 * rows, 8 * shard
+    low, wide = jnp.bfloat16, jnp.float32
+    tiles, heads = everyone // TILE, local // HEAD_DIM
+    vmem, hbm = specs()
+    return pl.pallas_call(
+        mixer_forward_kernel,
+        out_shape=(
+            shape(depth, mix_own.shape[1]),
+            shape(depth, local),
+            shape(depth, feed_own.shape[1]),
+            shape(width, everyone),
+            shape(everyone, local),
+            shape(everyone + TILE, local),
+            shape(everyone + TILE, local),
+            shape(everyone, local),
+            shape(tiles, heads * TILE, 2 * TILE),
+            shape(everyone, local),
+            shape(rows, width, kind=wide),
+            shape(everyone, width),
+            shape(8, LANES, kind=wide),
+        ),
+        in_specs=[vmem] * 8 + [hbm] * 3,
+        out_specs=(hbm,) * 13,
+        scratch_shapes=[
+            pltpu.VMEM((depth, mix_own.shape[1]), low),
+            pltpu.VMEM((depth, local), low),
+            pltpu.VMEM((everyone, width), low),
+            pltpu.VMEM((width, everyone), low),
+            pltpu.VMEM((everyone, width), low),
+            pltpu.VMEM((everyone, local), low),
+            pltpu.VMEM((everyone + TILE, local), low),
+            pltpu.VMEM((everyone + TILE, local), low),
+            pltpu.VMEM((everyone, local), low),
+            pltpu.VMEM((tiles, heads * TILE, 2 * TILE), low),
+            pltpu.VMEM((everyone, local), low),
+            pltpu.VMEM((3, rows, width), low),
+            pltpu.VMEM((3, rows, width), low),
+            pltpu.VMEM((rows, width), wide),
+            pltpu.VMEM((6, 8, LANES), wide),
+            pltpu.VMEM((5, 8, LANES), wide),
+            dma(56),
+            dma(56),
+            dma(3),
+            dma(12),
+        ],
+        compiler_params=params(1),
+    )(x, valid, gain_one, gain_two, seg_q, seg_k, same, taps, mix_own, out_own, feed_own)
+
+
+def feed_lanes(hidden):
+    main = hidden // LANES * LANES
+    cut = main // 2 // LANES * LANES
+    parts = [(0, cut), (cut, main - cut)]
+    return [(pl.ds(a, n), pl.ds(a, n), pl.ds(main + a, n)) for a, n in parts], main
+
+
+def gated(gate, up):
+    sigmoid = jax.nn.sigmoid(gate)
+    silu = gate * sigmoid
+    return silu * up, up * sigmoid * (1.0 + gate * (1.0 - sigmoid)), silu
+
+
+def feed_forward_kernel(
+    valid, count, h2_in, feed_in, x1_in, cotangent_in, teacher_in, down_own,
+    down_out, slopes_out, active_out, act_out, dy_out, dyb_out, dybt_out, h2t_out, squares_out,
+    h2, feed, down, slopes, active, x1, cotangent, teacher, dyb, turned, send, receive, total,
+    send_sems, recv_sems, local_sems, load_sems, out_sems,
+):
+    at = neighbours()
+    sems = (send_sems, recv_sems)
+    rows, shard = x1.shape[0], down_own.shape[0]
+    low = jnp.bfloat16
+    greet(at)
+    ring = RingGather(
+        at, [down_own],
+        [lambda i, first, size: down.at[pl.ds(pl.multiple_of(i * shard + first, 16), size)]],
+        sems, 0, local_sems,
+    )
+    group = GatherTensor(at, dyb, rows, sems, 17)
+    loads = [
+        pltpu.make_async_copy(source, target, load_sems.at[n])
+        for n, (source, target) in enumerate(
+            ((h2_in, h2), (feed_in, feed), (x1_in, x1), (cotangent_in, cotangent), (teacher_in, teacher))
+        )
+    ]
+    keeps = []
+
+    def keep(source, target):
+        copy = pltpu.make_async_copy(source, target, out_sems.at[len(keeps)])
+        copy.start()
+        keeps.append(copy)
+
+    ring.start()
+    for load in loads:
+        load.start()
+    hidden = active.shape[1]
+    parts, main = feed_lanes(hidden)
+    tail = hidden - main
+    loads[0].wait()
+    loads[1].wait()
+
+    def widen(first, last):
+        @pl.loop(first, last)
+        def _(j):
+            here = pl.ds(pl.multiple_of(j * rows, rows), rows)
+            left = h2[here]
+            for own, gate_lanes, up_lanes in parts:
+                a, by_gate, by_up = gated(nn_dot(left, feed[:, gate_lanes]), nn_dot(left, feed[:, up_lanes]))
+                active[here, own] = a.astype(low)
+                slopes[here, gate_lanes] = by_gate.astype(low)
+                slopes[here, up_lanes] = by_up.astype(low)
+            both = nn_dot(left, feed[:, pl.ds(2 * main, 2 * tail)])
+            a, by_gate, by_up = gated(both[:, :tail], both[:, tail:])
+            active[here, pl.ds(main, tail)] = a.astype(low)
+            slopes[here, pl.ds(2 * main, 2 * tail)] = jnp.concatenate([by_gate, by_up], axis=1).astype(low)
+
+    ring.step()
+    widen(0, 2)
+    ring.step()
+    widen(2, 4)
+    keep(active, active_out)
+    keep(slopes, slopes_out)
+    ring.step()
+
+    def turn(source, block):
+        here = pl.multiple_of(block * rows, rows)
+        turned[:, pl.ds(here, rows)] = source[pl.ds(here, rows)].T
+
+    @pl.loop(0, 4)
+    def _(j):
+        turn(h2, j)
+
+    keep(turned, h2t_out)
+    ring.finish()
+    keep(down, down_out)
+    for load in loads[2:]:
+        load.wait()
+
+    def part(block):
+        return nt_dot(active[pl.ds(pl.multiple_of(block * rows, rows), rows)], down[...])
+
+    sum_rows(at, part, send, receive, total, sems, 14)
+    weight = (rows * 4 * 8) / count[0:1, 0:1]
+    squares_out[...] = jnp.zeros_like(squares_out)
+
+    @chunks_of(rows, 32)
+    def _(row, size):
+        here = pl.ds(row, size)
+        result = total[here] + x1[here]
+        deviation = result - teacher[here].astype(jnp.float32)
+        kept = valid[here, 0:1] * deviation
+        total[here] = result
+        squares_out[0:1] += jnp.sum(kept * deviation, axis=0, keepdims=True)
+        grad = cotangent[here] + kept * weight
+        x1[here] = grad
+        dyb[pl.ds(pl.multiple_of(at["t"] * rows + row, size), size)] = grad.astype(low)
+
+    group.start()
+    keep(total, act_out)
+    keep(x1, dy_out)
+    keeps[2].wait()
+    turn(dyb, at["t"])
+    group.receives[0].wait_recv()
+    turn(dyb, at["core"])
+    group.relay()
+    turn(dyb, at["cross"])
+    group.receives[2].wait_recv()
+    turn(dyb, at["cross_core"])
+    group.drain()
+    keep(dyb, dyb_out)
+    keep(turned, dybt_out)
+    ring.drain()
+    for n, copy in enumerate(keeps):
+        if n != 2:
+            copy.wait()
+
+
+def feed_forward(valid, count, h2, feed, x1, cotangent, teacher, down_own):
+    rows, width = x1.shape
+    shard, hidden = down_own.shape
+    everyone, depth = 4 * rows, 8 * shard
+    low, wide = jnp.bfloat16, jnp.float32
+    vmem, hbm = specs()
+    return pl.pallas_call(
+        feed_forward_kernel,
+        out_shape=(
+            shape(depth, hidden),
+            shape(everyone, 2 * hidden),
+            shape(everyone, hidden),
+            shape(rows, width, kind=wide),
+            shape(rows, width, kind=wide),
+            shape(everyone, width),
+            shape(width, everyone),
+            shape(width, everyone),
+            shape(8, width, kind=wide),
+        ),
+        in_specs=[vmem] * 2 + [hbm] * 6,
+        out_specs=(hbm,) * 8 + (vmem,),
+        scratch_shapes=[
+            pltpu.VMEM((everyone, width), low),
+            pltpu.VMEM((depth, 2 * hidden), low),
+            pltpu.VMEM((depth, hidden), low),
+            pltpu.VMEM((everyone, 2 * hidden), low),
+            pltpu.VMEM((everyone, hidden), low),
+            pltpu.VMEM((rows, width), wide),
+            pltpu.VMEM((rows, width), wide),
+            pltpu.VMEM((rows, width), low),
+            pltpu.VMEM((everyone, width), low),
+            pltpu.VMEM((width, everyone), low),
+            pltpu.VMEM((3, rows, width), low),
+            pltpu.VMEM((3, rows, width), low),
+            pltpu.VMEM((rows, width), wide),
+            dma(20),
+            dma(20),
+            dma(1),
+            dma(5),
+            dma(8),
+        ],
+        compiler_params=params(2),
+    )(valid, count, h2, feed, x1, cotangent, teacher, down_own)
+
+
+def feed_backward_kernel(
+    gain, dyb_in, dybt_in, h2t_in, down_in, feed_in, active_in, slopes_in, x1_in, dy_in,
+    down_grad, feed_grad, gain_part, dx1_out, dx1b_out, dx1t_out,
+    dyb, dybt, h2t, down, feed, active, slopes, side, total, down_slots, feed_slots, term, send, receive,
+    send_sems, recv_sems, load_sems, out_sems,
+):
+    at = neighbours()
+    sems = (send_sems, recv_sems)
+    rows = total.shape[0]
+    low = jnp.bfloat16
+    loads = [
+        pltpu.make_async_copy(source, target, load_sems.at[n])
+        for n, (source, target) in enumerate(
+            (
+                (dybt_in, dybt), (active_in, active), (dyb_in, dyb), (down_in, down), (slopes_in, slopes),
+                (feed_in, feed), (h2t_in, h2t), (x1_in, side), (dy_in, side),
+            )
+        )
+    ]
+    for load in loads[:-1]:
+        load.start()
+    greet(at)
+    first = RingScatter(
+        at, dybt, active, down_slots, term, down_grad, sems, 0
+    )
+    second = RingScatter(at, h2t, slopes, feed_slots, term, feed_grad, sems, 14)
+    group = GatherTensor(at, dyb, rows, sems, 31)
+    hidden = active.shape[1]
+    parts, main = feed_lanes(hidden)
+    tail = hidden - main
+    loads[0].wait()
+    loads[1].wait()
+    first.start()
+    for load in loads[2:5]:
+        load.wait()
+
+    def slope_back(first_block, last_block):
+        @pl.loop(first_block, last_block)
+        def _(j):
+            here = pl.ds(pl.multiple_of(j * rows, rows), rows)
+            left = dyb[here]
+            for own, gate_lanes, up_lanes in parts:
+                da = nn_dot(left, down[:, own])
+                slopes[here, gate_lanes] = (da * slopes[here, gate_lanes].astype(jnp.float32)).astype(low)
+                slopes[here, up_lanes] = (da * slopes[here, up_lanes].astype(jnp.float32)).astype(low)
+            da = nn_dot(left, down[:, pl.ds(main, tail)])
+            ends = pl.ds(2 * main, 2 * tail)
+            both = jnp.concatenate([da, da], axis=1) * slopes[here, ends].astype(jnp.float32)
+            slopes[here, ends] = both.astype(low)
+
+    slope_back(0, 2)
+    first.step()
+    slope_back(2, 4)
+    first.step()
+    loads[6].wait()
+    second.start()
+    loads[5].wait()
+    loads[7].wait()
+
+    def part(block):
+        return nt_dot(slopes[pl.ds(pl.multiple_of(block * rows, rows), rows)], feed[...])
+
+    def idle():
+        first.step()
+        first.step()
+        second.step()
+
+    sum_rows(at, part, send, receive, total, sems, 28, idle=idle)
+    gain_part[...] = jnp.zeros_like(gain_part)
+
+    @chunks_of(rows, 32)
+    def _(row, size):
+        here = pl.ds(row, size)
+        through, term_gain = norm_back(side[here], total[here], gain[...])
+        gain_part[0:1] += term_gain
+        total[here] = through
+
+    loads[8].start()
+    loads[8].wait()
+
+    @chunks_of(rows, 32)
+    def _(row, size):
+        here = pl.ds(row, size)
+        grad = total[here] + side[here]
+        total[here] = grad
+        dyb[pl.ds(pl.multiple_of(at["t"] * rows + row, size), size)] = grad.astype(low)
+
+    group.start()
+    keeps = [pltpu.make_async_copy(total, dx1_out, out_sems.at[0])]
+    keeps[0].start()
+    first.step()
+    second.step()
+    first.step()
+    second.step()
+    group.relay()
+    first.finish()
+    second.step()
+    group.finish()
+
+    @pl.loop(0, 4)
+    def _(j):
+        here = pl.multiple_of(j * rows, rows)
+        dybt[:, pl.ds(here, rows)] = dyb[pl.ds(here, rows)].T
+
+    for source, target in ((dyb, dx1b_out), (dybt, dx1t_out)):
+        keeps.append(pltpu.make_async_copy(source, target, out_sems.at[len(keeps)]))
+        keeps[-1].start()
+    second.finish()
+    for copy in keeps:
+        copy.wait()
+
+
+def feed_backward(gain, dyb, dybt, h2t, down, feed, active, slopes, x1, dy):
+    rows, width = x1.shape
+    depth, hidden = down.shape
+    everyone, shard = 4 * rows, depth // 8
+    low, wide = jnp.bfloat16, jnp.float32
+    vmem, hbm = specs()
+    return pl.pallas_call(
+        feed_backward_kernel,
+        out_shape=(
+            shape(shard, hidden, kind=wide),
+            shape(shard, 2 * hidden, kind=wide),
+            shape(8, width, kind=wide),
+            shape(rows, width, kind=wide),
+            shape(everyone, width),
+            shape(width, everyone),
+        ),
+        in_specs=[vmem] + [hbm] * 9,
+        out_specs=(vmem,) * 3 + (hbm,) * 3,
+        scratch_shapes=[
+            pltpu.VMEM((everyone, width), low),
+            pltpu.VMEM((width, everyone), low),
+            pltpu.VMEM((width, everyone), low),
+            pltpu.VMEM((depth, hidden), low),
+            pltpu.VMEM((depth, 2 * hidden), low),
+            pltpu.VMEM((everyone, hidden), low),
+            pltpu.VMEM((everyone, 2 * hidden), low),
+            pltpu.VMEM((rows, width), wide),
+            pltpu.VMEM((rows, width), wide),
+            pltpu.VMEM((2, 8, shard // 2, hidden), low),
+            pltpu.VMEM((2, 8, shard // 2, 2 * hidden), low),
+            pltpu.VMEM((shard, 2 * hidden), wide),
+            pltpu.VMEM((3, rows, width), low),
+            pltpu.VMEM((3, rows, width), low),
+            dma(34),
+            dma(34),
+            dma(9),
+            dma(3),
+        ],
+        compiler_params=params(3),
+    )(gain, dyb, dybt, h2t, down, feed, active, slopes, x1, dy)
+
+
+def mixer_backward_kernel(
+    x, gain, same, taps, gain_part, squares,
+    dx1b_in, dx1t_in, o_in, last_in, q_in, k_in, v_in, u_in, p_in, h1t_in, mix_in, dx1_in,
+    out_grad, mix_grad, input_grad, small_out, conv_out,
+    dx1b, dx1t, o, last, q, k_pad, v_pad, u, p, h1t, mix,
+    do, dq, du, dk, dv, grads, out_slots, mix_slots, term, send, receive, total,
+    small, small_in, conv, conv_in,
+    send_sems, recv_sems, load_sems,
+):
+    at = neighbours()
+    sems = (send_sems, recv_sems)
+    rows = total.shape[0]
+    low = jnp.bfloat16
+    loads = [
+        pltpu.make_async_copy(source, target, load_sems.at[n])
+        for n, (source, target) in enumerate(
+            (
+                (dx1t_in, dx1t), (o_in, o), (dx1b_in, dx1b), (last_in, last), (q_in, q), (k_in, k_pad),
+                (v_in, v_pad), (u_in, u), (p_in, p), (h1t_in, h1t), (mix_in, mix), (dx1_in, input_grad),
+            )
+        )
+    ]
+    for load in loads:
+        load.start()
+    greet(at, everyone=True)
+    local = q.shape[1]
+    main = local // LANES * LANES
+    tail = local - main
+    first = RingScatter(at, dx1t, o, out_slots, term, out_grad, sems, 0)
+    second = RingScatter(at, h1t, grads, mix_slots, term, mix_grad, sems, 14)
+    small_sum = SumAll(at, small, small_in, sems, 31)
+    conv_all = SumAll(at, conv, conv_in, sems, 36)
+    loads[0].wait()
+    loads[1].wait()
+    first.start()
+    loads[2].wait()
+    loads[3].wait()
+    dk[...] = jnp.zeros_like(dk)
+    dv[...] = jnp.zeros_like(dv)
+    conv[0] = jnp.zeros(conv.shape[1:], jnp.float32)
+
+    @pl.loop(0, 4)
+    def _(j):
+        here = pl.ds(pl.multiple_of(j * rows, rows), rows)
+        do[here] = nn_dot(dx1b[here], last[...]).astype(low)
+
+    first.step()
+    for load in loads[4:9]:
+        load.wait()
+    tiles = q.shape[0] // TILE
+    conv_sum = conv.at[0, at["t"]]
+
+    def attend(a, b):
+        @pl.loop(a, b)
+        def _(i):
+            attend_back_tile(i, q, k_pad, v_pad, u, p, same, taps, do, dq, du, dk, dv, conv_sum)
+
+    for k in range(4):
+        attend(k * tiles // 4, (k + 1) * tiles // 4)
+        first.step()
+    conv_all.start()
+
+    @chunks_of(q.shape[0])
+    def _(row, size):
+        here, there = pl.ds(row, size), pl.ds(pl.multiple_of(row + TILE, TILE), size)
+        four = [dq[here].astype(jnp.float32), dk[there], dv[there], du[here].astype(jnp.float32)]
+        for n, value in enumerate(four):
+            grads[here, pl.ds(n * main, main)] = value[:, :main].astype(low)
+        ends = jnp.concatenate([value[:, main:] for value in four], axis=1)
+        grads[here, pl.ds(4 * main, 4 * tail)] = ends.astype(low)
+
+    loads[9].wait()
+    second.start()
+    first.finish()
+    loads[10].wait()
+    loads[11].wait()
+
+    def part(block):
+        return nt_dot(grads[pl.ds(pl.multiple_of(block * rows, rows), rows)], mix[...])
+
+    def idle():
+        second.step()
+        conv_all.step()
+        second.step()
+        conv_all.step()
+
+    sum_rows(at, part, send, receive, total, sems, 28, idle=idle)
+    small[0, 0:1] = jnp.zeros((1, small.shape[2]), jnp.float32)
+    small[0, 1:2] = gain_part[0:1]
+    small[0, 2:3] = squares[0:1]
+    small[0, 3:8] = jnp.zeros((5, small.shape[2]), jnp.float32)
+
+    @chunks_of(rows, 32)
+    def _(row, size):
+        here = pl.ds(row, size)
+        through, term_gain = norm_back(x[here].astype(jnp.float32), total[here], gain[...])
+        small[0, 0:1] += term_gain
+        input_grad[here] += through
+
+    small_sum.start()
+    while second.s < 6:
+        second.step()
+        if conv_all.s < 5:
+            conv_all.step()
+        small_sum.step()
+    small_sum.finish()
+    conv_all.finish()
+    second.finish()
+    small_out[...] = small[5]
+    conv_out[...] = conv[5]
+
+
+def mixer_backward(
+    x, gain, same, taps, gain_part, squares, dx1b, dx1t, o, last, q, k_pad, v_pad, u, p, h1t, mix, dx1
+):
+    rows, width = x.shape
+    depth, local = last.shape
+    everyone, shard = 4 * rows, depth // 8
+    low, wide = jnp.bfloat16, jnp.float32
+    vmem, hbm = specs()
+    arrays = (dx1b, dx1t, o, last, q, k_pad, v_pad, u, p, h1t, mix)
+    return pl.pallas_call(
+        mixer_backward_kernel,
+        out_shape=(
+            shape(shard, local, kind=wide),
+            shape(shard, 4 * local, kind=wide),
+            shape(rows, width, kind=wide),
+            shape(8, width, kind=wide),
+            shape(4, 8, local, kind=wide),
+        ),
+        in_specs=[vmem] * 6 + [hbm] * 12,
+        out_specs=(vmem,) * 5,
+        scratch_shapes=[pltpu.VMEM(array.shape, array.dtype) for array in arrays]
+        + [
+            pltpu.VMEM((everyone, local), low),
+            pltpu.VMEM((everyone, local), low),
+            pltpu.VMEM((everyone, local), low),
+            pltpu.VMEM((everyone + TILE, local), wide),
+            pltpu.VMEM((everyone + TILE, local), wide),
+            pltpu.VMEM((everyone, 4 * local), low),
+            pltpu.VMEM((2, 8, shard // 2, local), low),
+            pltpu.VMEM((2, 8, shard // 2, 4 * local), low),
+            pltpu.VMEM((shard, 4 * local), wide),
+            pltpu.VMEM((3, rows, width), low),
+            pltpu.VMEM((3, rows, width), low),
+            pltpu.VMEM((rows, width), wide),
+            pltpu.VMEM((6, 8, width), wide),
+            pltpu.VMEM((5, 8, width), wide),
+            pltpu.VMEM((6, 4, 8, local), wide),
+            pltpu.VMEM((5, 4, 8, local), wide),
+            dma(41),
+            dma(41),
+            dma(12),
+        ],
+        compiler_params=params(4),
+    )(x, gain, same, taps, gain_part, squares, *arrays, dx1)
+
+
+def segment_tables(segments):
+    padded = jnp.concatenate([jnp.full((TILE,), -1, jnp.int32), segments])
+    seg_k = jnp.concatenate(
+        [padded[:-TILE].reshape(-1, 1, TILE), padded[TILE:].reshape(-1, 1, TILE)], axis=2
+    )
+    same = [
+        jnp.concatenate(
+            [jnp.zeros((m,), jnp.float32), (segments[m:] == segments[:-m]).astype(jnp.float32)]
+        )
+        for m in range(1, CONV)
+    ]
+    return segments[:, None], seg_k, jnp.stack(same, axis=1)
+
+
+def pack(*weights):
+    main = weights[0].shape[1] // LANES * LANES
+    return jnp.concatenate([w[:, :main] for w in weights] + [w[:, main:] for w in weights], axis=1)
+
+
+def unpack(packed, count):
+    width = packed.shape[1] // count
+    main = width // LANES * LANES
+    tail = width - main
+    return [
+        jnp.concatenate(
+            [
+                packed[:, n * main : (n + 1) * main],
+                packed[:, count * main + n * tail : count * main + (n + 1) * tail],
+            ],
+            axis=1,
+        )
+        for n in range(count)
+    ]
+
+
+def on_rings(
+    block_input,
+    cotangent,
+    teacher,
+    segments,
+    valid_mask,
+    query_weight,
+    key_weight,
+    value_weight,
+    mixgate_weight,
+    output_weight,
+    conv_weight,
+    gain_mixer,
+    gain_feed,
+    gate_weight,
+    up_weight,
+    down_weight,
+):
+    local = query_weight.shape[1]
+    taps = lax.dynamic_slice_in_dim(conv_weight, lax.axis_index("tensor") * local, local, 1)
+    seg_q, seg_k, same = segment_tables(segments)
+    valid = valid_mask.astype(jnp.float32)
+    mix_own = pack(query_weight, key_weight, value_weight, mixgate_weight)
+    feed_own = pack(gate_weight, up_weight)
+    gain_one, gain_two = gain_mixer[None], gain_feed[None]
+    mix, last, feed, h1t, q, k_pad, v_pad, u, p, o, x1, h2, count = mixer_forward(
+        block_input, valid.reshape(-1, LANES), gain_one, gain_two, seg_q, seg_k, same, taps,
+        mix_own, output_weight.T, feed_own,
+    )
+    down, slopes, active, outputs, dy, dyb, dybt, h2t, squares = feed_forward(
+        valid[:, None], count, h2, feed, x1, cotangent, teacher, down_weight.T
+    )
+    down_grad, feed_grad, gain_part, dx1, dx1b, dx1t = feed_backward(
+        gain_two, dyb, dybt, h2t, down, feed, active, slopes, x1, dy
+    )
+    out_grad, mix_grad, input_grad, small, conv = mixer_backward(
+        block_input, gain_one, same, taps, gain_part, squares, dx1b, dx1t, o, last, q, k_pad, v_pad,
+        u, p, h1t, mix, dx1,
+    )
+    gate_grad, up_grad = unpack(feed_grad, 2)
+    mean_loss = jnp.sum(small[2]) / (count[0, 0] * D)
+    return (
+        mean_loss,
+        outputs,
+        input_grad,
+        *unpack(mix_grad, 4),
+        out_grad.T,
+        conv[:, :CONV].transpose(1, 0, 2).reshape(CONV, -1),
+        small[0],
+        small[1],
+        gate_grad,
+        up_grad,
+        down_grad.T,
+    )
+
+
+def on_any_mesh(
     block_input,
     cotangent,
     teacher,
@@ -471,8 +1632,9 @@
 
 
 def solution(mesh):
+    rings = mesh.shape["dp"] == 8 and mesh.shape["tensor"] == 4
     return jax.shard_map(
-        on_device,
+        on_rings if rings else on_any_mesh,
         mesh=mesh,
         in_specs=(
             P(("dp", "tensor"), None),

time: 1290 us -> 604 us (0.47)
  Pallas kernels: 0 us -> 560 us
  waiting for transfers between devices: 517 us -> 0 us
  local copies, waits for them, and re-layouts: 308 us -> 22.7 us
  matrix products: 202 us -> 0 us
  starting transfers between devices: 186 us -> 0 us
  other arithmetic: 58.6 us -> 9.77 us
    pallas_call x0 -> x4, Pallas kernels: none -> 560 us  [the longest x1 190 us: mixer_forward(): pl.pallas_call(mixer_forward_kernel, out_shape=(shape(depth, mix_own.shap...]
    ppermute x111 -> x0, waiting for transfers between devices: 517 us -> none  [the longest x3 93.3 us: gather_dp(): mate_above = lax.ppermute(mate, 'dp', down)]
    dot_general x38 -> x0, matrix products: 202 us -> none  [the longest x8 67.6 us: cols_inner(): lax.dot_general(matrix_left, matrix_right, (((1,), (1,)), ((), ())), pref...]
    ppermute x111 -> x0, starting transfers between devices: 186 us -> none  [the longest x8 33.9 us: scatter_dp(): own_from_above = lax.ppermute(pick(parts, below), 'dp', down)]
    dynamic_update_slice x46 -> x0, local copies, waits for them, and re-layouts: 106 us -> none  [the longest x35 43.8 us: put(): return lax.dynamic_update_slice_in_dim(buffer, block[None], index, 0)]
    dynamic_slice x42 -> x1, local copies, waits for them, and re-layouts: 76.8 us -> 0.67 us  [on_rings(): lax.dynamic_slice_in_dim(conv_weight, lax.axis_index('tensor') * local, l...]
    unnamed x255 -> x23, local copies, waits for them, and re-layouts: 36.5 us -> 6.89 us
    convert_element_type x7 -> x0, local copies, waits for them, and re-layouts: 22.3 us -> none  [the longest x1 7.2 us: on_device(): up_part.astype(jnp.bfloat16).reshape(-1, shard, local_hidden)]
  transfers between devices with their start and end apart: 111 -> 0, of which waited for: 56 -> 0; matrix products, arithmetic and copies ran while one was open for 26% -> 0% of each run, Pallas kernels for 0% -> 0%
where the time goes in v2:
time: 604 us; the launch traced here: 596 us
  Pallas kernels  560 us (93%)
  local copies, waits for them, and re-layouts  22.7 us (4%)
  other arithmetic  9.77 us (2%)
    pallas_call x1, Pallas kernels, mixer_forward(): pl.pallas_call(mixer_forward_kernel, out_shape=(shape(depth, mix_own.shap...  190 us
    pallas_call x1, Pallas kernels, feed_backward(): pl.pallas_call(feed_backward_kernel, out_shape=(shape(shard, hidden, kind...  140 us
    pallas_call x1, Pallas kernels, mixer_backward(): pl.pallas_call(mixer_backward_kernel, out_shape=(shape(shard, local, kind...  124 us
    pallas_call x1, Pallas kernels, feed_forward(): pl.pallas_call(feed_forward_kernel, out_shape=(shape(depth, hidden), shap...  106 us

profile of v2, /device:TPU:0, one launch (start us, length us, event | category | flops | bytes accessed | tf_op | source)
XLA Modules:
  0.0 595.6 jit_solution(17850085787368313480)
XLA Ops:
  0.6 0.0 copy-start
  0.7 0.0 slice-start.10
  0.7 0.0 slice-start.11
  0.7 0.0 slice-start.8
  0.7 0.0 slice-start.9
  0.7 0.0 slice-start.6
  0.7 0.0 slice-start.4
  0.7 0.0 slice-start.5
  0.8 0.9 slice_compare_fusion.1
  1.7 0.1 pad_add_fusion.2
  1.7 0.8 slice_compare_fusion
  2.6 0.1 concatenate.38
  2.7 1.2 convert_bitcast_fusion
  3.9 0.8 pad_slice_fusion
  4.7 0.1 reshape.51
  4.8 1.3 broadcast_in_dim.13.gain_one.gain
  6.1 1.3 broadcast_in_dim.14.gain_two.gain
  7.4 0.7 constant_dynamic-slice_fusion.taps
  8.1 0.8 reshape.52
  8.8 0.7 pad_add_fusion.1.seg_k
  9.5 0.3 copy.39
  9.8 0.8 copy.42.valid
  10.7 1.1 concatenate.41.mix_own
  11.8 0.8 copy.40
  12.6 0.8 stack.16.same
  13.4 1.9 concatenate.42.feed_own
  15.4 1.0 copy.41.seg_q
  16.4 189.9 %shard_map.263 = (bf16[1792,1792]{1,0:T(8,128)(2,1)}, bf16[1792,448]{1,0:T(8,128)(2,1)}, bf16[1792,2432]{1,0:T(8,128)(2,1)}, bf16[1792,1024]{1,0:T(8,128)(2,1)},...) custom-call(bf16[256,1792]{1,0:T(8,128)(2,1)} %x.7, ...), custom_call_target="tpu_custom_call" | custom-call | tf_op jit(solution)/shard_map/pallas_call | solution.py:849
  206.4 1.2 slice.128
  208.2 105.7 %shard_map.264 = (bf16[1792,1216]{1,0:T(8,128)(2,1)}, bf16[1024,2432]{1,0:T(8,128)(2,1)}, bf16[1024,1216]{1,0:T(8,128)(2,1)}, f32[256,1792]{1,0:T(8,128)}, f32[2...) custom-call(f32[256,1]{1,0:T(8,128)} %copy.42.valid, ...), custom_call_target="tpu_custom_call" | custom-call | tf_op jit(solution)/shard_map/pallas_call | solution.py:1028
  313.9 140.2 %shard_map.265 = (f32[224,1216]{1,0:T(8,128)}, f32[224,2432]{1,0:T(8,128)}, f32[8,1792]{1,0:T(8,128)}, f32[256,1792]{1,0:T(8,128)}, bf16[1024,1792]{1,0:T(8,128)(2,1)}, /*index=5*/bf16[1792,1024]{1,0:T(8,128)(2,1)}) custom-call(f32[1,1792]{1,0:T(1,128)} %broadcast_in_dim.14.gain_two.gain, bf16[1024,1792]{1,0:T(8,128)(2,1)} %get-tuple-element.51.dyb_in, ...), custom_call_target="tpu_custom_call" | custom-call | tf_op jit(solution)/shard_map/pallas_call | solution.py:1185
  454.1 123.8 %shard_map.266 = (f32[224,448]{1,0:T(8,128)}, f32[224,1792]{1,0:T(8,128)}, f32[256,1792]{1,0:T(8,128)}, f32[8,1792]{1,0:T(8,128)}, f32[4,8,448]{2,1,0:T(8,128)}) custom-call(bf16[256,1792]{1,0:T(8,128)(2,1)} %x.7, f32[1,1792]{1,0:T(1,128)} %broadcast_in_dim.13.gain_one.gain, f32[1024,2]{1,0:T(8,128)} %stack.16.same, ...), custom_call_target="tpu_custom_call" | custom-call | tf_op jit(solution)/shard_map/pallas_call | solution.py:1342
  577.8 1.6 slice_reduce_fusion
  580.1 0.8 slice_bitcast_fusion
  580.9 0.7 reshape.53
  581.6 1.1 fusion.1
  582.7 1.7 fusion
  584.4 1.5 pad_maximum_fusion
  585.9 1.0 copy.44
  586.9 0.1 fusion.3
  587.0 0.1 fusion.2
  587.1 1.0 pad_maximum_fusion.4
  588.2 1.0 pad_maximum_fusion.2
  589.2 1.2 copy.48
  590.4 0.9 copy-done.4
  591.4 1.2 copy.49
  592.6 0.7 copy-done.5
  593.3 1.0 copy.50
  (36 shorter events, 0.1 us)
Async XLA Ops:
  0.6 6.7 %copy-start = (f32[3,1792]{1,0:T(4,128)S(1)}, f32[3,1792]{1,0:T(4,128)}, u32[]{:S(2)}) copy-start(f32[3,1792]{1,0:T(4,128)} %param.26) | copy-start | bytes 64516
  0.7 9.9 %slice-start.10 = ((bf16[224,448]{1,0:T(8,128)(2,1)}), bf16[224,64]{1,0:T(8,128)(2,1)S(1)}, s32[]{:S(2)}) async-start(bf16[224,448]{1,0:T(8,128)(2,1)} %param.24), calls=%async_computation.10 | async-start | bytes 114688 | tf_op jit(solution)/shard_map/slice | solution.py:1395
  0.7 9.9 %slice-start.11 = ((bf16[224,448]{1,0:T(8,128)(2,1)}), bf16[224,384]{1,0:T(8,128)(2,1)S(1)}, s32[]{:S(2)}) async-start(bf16[224,448]{1,0:T(8,128)(2,1)} %param.24), calls=%async_computation.11 | async-start | bytes 344064 | tf_op jit(solution)/shard_map/slice | solution.py:1395
  0.7 9.9 %slice-start.8 = ((bf16[224,448]{1,0:T(8,128)(2,1)}), bf16[224,64]{1,0:T(8,128)(2,1)S(1)}, s32[]{:S(2)}) async-start(bf16[224,448]{1,0:T(8,128)(2,1)} %param.23), calls=%async_computation.8 | async-start | bytes 114688 | tf_op jit(solution)/shard_map/slice | solution.py:1395
  0.7 9.9 %slice-start.9 = ((bf16[224,448]{1,0:T(8,128)(2,1)}), bf16[224,384]{1,0:T(8,128)(2,1)S(1)}, s32[]{:S(2)}) async-start(bf16[224,448]{1,0:T(8,128)(2,1)} %param.23), calls=%async_computation.9 | async-start | bytes 344064 | tf_op jit(solution)/shard_map/slice | solution.py:1395
  0.7 9.9 %slice-start.6 = ((bf16[224,448]{1,0:T(8,128)(2,1)}), bf16[224,64]{1,0:T(8,128)(2,1)S(1)}, s32[]{:S(2)}) async-start(bf16[224,448]{1,0:T(8,128)(2,1)} %param.22), calls=%async_computation.6 | async-start | bytes 114688 | tf_op jit(solution)/shard_map/slice | solution.py:1395
  0.7 9.9 %slice-start.7 = ((bf16[224,448]{1,0:T(8,128)(2,1)}), bf16[224,384]{1,0:T(8,128)(2,1)S(1)}, s32[]{:S(2)}) async-start(bf16[224,448]{1,0:T(8,128)(2,1)} %param.22), calls=%async_computation.7 | async-start | bytes 344064 | tf_op jit(solution)/shard_map/slice | solution.py:1395
  0.7 9.9 %slice-start.4 = ((bf16[224,448]{1,0:T(8,128)(2,1)}), bf16[224,64]{1,0:T(8,128)(2,1)S(1)}, s32[]{:S(2)}) async-start(bf16[224,448]{1,0:T(8,128)(2,1)} %param.21), calls=%async_computation.4 | async-start | bytes 114688 | tf_op jit(solution)/shard_map/slice | solution.py:1395
  0.7 9.9 %slice-start.5 = ((bf16[224,448]{1,0:T(8,128)(2,1)}), bf16[224,384]{1,0:T(8,128)(2,1)S(1)}, s32[]{:S(2)}) async-start(bf16[224,448]{1,0:T(8,128)(2,1)} %param.21), calls=%async_computation.5 | async-start | bytes 344064 | tf_op jit(solution)/shard_map/slice | solution.py:1395
  9.5 2.2 copy-start.7
  11.7 1.7 slice-start
  11.7 1.7 slice-start.1
  11.8 1.7 slice-start.2
  11.8 1.7 slice-start.3
  13.4 2.0 copy-start.8
  584.4 1.6 copy-start.6
  584.4 2.5 copy-start.2
  587.1 2.1 copy-start.3
  589.2 2.2 copy-start.4
  591.4 1.9 copy-start.5
  591.4 2.9 copy-start.1

commit v3 on v2

--- a/solution.py
+++ b/solution.py
@@ -12,7 +12,7 @@
 BLOCK = 512
 EPS = 1e-05
 MESH = pl.DeviceIdType.MESH
-VMEM_LIMIT = 62 * 2**20
+VMEM_LIMIT = 63 * 2**20
 
 
 def rms_scale(values):
@@ -358,45 +358,52 @@
     )
 
 
+def pieces_of(half, count):
+    if count == 1:
+        return [(0, half)]
+    first = (half // 2 + 15) // 16 * 16
+    return [(0, first), (first, half - first)]
+
+
 class RingGather:
-    def __init__(self, at, owns, slots, sems, base, local_sem):
-        half = owns[0].shape[0] // 2
+    def __init__(self, at, own, slot, sems, base, local_sem, count=2):
+        half = own.shape[0] // 2
         ring, t = at["ring"], at["t"]
-        self.local = [
-            pltpu.make_async_copy(own, slot(at["d"], 0, 2 * half), local_sem.at[n])
-            for n, (own, slot) in enumerate(zip(owns, slots))
-        ]
-        self.sends, self.receives, self.s = [], [], 0
+        self.local = pltpu.make_async_copy(own, slot(at["d"], 0, 2 * half), local_sem)
+        self.sends, self.receives, self.at = [], [], 0
         for s in range(7):
-            sends, receives = [], []
-            for way, sign in ((0, 1), (1, -1)):
-                to = (ring(sign), t)
-                for n, (own, slot) in enumerate(zip(owns, slots)):
-                    index = base + (2 * s + way) * len(owns) + n
-                    here = slot(ring(-sign * s), way * half, half)
-                    there = slot(ring(-sign * (s + 1)), way * half, half)
-                    source = own.at[pl.ds(way * half, half)] if s == 0 else here
+            for k, (first, size) in enumerate(pieces_of(half, count)):
+                sends, receives = [], []
+                for way, sign in ((0, 1), (1, -1)):
+                    to, row = (ring(sign), t), way * half + first
+                    index = base + (s * count + k) * 2 + way
+                    here = slot(ring(-sign * s), row, size)
+                    there = slot(ring(-sign * (s + 1)), row, size)
+                    source = own.at[pl.ds(row, size)] if s == 0 else here
                     sends.append(remote(source, here, sems, index, to))
                     receives.append(remote(there, there, sems, index, to))
-            self.sends.append(sends)
-            self.receives.append(receives)
+                self.sends.append(sends)
+                self.receives.append(receives)
+        self.count = count
 
     def start(self):
-        for copy in self.sends[0] + self.local:
-            copy.start()
-
-    def step(self):
-        for k, copy in enumerate(self.receives[self.s]):
-            copy.wait_recv()
-            if self.s < 6:
-                self.sends[self.s + 1][k].start()
-        self.s += 1
+        for copies in self.sends[: self.count]:
+            for copy in copies:
+                copy.start()
+        self.local.start()
+
+    def tick(self):
+        if self.at < len(self.receives):
+            for way in range(2):
+                self.receives[self.at][way].wait_recv()
+                if self.at + self.count < len(self.sends):
+                    self.sends[self.at + self.count][way].start()
+            self.at += 1
 
     def finish(self):
-        while self.s < 7:
-            self.step()
-        for copy in self.local:
-            copy.wait()
+        while self.at < len(self.receives):
+            self.tick()
+        self.local.wait()
 
     def drain(self):
         for sends in self.sends:
@@ -405,21 +412,25 @@
 
 
 class RingScatter:
-    def __init__(self, at, left, right, slots, term, out, sems, base):
+    def __init__(self, at, left, right, slots, term, out, sems, base, count=2):
         self.ring, self.left, self.right = at["ring"], left, right
         self.slots, self.term, self.out = slots, term, out
         self.half, self.columns = slots.shape[2], slots.shape[3]
-        self.s = 0
-        self.sends = [
-            [
-                remote(
-                    slots.at[way, s], slots.at[way, s + 1], sems, base + 2 * s + way,
-                    (at["ring"](sign), at["t"]),
+        self.pieces = pieces_of(self.half, count)
+        self.at = 0
+        self.sends = []
+        for s in range(7):
+            for k, (first, size) in enumerate(self.pieces):
+                rows = pl.ds(first, size)
+                self.sends.append(
+                    [
+                        remote(
+                            slots.at[way, s, rows], slots.at[way, s + 1, rows], sems,
+                            base + (s * count + k) * 2 + way, (at["ring"](sign), at["t"]),
+                        )
+                        for way, sign in ((0, 1), (1, -1))
+                    ]
                 )
-                for way, sign in ((0, 1), (1, -1))
-            ]
-            for s in range(7)
-        ]
 
     def compute(self, away):
         half = self.half
@@ -443,28 +454,36 @@
 
     def start(self):
         self.compute(1)
+        for k, (first, size) in enumerate(self.pieces):
+            for way in range(2):
+                self.slots[way, 0, pl.ds(first, size)] = self.term[
+                    pl.ds(way * self.half + first, size)
+                ].astype(jnp.bfloat16)
+                self.sends[k][way].start()
+        self.compute(2)
+
+    def tick(self):
+        if self.at == len(self.sends):
+            return
+        count = len(self.pieces)
+        s, k = divmod(self.at, count)
+        first, size = self.pieces[k]
         for way in range(2):
-            rows = pl.ds(way * self.half, self.half)
-            self.slots[way, 0] = self.term[rows, pl.ds(0, self.columns)].astype(jnp.bfloat16)
-            self.sends[0][way].start()
-
-    def step(self):
-        s, half = self.s, self.half
-        self.compute(s + 2)
-        for way in range(2):
-            rows = pl.ds(way * half, half)
-            self.sends[s][way].wait_recv()
-            total = self.slots[way, s + 1].astype(jnp.float32) + self.term[rows, pl.ds(0, self.columns)]
+            here, rows = pl.ds(first, size), pl.ds(way * self.half + first, size)
+            self.sends[self.at][way].wait_recv()
+            total = self.slots[way, s + 1, here].astype(jnp.float32) + self.term[rows]
             if s < 6:
-                self.slots[way, s + 1] = total.astype(jnp.bfloat16)
-                self.sends[s + 1][way].start()
+                self.slots[way, s + 1, here] = total.astype(jnp.bfloat16)
+                self.sends[self.at + count][way].start()
             else:
                 self.out[rows] = total
-        self.s += 1
+        self.at += 1
+        if k == count - 1 and s < 6:
+            self.compute(s + 3)
 
     def finish(self):
-        while self.s < 7:
-            self.step()
+        while self.at < len(self.sends):
+            self.tick()
         for sends in self.sends:
             for copy in sends:
                 copy.wait_send()
@@ -503,7 +522,7 @@
         self.drain()
 
 
-def sum_rows(at, block_part, send, receive, total, sems, base, idle=None):
+def sum_rows(at, block_part, send, receive, total, sems, base, idle=lambda point: None):
     to_core, to_cross = (at["d"], at["core"]), (at["d"], at["cross"])
     low = jnp.bfloat16
     first = remote(send.at[0], receive.at[0], sems, base, to_core)
@@ -515,14 +534,16 @@
     first.wait_recv()
     send[1] = (total[...] + receive[0].astype(jnp.float32)).astype(low)
     second.start()
+    idle(0)
     send[2] = block_part(at["core"]).astype(low)
     third.start()
+    idle(1)
     total[...] = block_part(at["t"])
-    if idle is not None:
-        idle()
     third.wait_recv()
+    total[...] += receive[2].astype(jnp.float32)
+    idle(2)
     second.wait_recv()
-    total[...] += receive[2].astype(jnp.float32) + receive[1].astype(jnp.float32)
+    total[...] += receive[1].astype(jnp.float32)
     for copy in (first, second, third):
         copy.wait_send()
 
@@ -631,7 +652,7 @@
 
 
 def attend_back_tile(
-    i, q, k_pad, v_pad, u, p, same, taps, do, dq, du, dk, dv, conv_sum
+    i, q, k_pad, v_pad, u, p, same, taps, do, dk, dv, conv_sum
 ):
     row = pl.multiple_of(i * TILE, TILE)
     at_row, at_window = pl.ds(row, TILE), pl.ds(row, 2 * TILE)
@@ -646,11 +667,11 @@
         weighted = chance * nt_dot(grad_heads, values)
         slope = weighted - chance * jnp.sum(weighted, axis=1, keepdims=True)
         slope = (slope * (HEAD_DIM**-0.5)).astype(jnp.bfloat16)
-        dq[at_row, lanes] = join_heads(nn_dot(slope, keys), heads).astype(jnp.bfloat16)
         dk[at_window, lanes] += tn_dot(slope, split_heads(q[at_row, lanes], heads))
+        q[at_row, lanes] = join_heads(nn_dot(slope, keys), heads).astype(jnp.bfloat16)
         convolved, rows = convolve(values.astype(jnp.float32), taps, lanes, same_one, same_two)
         grad = grad.astype(jnp.float32)
-        du[at_row, lanes] = (grad * convolved).astype(jnp.bfloat16)
+        do[at_row, lanes] = (grad * convolved).astype(jnp.bfloat16)
         grad_conv = grad * u[at_row, lanes].astype(jnp.float32)
         back = tn_dot(chance_low, grad_heads)
         zero = jnp.zeros_like(grad_conv)
@@ -699,13 +720,12 @@
     def slot_of(full):
         return lambda i, first, size: full.at[pl.ds(pl.multiple_of(i * shard + first, 16), size)]
 
-    early = RingGather(
-        at, [mix_own, out_own], [slot_of(mix), slot_of(last)], sems, 0, local_sems.at[pl.ds(0, 2)]
-    )
-    late = RingGather(at, [feed_own], [slot_of(feed)], sems, 28, local_sems.at[pl.ds(2, 1)])
-    group_one = GatherTensor(at, h1, rows, sems, 42)
-    group_two = GatherTensor(at, h2, rows, sems, 45)
-    counting = SumAll(at, count, count_in, sems, 51)
+    early = RingGather(at, mix_own, slot_of(mix), sems, 0, local_sems.at[0])
+    middle = RingGather(at, out_own, slot_of(last), sems, 28, local_sems.at[1], count=1)
+    late = RingGather(at, feed_own, slot_of(feed), sems, 42, local_sems.at[2])
+    group_one = GatherTensor(at, h1, rows, sems, 70)
+    group_two = GatherTensor(at, h2, rows, sems, 73)
+    counting = SumAll(at, count, count_in, sems, 79)
     local = q.shape[1]
     main = local // LANES * LANES
     tail = local - main
@@ -729,17 +749,21 @@
     counting.start()
     k_pad[pl.ds(0, TILE)] = jnp.zeros((TILE, local), k_pad.dtype)
     v_pad[pl.ds(0, TILE)] = jnp.zeros((TILE, local), v_pad.dtype)
-    early.step()
+    early.tick()
+    early.tick()
     counting.step()
-    early.step()
+    early.tick()
+    early.tick()
     counting.step()
+    early.tick()
     group_one.relay()
-    early.step()
+    early.tick()
     counting.step()
-    early.step()
+    early.tick()
+    early.tick()
     counting.step()
     group_one.finish()
-    early.step()
+    early.tick()
 
     @pl.loop(0, 4)
     def _(j):
@@ -747,13 +771,19 @@
         h1t[:, pl.ds(here, rows)] = h1[pl.ds(here, rows)].T
 
     keep(h1t, h1t_out)
+    early.tick()
     counting.finish()
     keep(count.at[5], count_out)
-    early.step()
+    middle.start()
+    early.tick()
+    early.tick()
+    middle.tick()
     late.start()
+    early.tick()
+    middle.tick()
     early.finish()
+    middle.tick()
     keep(mix, mix_out)
-    keep(last, last_out)
 
     def project(j):
         here = pl.ds(pl.multiple_of(j * rows, rows), rows)
@@ -772,13 +802,21 @@
         v_pad[there, pl.ds(main, tail)] = ends[:, 2 * tail : 3 * tail].astype(low)
         u[here, pl.ds(main, tail)] = ends[:, 3 * tail :].astype(low)
 
-    @pl.loop(0, h1.shape[0] // rows)
-    def _(j):
-        project(j)
-
+    def projects(first, last_block):
+        @pl.loop(first, last_block)
+        def _(j):
+            project(j)
+
+    def tick():
+        late.tick()
+        middle.tick()
+
+    projects(0, 2)
+    tick()
+    projects(2, 4)
     for source, target in ((q, q_out), (k_pad, k_out), (v_pad, v_out), (u, u_out)):
         keep(source, target)
-    late.step()
+    tick()
     tiles = q.shape[0] // TILE
 
     def attend(first, last_tile):
@@ -786,19 +824,23 @@
         def _(i):
             attend_tile(i, q, k_pad, v_pad, u, seg_q, seg_k, same, taps, p, o)
 
-    attend(0, tiles // 2)
-    late.step()
-    attend(tiles // 2, tiles)
+    for k in range(4):
+        attend(k * tiles // 4, (k + 1) * tiles // 4)
+        tick()
+    middle.finish()
+    keep(last, last_out)
     keep(p, p_out)
     keep(o, o_out)
 
     def part(block):
         return nt_dot(o[pl.ds(pl.multiple_of(block * rows, rows), rows)], last[...])
 
-    def idle():
-        late.step()
-
-    sum_rows(at, part, send, receive, total, sems, 48, idle=idle)
+    def idle(point):
+        late.tick()
+        if point == 2:
+            late.tick()
+
+    sum_rows(at, part, send, receive, total, sems, 76, idle=idle)
 
     @chunks_of(rows)
     def _(row, size):
@@ -809,14 +851,15 @@
 
     group_two.start()
     keep(total, x1_out)
-    late.step()
-    late.step()
+    for _ in range(3):
+        late.tick()
     group_two.relay()
+    late.tick()
     group_two.finish()
     keep(h2, h2_out)
     late.finish()
-    early.drain()
-    late.drain()
+    for ring in (early, middle, late):
+        ring.drain()
     for copy in keeps:
         copy.wait()
 
@@ -882,8 +925,8 @@
             pltpu.VMEM((rows, width), wide),
             pltpu.VMEM((6, 8, LANES), wide),
             pltpu.VMEM((5, 8, LANES), wide),
-            dma(56),
-            dma(56),
+            dma(84),
+            dma(84),
             dma(3),
             dma(12),
         ],
@@ -916,11 +959,10 @@
     low = jnp.bfloat16
     greet(at)
     ring = RingGather(
-        at, [down_own],
-        [lambda i, first, size: down.at[pl.ds(pl.multiple_of(i * shard + first, 16), size)]],
-        sems, 0, local_sems,
-    )
-    group = GatherTensor(at, dyb, rows, sems, 17)
+        at, down_own, lambda i, first, size: down.at[pl.ds(pl.multiple_of(i * shard + first, 16), size)],
+        sems, 0, local_sems.at[0],
+    )
+    group = GatherTensor(at, dyb, rows, sems, 31)
     loads = [
         pltpu.make_async_copy(source, target, load_sems.at[n])
         for n, (source, target) in enumerate(
@@ -958,13 +1000,13 @@
             active[here, pl.ds(main, tail)] = a.astype(low)
             slopes[here, pl.ds(2 * main, 2 * tail)] = jnp.concatenate([by_gate, by_up], axis=1).astype(low)
 
-    ring.step()
-    widen(0, 2)
-    ring.step()
-    widen(2, 4)
+    ring.tick()
+    for k in range(4):
+        widen(k, k + 1)
+        ring.tick()
     keep(active, active_out)
     keep(slopes, slopes_out)
-    ring.step()
+    ring.tick()
 
     def turn(source, block):
         here = pl.multiple_of(block * rows, rows)
@@ -983,7 +1025,7 @@
     def part(block):
         return nt_dot(active[pl.ds(pl.multiple_of(block * rows, rows), rows)], down[...])
 
-    sum_rows(at, part, send, receive, total, sems, 14)
+    sum_rows(at, part, send, receive, total, sems, 28)
     weight = (rows * 4 * 8) / count[0:1, 0:1]
     squares_out[...] = jnp.zeros_like(squares_out)
 
@@ -1054,8 +1096,8 @@
             pltpu.VMEM((3, rows, width), low),
             pltpu.VMEM((3, rows, width), low),
             pltpu.VMEM((rows, width), wide),
-            dma(20),
-            dma(20),
+            dma(34),
+            dma(34),
             dma(1),
             dma(5),
             dma(8),
@@ -1065,9 +1107,10 @@
 
 
 def feed_backward_kernel(
-    gain, dyb_in, dybt_in, h2t_in, down_in, feed_in, active_in, slopes_in, x1_in, dy_in,
-    down_grad, feed_grad, gain_part, dx1_out, dx1b_out, dx1t_out,
-    dyb, dybt, h2t, down, feed, active, slopes, side, total, down_slots, feed_slots, term, send, receive,
+    gain, dyb_in, dybt_in, h2t_in, down_in, feed_in, active_in, slopes_in, last_in, x1_in, dy_in,
+    down_grad, gate_grad, gain_part, dx1_out, dx1t_out, do_out, slopes_out,
+    dyb, dybt, h2t, down, feed, active, slopes, last, do, side, total, down_slots, gate_slots,
+    down_term, gate_term, send, receive,
     send_sems, recv_sems, load_sems, out_sems,
 ):
     at = neighbours()
@@ -1079,21 +1122,28 @@
         for n, (source, target) in enumerate(
             (
                 (dybt_in, dybt), (active_in, active), (dyb_in, dyb), (down_in, down), (slopes_in, slopes),
-                (feed_in, feed), (h2t_in, h2t), (x1_in, side), (dy_in, side),
+                (h2t_in, h2t), (feed_in, feed), (last_in, last), (x1_in, side), (dy_in, side),
             )
         )
     ]
     for load in loads[:-1]:
         load.start()
     greet(at)
-    first = RingScatter(
-        at, dybt, active, down_slots, term, down_grad, sems, 0
-    )
-    second = RingScatter(at, h2t, slopes, feed_slots, term, feed_grad, sems, 14)
-    group = GatherTensor(at, dyb, rows, sems, 31)
     hidden = active.shape[1]
     parts, main = feed_lanes(hidden)
     tail = hidden - main
+    first = RingScatter(at, dybt, active, down_slots, down_term, down_grad, sems, 0)
+    second = RingScatter(
+        at, h2t, slopes.at[:, pl.ds(0, main)], gate_slots, gate_term, gate_grad, sems, 28
+    )
+    group = GatherTensor(at, dyb, rows, sems, 59)
+    keeps = []
+
+    def keep(source, target):
+        copy = pltpu.make_async_copy(source, target, out_sems.at[len(keeps)])
+        copy.start()
+        keeps.append(copy)
+
     loads[0].wait()
     loads[1].wait()
     first.start()
@@ -1114,24 +1164,26 @@
             both = jnp.concatenate([da, da], axis=1) * slopes[here, ends].astype(jnp.float32)
             slopes[here, ends] = both.astype(low)
 
-    slope_back(0, 2)
-    first.step()
-    slope_back(2, 4)
-    first.step()
+    for k in range(4):
+        slope_back(k, k + 1)
+        first.tick()
+    keep(slopes.at[:, pl.ds(main, 2 * hidden - main)], slopes_out)
+    loads[5].wait()
+    second.start()
     loads[6].wait()
-    second.start()
-    loads[5].wait()
-    loads[7].wait()
+    loads[8].wait()
 
     def part(block):
         return nt_dot(slopes[pl.ds(pl.multiple_of(block * rows, rows), rows)], feed[...])
 
-    def idle():
-        first.step()
-        first.step()
-        second.step()
-
-    sum_rows(at, part, send, receive, total, sems, 28, idle=idle)
+    def idle(point):
+        first.tick()
+        second.tick()
+        if point == 2:
+            first.tick()
+            second.tick()
+
+    sum_rows(at, part, send, receive, total, sems, 56, idle=idle)
     gain_part[...] = jnp.zeros_like(gain_part)
 
     @chunks_of(rows, 32)
@@ -1141,8 +1193,10 @@
         gain_part[0:1] += term_gain
         total[here] = through
 
-    loads[8].start()
-    loads[8].wait()
+    loads[9].start()
+    first.tick()
+    second.tick()
+    loads[9].wait()
 
     @chunks_of(rows, 32)
     def _(row, size):
@@ -1152,33 +1206,41 @@
         dyb[pl.ds(pl.multiple_of(at["t"] * rows + row, size), size)] = grad.astype(low)
 
     group.start()
-    keeps = [pltpu.make_async_copy(total, dx1_out, out_sems.at[0])]
-    keeps[0].start()
-    first.step()
-    second.step()
-    first.step()
-    second.step()
+    keep(total, dx1_out)
+    loads[7].wait()
+
+    def spread(block):
+        here = pl.ds(pl.multiple_of(block * rows, rows), rows)
+        dybt[:, here] = dyb[here].T
+        do[here] = nn_dot(dyb[here], last[...]).astype(low)
+
+    while first.at < len(first.sends):
+        first.tick()
+        second.tick()
+    spread(at["t"])
+    second.tick()
+    group.receives[0].wait_recv()
+    spread(at["core"])
+    second.tick()
     group.relay()
+    second.tick()
+    spread(at["cross"])
+    group.receives[2].wait_recv()
+    spread(at["cross_core"])
+    group.drain()
+    keep(dybt, dx1t_out)
+    keep(do, do_out)
+    second.finish()
     first.finish()
-    second.step()
-    group.finish()
-
-    @pl.loop(0, 4)
-    def _(j):
-        here = pl.multiple_of(j * rows, rows)
-        dybt[:, pl.ds(here, rows)] = dyb[pl.ds(here, rows)].T
-
-    for source, target in ((dyb, dx1b_out), (dybt, dx1t_out)):
-        keeps.append(pltpu.make_async_copy(source, target, out_sems.at[len(keeps)]))
-        keeps[-1].start()
-    second.finish()
     for copy in keeps:
         copy.wait()
 
 
-def feed_backward(gain, dyb, dybt, h2t, down, feed, active, slopes, x1, dy):
+def feed_backward(gain, dyb, dybt, h2t, down, feed, active, slopes, last, x1, dy):
     rows, width = x1.shape
     depth, hidden = down.shape
+    local = last.shape[1]
+    main = hidden // LANES * LANES
     everyone, shard = 4 * rows, depth // 8
     low, wide = jnp.bfloat16, jnp.float32
     vmem, hbm = specs()
@@ -1186,14 +1248,15 @@
         feed_backward_kernel,
         out_shape=(
             shape(shard, hidden, kind=wide),
-            shape(shard, 2 * hidden, kind=wide),
+            shape(shard, main, kind=wide),
             shape(8, width, kind=wide),
             shape(rows, width, kind=wide),
-            shape(everyone, width),
             shape(width, everyone),
+            shape(everyone, local),
+            shape(everyone, 2 * hidden - main),
         ),
-        in_specs=[vmem] + [hbm] * 9,
-        out_specs=(vmem,) * 3 + (hbm,) * 3,
+        in_specs=[vmem] + [hbm] * 10,
+        out_specs=(vmem,) * 3 + (hbm,) * 4,
         scratch_shapes=[
             pltpu.VMEM((everyone, width), low),
             pltpu.VMEM((width, everyone), low),
@@ -1202,28 +1265,31 @@
             pltpu.VMEM((depth, 2 * hidden), low),
             pltpu.VMEM((everyone, hidden), low),
             pltpu.VMEM((everyone, 2 * hidden), low),
+            pltpu.VMEM((depth, local), low),
+            pltpu.VMEM((everyone, local), low),
             pltpu.VMEM((rows, width), wide),
             pltpu.VMEM((rows, width), wide),
             pltpu.VMEM((2, 8, shard // 2, hidden), low),
-            pltpu.VMEM((2, 8, shard // 2, 2 * hidden), low),
-            pltpu.VMEM((shard, 2 * hidden), wide),
+            pltpu.VMEM((2, 8, shard // 2, main), low),
+            pltpu.VMEM((shard, hidden), wide),
+            pltpu.VMEM((shard, main), wide),
             pltpu.VMEM((3, rows, width), low),
             pltpu.VMEM((3, rows, width), low),
-            dma(34),
-            dma(34),
-            dma(9),
-            dma(3),
+            dma(62),
+            dma(62),
+            dma(10),
+            dma(4),
         ],
         compiler_params=params(3),
-    )(gain, dyb, dybt, h2t, down, feed, active, slopes, x1, dy)
+    )(gain, dyb, dybt, h2t, down, feed, active, slopes, last, x1, dy)
 
 
 def mixer_backward_kernel(
     x, gain, same, taps, gain_part, squares,
-    dx1b_in, dx1t_in, o_in, last_in, q_in, k_in, v_in, u_in, p_in, h1t_in, mix_in, dx1_in,
-    out_grad, mix_grad, input_grad, small_out, conv_out,
-    dx1b, dx1t, o, last, q, k_pad, v_pad, u, p, h1t, mix,
-    do, dq, du, dk, dv, grads, out_slots, mix_slots, term, send, receive, total,
+    dx1t_in, o_in, h2t_in, slopes_in, q_in, k_in, v_in, u_in, p_in, do_in, mix_in, h1t_in, dx1_in,
+    out_grad, up_grad, mix_grad, input_grad, small_out, conv_out,
+    turned, o, h2t, slopes, q, k_pad, v_pad, u, p, do, mix,
+    dk, dv, grads, out_slots, up_slots, mix_slots, out_term, up_term, mix_term, send, receive, total,
     small, small_in, conv, conv_in,
     send_sems, recv_sems, load_sems,
 ):
@@ -1235,37 +1301,34 @@
         pltpu.make_async_copy(source, target, load_sems.at[n])
         for n, (source, target) in enumerate(
             (
-                (dx1t_in, dx1t), (o_in, o), (dx1b_in, dx1b), (last_in, last), (q_in, q), (k_in, k_pad),
-                (v_in, v_pad), (u_in, u), (p_in, p), (h1t_in, h1t), (mix_in, mix), (dx1_in, input_grad),
+                (dx1t_in, turned), (o_in, o), (h2t_in, h2t), (slopes_in, slopes), (q_in, q), (k_in, k_pad),
+                (v_in, v_pad), (u_in, u), (p_in, p), (do_in, do), (mix_in, mix), (dx1_in, input_grad),
+                (h1t_in, turned),
             )
         )
     ]
-    for load in loads:
+    for load in loads[:-1]:
         load.start()
     greet(at, everyone=True)
     local = q.shape[1]
     main = local // LANES * LANES
     tail = local - main
-    first = RingScatter(at, dx1t, o, out_slots, term, out_grad, sems, 0)
-    second = RingScatter(at, h1t, grads, mix_slots, term, mix_grad, sems, 14)
-    small_sum = SumAll(at, small, small_in, sems, 31)
-    conv_all = SumAll(at, conv, conv_in, sems, 36)
+    first = RingScatter(at, turned, o, out_slots, out_term, out_grad, sems, 0, count=1)
+    second = RingScatter(at, h2t, slopes, up_slots, up_term, up_grad, sems, 14)
+    third = RingScatter(at, turned, grads, mix_slots, mix_term, mix_grad, sems, 42)
+    small_sum = SumAll(at, small, small_in, sems, 73)
+    conv_all = SumAll(at, conv, conv_in, sems, 78)
     loads[0].wait()
     loads[1].wait()
     first.start()
     loads[2].wait()
     loads[3].wait()
+    second.start()
     dk[...] = jnp.zeros_like(dk)
     dv[...] = jnp.zeros_like(dv)
     conv[0] = jnp.zeros(conv.shape[1:], jnp.float32)
-
-    @pl.loop(0, 4)
-    def _(j):
-        here = pl.ds(pl.multiple_of(j * rows, rows), rows)
-        do[here] = nn_dot(dx1b[here], last[...]).astype(low)
-
-    first.step()
-    for load in loads[4:9]:
+    first.tick()
+    for load in loads[4:10]:
         load.wait()
     tiles = q.shape[0] // TILE
     conv_sum = conv.at[0, at["t"]]
@@ -1273,38 +1336,43 @@
     def attend(a, b):
         @pl.loop(a, b)
         def _(i):
-            attend_back_tile(i, q, k_pad, v_pad, u, p, same, taps, do, dq, du, dk, dv, conv_sum)
+            attend_back_tile(i, q, k_pad, v_pad, u, p, same, taps, do, dk, dv, conv_sum)
 
     for k in range(4):
         attend(k * tiles // 4, (k + 1) * tiles // 4)
-        first.step()
+        first.tick()
+        second.tick()
     conv_all.start()
 
     @chunks_of(q.shape[0])
     def _(row, size):
         here, there = pl.ds(row, size), pl.ds(pl.multiple_of(row + TILE, TILE), size)
-        four = [dq[here].astype(jnp.float32), dk[there], dv[there], du[here].astype(jnp.float32)]
+        four = [q[here].astype(jnp.float32), dk[there], dv[there], do[here].astype(jnp.float32)]
         for n, value in enumerate(four):
             grads[here, pl.ds(n * main, main)] = value[:, :main].astype(low)
         ends = jnp.concatenate([value[:, main:] for value in four], axis=1)
         grads[here, pl.ds(4 * main, 4 * tail)] = ends.astype(low)
 
-    loads[9].wait()
-    second.start()
     first.finish()
+    loads[12].start()
+    second.tick()
+    second.tick()
+    loads[12].wait()
     loads[10].wait()
     loads[11].wait()
+    third.start()
 
     def part(block):
         return nt_dot(grads[pl.ds(pl.multiple_of(block * rows, rows), rows)], mix[...])
 
-    def idle():
-        second.step()
-        conv_all.step()
-        second.step()
-        conv_all.step()
-
-    sum_rows(at, part, send, receive, total, sems, 28, idle=idle)
+    def idle(point):
+        second.tick()
+        third.tick()
+        if point == 2:
+            second.tick()
+            conv_all.step()
+
+    sum_rows(at, part, send, receive, total, sems, 70, idle=idle)
     small[0, 0:1] = jnp.zeros((1, small.shape[2]), jnp.float32)
     small[0, 1:2] = gain_part[0:1]
     small[0, 2:3] = squares[0:1]
@@ -1318,48 +1386,52 @@
         input_grad[here] += through
 
     small_sum.start()
-    while second.s < 6:
-        second.step()
-        if conv_all.s < 5:
-            conv_all.step()
+    for k in range(4):
+        second.tick()
+        third.tick()
+        conv_all.step()
+        second.tick()
+        third.tick()
         small_sum.step()
     small_sum.finish()
     conv_all.finish()
     second.finish()
+    third.finish()
     small_out[...] = small[5]
     conv_out[...] = conv[5]
 
 
 def mixer_backward(
-    x, gain, same, taps, gain_part, squares, dx1b, dx1t, o, last, q, k_pad, v_pad, u, p, h1t, mix, dx1
+    x, gain, same, taps, gain_part, squares, dx1t, o, h2t, slopes, q, k_pad, v_pad, u, p, do, mix, h1t, dx1
 ):
     rows, width = x.shape
-    depth, local = last.shape
-    everyone, shard = 4 * rows, depth // 8
+    everyone, local = o.shape
+    shard, ups = width // 8, slopes.shape[1]
     low, wide = jnp.bfloat16, jnp.float32
     vmem, hbm = specs()
-    arrays = (dx1b, dx1t, o, last, q, k_pad, v_pad, u, p, h1t, mix)
+    arrays = (dx1t, o, h2t, slopes, q, k_pad, v_pad, u, p, do, mix)
     return pl.pallas_call(
         mixer_backward_kernel,
         out_shape=(
             shape(shard, local, kind=wide),
+            shape(shard, ups, kind=wide),
             shape(shard, 4 * local, kind=wide),
             shape(rows, width, kind=wide),
             shape(8, width, kind=wide),
             shape(4, 8, local, kind=wide),
         ),
-        in_specs=[vmem] * 6 + [hbm] * 12,
-        out_specs=(vmem,) * 5,
+        in_specs=[vmem] * 6 + [hbm] * 13,
+        out_specs=(vmem,) * 6,
         scratch_shapes=[pltpu.VMEM(array.shape, array.dtype) for array in arrays]
         + [
-            pltpu.VMEM((everyone, local), low),
-            pltpu.VMEM((everyone, local), low),
-            pltpu.VMEM((everyone, local), low),
             pltpu.VMEM((everyone + TILE, local), wide),
             pltpu.VMEM((everyone + TILE, local), wide),
             pltpu.VMEM((everyone, 4 * local), low),
             pltpu.VMEM((2, 8, shard // 2, local), low),
+            pltpu.VMEM((2, 8, shard // 2, ups), low),
             pltpu.VMEM((2, 8, shard // 2, 4 * local), low),
+            pltpu.VMEM((shard, local), wide),
+            pltpu.VMEM((shard, ups), wide),
             pltpu.VMEM((shard, 4 * local), wide),
             pltpu.VMEM((3, rows, width), low),
             pltpu.VMEM((3, rows, width), low),
@@ -1368,12 +1440,12 @@
             pltpu.VMEM((5, 8, width), wide),
             pltpu.VMEM((6, 4, 8, local), wide),
             pltpu.VMEM((5, 4, 8, local), wide),
-            dma(41),
-            dma(41),
-            dma(12),
+            dma(83),
+            dma(83),
+            dma(13),
         ],
         compiler_params=params(4),
-    )(x, gain, same, taps, gain_part, squares, *arrays, dx1)
+    )(x, gain, same, taps, gain_part, squares, *arrays, h1t, dx1)
 
 
 def segment_tables(segments):
@@ -1443,14 +1515,17 @@
     down, slopes, active, outputs, dy, dyb, dybt, h2t, squares = feed_forward(
         valid[:, None], count, h2, feed, x1, cotangent, teacher, down_weight.T
     )
-    down_grad, feed_grad, gain_part, dx1, dx1b, dx1t = feed_backward(
-        gain_two, dyb, dybt, h2t, down, feed, active, slopes, x1, dy
-    )
-    out_grad, mix_grad, input_grad, small, conv = mixer_backward(
-        block_input, gain_one, same, taps, gain_part, squares, dx1b, dx1t, o, last, q, k_pad, v_pad,
-        u, p, h1t, mix, dx1,
-    )
-    gate_grad, up_grad = unpack(feed_grad, 2)
+    down_grad, gate_main, gain_part, dx1, dx1t, do, slopes_up = feed_backward(
+        gain_two, dyb, dybt, h2t, down, feed, active, slopes, last, x1, dy
+    )
+    out_grad, up_rest, mix_grad, input_grad, small, conv = mixer_backward(
+        block_input, gain_one, same, taps, gain_part, squares, dx1t, o, h2t, slopes_up, q, k_pad, v_pad,
+        u, p, do, mix, h1t, dx1,
+    )
+    main = gate_main.shape[1]
+    tail = gate_weight.shape[1] - main
+    gate_grad = jnp.concatenate([gate_main, up_rest[:, main : main + tail]], axis=1)
+    up_grad = jnp.concatenate([up_rest[:, :main], up_rest[:, main + tail :]], axis=1)
     mean_loss = jnp.sum(small[2]) / (count[0, 0] * D)
     return (
         mean_loss,

time: 604 us -> 565 us (0.935)
  Pallas kernels: 560 us -> 520 us
    pallas_call x1, Pallas kernels: 140 us -> 93.1 us  [feed_backward(): pl.pallas_call(feed_backward_kernel, out_shape=(shape(shard, hidden, kind...]
    pallas_call x1, Pallas kernels: 124 us -> 141 us  [mixer_backward(): pl.pallas_call(mixer_backward_kernel, out_shape=(shape(shard, local, kind...]
    pallas_call x1, Pallas kernels: 190 us -> 183 us  [mixer_forward(): pl.pallas_call(mixer_forward_kernel, out_shape=(shape(depth, mix_own.shap...]
where the time goes in v3:
time: 565 us; the launch traced here: 558 us
  Pallas kernels  520 us (92%)
  local copies, waits for them, and re-layouts  22.4 us (4%)
  other arithmetic  11.7 us (2%)
    pallas_call x1, Pallas kernels, mixer_forward(): pl.pallas_call(mixer_forward_kernel, out_shape=(shape(depth, mix_own.shap...  183 us
    pallas_call x1, Pallas kernels, mixer_backward(): pl.pallas_call(mixer_backward_kernel, out_shape=(shape(shard, local, kind...  141 us
    pallas_call x1, Pallas kernels, feed_forward(): pl.pallas_call(feed_forward_kernel, out_shape=(shape(depth, hidden), shap...  103 us
    pallas_call x1, Pallas kernels, feed_backward(): pl.pallas_call(feed_backward_kernel, out_shape=(shape(shard, hidden, kind...  93.1 us

profile of v3, /device:TPU:0, one launch (start us, length us, event | category | flops | bytes accessed | tf_op | source)
XLA Modules:
  0.0 557.7 jit_solution(14766262687626784373)
XLA Ops:
  0.6 0.0 copy-start
  0.7 0.0 slice-start.11
  0.7 0.0 slice-start.8
  0.7 0.0 slice-start.6
  0.7 0.0 slice-start.7
  0.8 0.9 slice_compare_fusion.1
  1.7 0.1 pad_add_fusion.2
  1.7 0.8 slice_compare_fusion
  2.6 0.1 concatenate.38
  2.7 1.2 convert_bitcast_fusion
  3.9 0.8 pad_slice_fusion
  4.7 0.1 reshape.51
  4.8 1.3 broadcast_in_dim.13.gain_one.gain
  6.1 1.3 broadcast_in_dim.14.gain_two.gain
  7.4 0.7 constant_dynamic-slice_fusion.taps
  8.1 0.8 reshape.52
  8.8 0.7 pad_add_fusion.1.seg_k
  9.5 0.3 copy.39
  9.8 0.8 copy.42.valid
  10.7 1.1 concatenate.41.mix_own
  11.8 0.8 copy.40
  12.6 0.8 stack.16.same
  13.4 1.9 concatenate.42.feed_own
  15.4 1.0 copy.41.seg_q
  16.4 183.2 %shard_map.263 = (bf16[1792,1792]{1,0:T(8,128)(2,1)}, bf16[1792,448]{1,0:T(8,128)(2,1)}, bf16[1792,2432]{1,0:T(8,128)(2,1)}, bf16[1792,1024]{1,0:T(8,128)(2,1)},...) custom-call(bf16[256,1792]{1,0:T(8,128)(2,1)} %x.7, ...), custom_call_target="tpu_custom_call" | custom-call | tf_op jit(solution)/shard_map/pallas_call | solution.py:892
  199.6 1.2 slice.125
  201.5 102.6 %shard_map.264 = (bf16[1792,1216]{1,0:T(8,128)(2,1)}, bf16[1024,2432]{1,0:T(8,128)(2,1)}, bf16[1024,1216]{1,0:T(8,128)(2,1)}, f32[256,1792]{1,0:T(8,128)}, f32[2...) custom-call(f32[256,1]{1,0:T(8,128)} %copy.42.valid, ...), custom_call_target="tpu_custom_call" | custom-call | tf_op jit(solution)/shard_map/pallas_call | solution.py:1070
  304.1 93.1 %shard_map.265 = (f32[224,1216]{1,0:T(8,128)}, f32[224,1152]{1,0:T(8,128)}, f32[8,1792]{1,0:T(8,128)}, f32[256,1792]{1,0:T(8,128)}, bf16[1792,1024]{1,0:T(8,128)...) custom-call(f32[1,1792]{1,0:T(1,128)} %broadcast_in_dim.14.gain_two.gain, ...), custom_call_target="tpu_custom_call" | custom-call | tf_op jit(solution)/shard_map/pallas_call | solution.py:1247
  397.2 140.9 %shard_map.266 = (f32[224,448]{1,0:T(8,128)}, f32[224,1280]{1,0:T(8,128)}, f32[224,1792]{1,0:T(8,128)}, f32[256,1792]{1,0:T(8,128)}, f32[8,1792]{1,0:T(8,128)}, /*index=5*/f32[4,8,448]{2,1,0:T(8,128)}) custom-call(bf16[256,1792]{1,0:T(8,128)(2,1)} %x.7, f32[1,1792]{1,0:T(1,128)} %broadcast_in_dim.13.gain_one.gain, f32[1024,2]{1,0:T(8,128)} %stack.16.same, ...), custom_call_target="tpu_custom_call" | custom-call | tf_op jit(solution)/shard_map/pallas_call | solution.py:1413
  538.1 1.6 slice_reduce_fusion
  540.4 0.8 slice_bitcast_fusion
  541.3 0.7 reshape.53
  542.0 2.0 copy.44
  544.0 1.4 fusion.1
  545.4 0.1 fusion
  545.5 0.0 copy-done.5
  545.5 0.1 slice.138
  545.6 0.8 pad_maximum_fusion.5
  546.4 0.8 pad_maximum_fusion.4
  547.3 0.8 pad_maximum_fusion.3
  548.1 0.8 pad_maximum_fusion.2
  548.9 1.1 pad_maximum_fusion
  550.0 1.1 pad_maximum_fusion.1
  551.1 1.2 copy.48
  552.3 0.9 copy-done.4
  553.2 1.2 copy.49
  554.5 0.7 copy-done.6
  555.1 1.0 copy.50
  (40 shorter events, 0.1 us)
Async XLA Ops:
  0.6 6.7 %copy-start = (f32[3,1792]{1,0:T(4,128)S(1)}, f32[3,1792]{1,0:T(4,128)}, u32[]{:S(2)}) copy-start(f32[3,1792]{1,0:T(4,128)} %param.26) | copy-start | bytes 64516
  0.7 9.9 %slice-start.10 = ((bf16[224,448]{1,0:T(8,128)(2,1)}), bf16[224,64]{1,0:T(8,128)(2,1)S(1)}, s32[]{:S(2)}) async-start(bf16[224,448]{1,0:T(8,128)(2,1)} %param.24), calls=%async_computation.10 | async-start | bytes 114688 | tf_op jit(solution)/shard_map/slice | solution.py:1467
  0.7 9.9 %slice-start.11 = ((bf16[224,448]{1,0:T(8,128)(2,1)}), bf16[224,384]{1,0:T(8,128)(2,1)S(1)}, s32[]{:S(2)}) async-start(bf16[224,448]{1,0:T(8,128)(2,1)} %param.24), calls=%async_computation.11 | async-start | bytes 344064 | tf_op jit(solution)/shard_map/slice | solution.py:1467
  0.7 9.9 %slice-start.8 = ((bf16[224,448]{1,0:T(8,128)(2,1)}), bf16[224,64]{1,0:T(8,128)(2,1)S(1)}, s32[]{:S(2)}) async-start(bf16[224,448]{1,0:T(8,128)(2,1)} %param.23), calls=%async_computation.8 | async-start | bytes 114688 | tf_op jit(solution)/shard_map/slice | solution.py:1467
  0.7 9.9 %slice-start.9 = ((bf16[224,448]{1,0:T(8,128)(2,1)}), bf16[224,384]{1,0:T(8,128)(2,1)S(1)}, s32[]{:S(2)}) async-start(bf16[224,448]{1,0:T(8,128)(2,1)} %param.23), calls=%async_computation.9 | async-start | bytes 344064 | tf_op jit(solution)/shard_map/slice | solution.py:1467
  0.7 9.9 %slice-start.6 = ((bf16[224,448]{1,0:T(8,128)(2,1)}), bf16[224,64]{1,0:T(8,128)(2,1)S(1)}, s32[]{:S(2)}) async-start(bf16[224,448]{1,0:T(8,128)(2,1)} %param.22), calls=%async_computation.6 | async-start | bytes 114688 | tf_op jit(solution)/shard_map/slice | solution.py:1467
  0.7 9.9 %slice-start.7 = ((bf16[224,448]{1,0:T(8,128)(2,1)}), bf16[224,384]{1,0:T(8,128)(2,1)S(1)}, s32[]{:S(2)}) async-start(bf16[224,448]{1,0:T(8,128)(2,1)} %param.22), calls=%async_computation.7 | async-start | bytes 344064 | tf_op jit(solution)/shard_map/slice | solution.py:1467
  0.7 9.9 %slice-start.4 = ((bf16[224,448]{1,0:T(8,128)(2,1)}), bf16[224,64]{1,0:T(8,128)(2,1)S(1)}, s32[]{:S(2)}) async-start(bf16[224,448]{1,0:T(8,128)(2,1)} %param.21), calls=%async_computation.4 | async-start | bytes 114688 | tf_op jit(solution)/shard_map/slice | solution.py:1467
  0.7 9.9 %slice-start.5 = ((bf16[224,448]{1,0:T(8,128)(2,1)}), bf16[224,384]{1,0:T(8,128)(2,1)S(1)}, s32[]{:S(2)}) async-start(bf16[224,448]{1,0:T(8,128)(2,1)} %param.21), calls=%async_computation.5 | async-start | bytes 344064 | tf_op jit(solution)/shard_map/slice | solution.py:1467
  9.5 2.2 copy-start.8
  11.7 1.7 slice-start
  11.7 1.7 slice-start.1
  11.8 1.7 slice-start.2
  11.8 1.7 slice-start.3
  13.4 2.0 copy-start.9
  538.1 7.3 %copy-start.2 = (f32[224,1792]{1,0:T(8,128)S(1)}, f32[224,1792]{1,0:T(8,128)}, u32[]{:S(2)}) copy-start(f32[224,1792]{1,0:T(8,128)} %get-tuple-element.78) | copy-start | bytes 4816900
  544.0 1.6 copy-start.5
  545.6 3.3 copy-start.7
  548.9 2.2 copy-start.3
  551.1 2.2 copy-start.4
  553.2 1.9 copy-start.6
  553.2 2.9 copy-start.1

commit v4 on v3

--- a/solution.py
+++ b/solution.py
@@ -684,6 +684,32 @@
         dv[at_window, lanes] += back
 
 
+def rolled(values, offset):
+    turned = pltpu.roll(values, offset, axis=1)
+    lane = lax.broadcasted_iota(jnp.int32, values.shape, 1)
+    return jnp.where(lane < offset, pltpu.roll(turned, 1, axis=0), turned)
+
+
+def make_tables(segments, seg_q, seg_k, same):
+    values = segments[...]
+    row = lax.broadcasted_iota(jnp.int32, values.shape, 0)
+    lane = lax.broadcasted_iota(jnp.int32, values.shape, 1)
+    columns = values.T
+    matches = [
+        jnp.where((values == rolled(values, m)) & ((row > 0) | (lane >= m)), 1.0, 0.0).astype(jnp.float32).T
+        for m in range(1, CONV)
+    ]
+    crossing = rolled(values, TILE)
+    crossing = jnp.where((row == 0) & (lane < TILE), -1, crossing)
+    for n in range(values.shape[0]):
+        rows = pl.ds(n * LANES, LANES)
+        seg_q[rows] = columns[:, n : n + 1]
+        for m, match in enumerate(matches):
+            same[rows, m : m + 1] = match[:, n : n + 1]
+        seg_k[2 * n] = crossing[n : n + 1]
+        seg_k[2 * n + 1] = values[n : n + 1]
+
+
 def norm_rows(values, gain):
     scale = lax.rsqrt(jnp.mean(values * values, axis=1, keepdims=True) + EPS)
     return (values * scale * gain).astype(jnp.bfloat16)
@@ -706,26 +732,33 @@
     return run
 
 
-def mixer_forward_kernel(
-    x, valid, gain_one, gain_two, seg_q, seg_k, same, taps, mix_own, out_own, feed_own,
-    mix_out, last_out, feed, h1t_out, q_out, k_out, v_out, u_out, p_out, o_out, x1_out, h2_out, count_out,
-    mix, last, h1, h1t, h2, q, k_pad, v_pad, u, p, o, send, receive, total, count, count_in,
-    send_sems, recv_sems, local_sems, out_sems,
+def forward_kernel(
+    x, valid_lanes, gains, segments, taps,
+    mix_own, out_own, feed_own, down_own, cotangent_in, teacher_in,
+    mix_out, last_out, feed_out, down_out, h1t_out, h2t_out, dybt_out, q_out, k_out, v_out, u_out, p_out,
+    o_out, x1_out, dyb_out, slopes_out, active_out, act_out, dy_out, count_out, squares_out, same,
+    valid, seg_q, seg_k, mix, last, feed, down, h1, turned, h2, q, k_pad, v_pad, u, p, o, slopes, active, x1, side, teacher,
+    send, receive, total, count, count_in,
+    send_sems, recv_sems, local_sems, load_sems, out_sems,
 ):
     at = neighbours()
     sems = (send_sems, recv_sems)
     rows, shard = x.shape[0], mix_own.shape[0]
+    low = jnp.bfloat16
     greet(at, everyone=True)
 
     def slot_of(full):
         return lambda i, first, size: full.at[pl.ds(pl.multiple_of(i * shard + first, 16), size)]
 
-    early = RingGather(at, mix_own, slot_of(mix), sems, 0, local_sems.at[0])
-    middle = RingGather(at, out_own, slot_of(last), sems, 28, local_sems.at[1], count=1)
-    late = RingGather(at, feed_own, slot_of(feed), sems, 42, local_sems.at[2])
-    group_one = GatherTensor(at, h1, rows, sems, 70)
-    group_two = GatherTensor(at, h2, rows, sems, 73)
-    counting = SumAll(at, count, count_in, sems, 79)
+    mix_ring = RingGather(at, mix_own, slot_of(mix), sems, 0, local_sems.at[0])
+    last_ring = RingGather(at, out_own, slot_of(last), sems, 28, local_sems.at[1], count=1)
+    feed_ring = RingGather(at, feed_own, slot_of(feed), sems, 42, local_sems.at[2])
+    down_ring = RingGather(at, down_own, slot_of(down), sems, 70, local_sems.at[3])
+    dyb = h1
+    group_one = GatherTensor(at, h1, rows, sems, 98)
+    group_two = GatherTensor(at, h2, rows, sems, 101)
+    group_back = GatherTensor(at, dyb, rows, sems, 104)
+    counting = SumAll(at, count, count_in, sems, 113)
     local = q.shape[1]
     main = local // LANES * LANES
     tail = local - main
@@ -735,61 +768,83 @@
         copy = pltpu.make_async_copy(source, target, out_sems.at[len(keeps)])
         copy.start()
         keeps.append(copy)
-
-    early.start()
+        return copy
+
+    def tick():
+        last_ring.tick()
+        if feed_ring.at < len(feed_ring.receives):
+            feed_ring.tick()
+            if feed_ring.at == len(feed_ring.receives) - 2:
+                down_ring.start()
+        else:
+            down_ring.tick()
+
+    def turn(source, block):
+        here = pl.ds(pl.multiple_of(block * rows, rows), rows)
+        turned[:, here] = source[here].T
+
+    mix_ring.start()
 
     @chunks_of(rows)
     def _(row, size):
         h1[pl.ds(pl.multiple_of(at["t"] * rows + row, size), size)] = norm_rows(
-            x[pl.ds(row, size)].astype(jnp.float32), gain_one[...]
+            x[pl.ds(row, size)].astype(jnp.float32), gains[0:1]
         )
 
     group_one.start()
-    count[0] = jnp.full(count.shape[1:], jnp.sum(valid[...]), jnp.float32)
+    flags = valid_lanes[...].astype(jnp.float32)
+    count[0] = jnp.full(count.shape[1:], jnp.sum(flags), jnp.float32)
     counting.start()
+    load_teacher = pltpu.make_async_copy(teacher_in, teacher, load_sems.at[0])
+    load_cotangent = pltpu.make_async_copy(cotangent_in, side, load_sems.at[1])
+    load_teacher.start()
+    load_cotangent.start()
     k_pad[pl.ds(0, TILE)] = jnp.zeros((TILE, local), k_pad.dtype)
     v_pad[pl.ds(0, TILE)] = jnp.zeros((TILE, local), v_pad.dtype)
-    early.tick()
-    early.tick()
+    make_tables(segments, seg_q, seg_k, same)
+    spare = jnp.zeros((8 - flags.shape[0], LANES), jnp.float32)
+    columns = jnp.concatenate([flags, spare], axis=0).T
+    for n in range(flags.shape[0]):
+        valid[pl.ds(n * LANES, LANES)] = columns[:, n : n + 1]
+    mix_ring.tick()
+    mix_ring.tick()
     counting.step()
-    early.tick()
-    early.tick()
+    mix_ring.tick()
+    mix_ring.tick()
     counting.step()
-    early.tick()
+    mix_ring.tick()
     group_one.relay()
-    early.tick()
+    mix_ring.tick()
     counting.step()
-    early.tick()
-    early.tick()
+    mix_ring.tick()
+    mix_ring.tick()
     counting.step()
     group_one.finish()
-    early.tick()
+    mix_ring.tick()
 
     @pl.loop(0, 4)
     def _(j):
-        here = pl.multiple_of(j * rows, rows)
-        h1t[:, pl.ds(here, rows)] = h1[pl.ds(here, rows)].T
-
-    keep(h1t, h1t_out)
-    early.tick()
+        turn(h1, j)
+
+    keep_h1t = keep(turned, h1t_out)
+    mix_ring.tick()
     counting.finish()
     keep(count.at[5], count_out)
-    middle.start()
-    early.tick()
-    early.tick()
-    middle.tick()
-    late.start()
-    early.tick()
-    middle.tick()
-    early.finish()
-    middle.tick()
+    last_ring.start()
+    mix_ring.tick()
+    mix_ring.tick()
+    last_ring.tick()
+    feed_ring.start()
+    mix_ring.tick()
+    last_ring.tick()
+    mix_ring.finish()
+    last_ring.tick()
     keep(mix, mix_out)
 
     def project(j):
         here = pl.ds(pl.multiple_of(j * rows, rows), rows)
         there = pl.ds(pl.multiple_of(j * rows + TILE, TILE), rows)
         left = h1[here]
-        low = jnp.bfloat16
         pair = nn_dot(left, mix[:, pl.ds(0, 2 * main)]).astype(low)
         q[here, pl.ds(0, main)] = pair[:, :main]
         k_pad[there, pl.ds(0, main)] = pair[:, main:]
@@ -807,10 +862,6 @@
         def _(j):
             project(j)
 
-    def tick():
-        late.tick()
-        middle.tick()
-
     projects(0, 2)
     tick()
     projects(2, 4)
@@ -827,41 +878,116 @@
     for k in range(4):
         attend(k * tiles // 4, (k + 1) * tiles // 4)
         tick()
-    middle.finish()
+    last_ring.finish()
     keep(last, last_out)
     keep(p, p_out)
     keep(o, o_out)
 
-    def part(block):
+    def mixed_part(block):
         return nt_dot(o[pl.ds(pl.multiple_of(block * rows, rows), rows)], last[...])
 
     def idle(point):
-        late.tick()
+        tick()
         if point == 2:
-            late.tick()
-
-    sum_rows(at, part, send, receive, total, sems, 76, idle=idle)
+            tick()
+
+    sum_rows(at, mixed_part, send, receive, total, sems, 107, idle=idle)
 
     @chunks_of(rows)
     def _(row, size):
         here = pl.ds(row, size)
         hidden = total[here] + x[here].astype(jnp.float32)
-        total[here] = hidden
-        h2[pl.ds(pl.multiple_of(at["t"] * rows + row, size), size)] = norm_rows(hidden, gain_two[...])
+        x1[here] = hidden
+        h2[pl.ds(pl.multiple_of(at["t"] * rows + row, size), size)] = norm_rows(hidden, gains[1:2])
 
     group_two.start()
-    keep(total, x1_out)
+    keep(x1, x1_out)
     for _ in range(3):
-        late.tick()
+        tick()
     group_two.relay()
-    late.tick()
+    tick()
     group_two.finish()
-    keep(h2, h2_out)
-    late.finish()
-    for ring in (early, middle, late):
+    while feed_ring.at < len(feed_ring.receives):
+        tick()
+    feed_ring.finish()
+    keep(feed, feed_out)
+    width = active.shape[1]
+    parts, cut = feed_lanes(width)
+    rest = width - cut
+
+    def widen(j):
+        here = pl.ds(pl.multiple_of(j * rows, rows), rows)
+        left = h2[here]
+        for own, gate_lanes, up_lanes in parts:
+            a, by_gate, by_up = gated(nn_dot(left, feed[:, gate_lanes]), nn_dot(left, feed[:, up_lanes]))
+            active[here, own] = a.astype(low)
+            slopes[here, gate_lanes] = by_gate.astype(low)
+            slopes[here, up_lanes] = by_up.astype(low)
+        both = nn_dot(left, feed[:, pl.ds(2 * cut, 2 * rest)])
+        a, by_gate, by_up = gated(both[:, :rest], both[:, rest:])
+        active[here, pl.ds(cut, rest)] = a.astype(low)
+        slopes[here, pl.ds(2 * cut, 2 * rest)] = jnp.concatenate([by_gate, by_up], axis=1).astype(low)
+
+    for k in range(4):
+
+        @pl.loop(k, k + 1)
+        def _(j):
+            widen(j)
+
+        tick()
+    keep(active, active_out)
+    keep(slopes, slopes_out)
+    keep_h1t.wait()
+
+    @pl.loop(0, 4)
+    def _(j):
+        turn(h2, j)
+
+    keep_h2t = keep(turned, h2t_out)
+    tick()
+    down_ring.finish()
+    keep(down, down_out)
+    load_teacher.wait()
+    load_cotangent.wait()
+
+    def fed_part(block):
+        return nt_dot(active[pl.ds(pl.multiple_of(block * rows, rows), rows)], down[...])
+
+    sum_rows(at, fed_part, send, receive, total, sems, 110)
+    weight = (rows * 4 * 8) / count[5, 0:1, 0:1]
+    squares_out[...] = jnp.zeros_like(squares_out)
+
+    @chunks_of(rows, 32)
+    def _(row, size):
+        here = pl.ds(row, size)
+        result = total[here] + x1[here]
+        deviation = result - teacher[here].astype(jnp.float32)
+        kept = valid[here, 0:1] * deviation
+        total[here] = result
+        squares_out[0:1] += jnp.sum(kept * deviation, axis=0, keepdims=True)
+        grad = side[here] + kept * weight
+        side[here] = grad
+        dyb[pl.ds(pl.multiple_of(at["t"] * rows + row, size), size)] = grad.astype(low)
+
+    group_back.start()
+    keep(total, act_out)
+    keep(side, dy_out)
+    keep_h2t.wait()
+    turn(dyb, at["t"])
+    group_back.receives[0].wait_recv()
+    turn(dyb, at["core"])
+    group_back.relay()
+    turn(dyb, at["cross"])
+    group_back.receives[2].wait_recv()
+    turn(dyb, at["cross_core"])
+    group_back.drain()
+    keep(dyb, dyb_out)
+    keep(turned, dybt_out)
+    for ring in (mix_ring, last_ring, feed_ring, down_ring):
         ring.drain()
     for copy in keeps:
-        copy.wait()
+        if copy is not keep_h1t and copy is not keep_h2t:
+            copy.wait()
 
 
 def specs():
@@ -882,19 +1008,25 @@
     return pltpu.SemaphoreType.DMA((count,))
 
 
-def mixer_forward(x, valid, gain_one, gain_two, seg_q, seg_k, same, taps, mix_own, out_own, feed_own):
+def forward(
+    x, valid_lanes, gains, segments, taps, mix_own, out_own, feed_own, down_own, cotangent, teacher
+):
     rows, width = x.shape
     shard, local = out_own.shape
+    hidden = down_own.shape[1]
     everyone, depth = 4 * rows, 8 * shard
     low, wide = jnp.bfloat16, jnp.float32
     tiles, heads = everyone // TILE, local // HEAD_DIM
     vmem, hbm = specs()
     return pl.pallas_call(
-        mixer_forward_kernel,
+        forward_kernel,
         out_shape=(
-            shape(depth, mix_own.shape[1]),
+            shape(depth, 4 * local),
             shape(depth, local),
-            shape(depth, feed_own.shape[1]),
+            shape(depth, 2 * hidden),
+            shape(depth, hidden),
+            shape(width, everyone),
+            shape(width, everyone),
             shape(width, everyone),
             shape(everyone, local),
             shape(everyone + TILE, local),
@@ -904,13 +1036,24 @@
             shape(everyone, local),
             shape(rows, width, kind=wide),
             shape(everyone, width),
+            shape(everyone, 2 * hidden),
+            shape(everyone, hidden),
+            shape(rows, width, kind=wide),
+            shape(rows, width, kind=wide),
             shape(8, LANES, kind=wide),
+            shape(8, width, kind=wide),
+            shape(everyone, CONV - 1, kind=wide),
         ),
-        in_specs=[vmem] * 8 + [hbm] * 3,
-        out_specs=(hbm,) * 13,
+        in_specs=[vmem] * 5 + [hbm] * 6,
+        out_specs=(hbm,) * 20 + (vmem,) * 2,
         scratch_shapes=[
-            pltpu.VMEM((depth, mix_own.shape[1]), low),
+            pltpu.VMEM((rows, 1), wide),
+            pltpu.VMEM((everyone, 1), jnp.int32),
+            pltpu.VMEM((tiles, 1, 2 * TILE), jnp.int32),
+            pltpu.VMEM((depth, 4 * local), low),
             pltpu.VMEM((depth, local), low),
+            pltpu.VMEM((depth, 2 * hidden), low),
+            pltpu.VMEM((depth, hidden), low),
             pltpu.VMEM((everyone, width), low),
             pltpu.VMEM((width, everyone), low),
             pltpu.VMEM((everyone, width), low),
@@ -920,18 +1063,26 @@
             pltpu.VMEM((everyone, local), low),
             pltpu.VMEM((tiles, heads * TILE, 2 * TILE), low),
             pltpu.VMEM((everyone, local), low),
+            pltpu.VMEM((everyone, 2 * hidden), low),
+            pltpu.VMEM((everyone, hidden), low),
+            pltpu.VMEM((rows, width), wide),
+            pltpu.VMEM((rows, width), wide),
+            pltpu.VMEM((rows, width), low),
             pltpu.VMEM((3, rows, width), low),
             pltpu.VMEM((3, rows, width), low),
             pltpu.VMEM((rows, width), wide),
             pltpu.VMEM((6, 8, LANES), wide),
             pltpu.VMEM((5, 8, LANES), wide),
-            dma(84),
-            dma(84),
-            dma(3),
-            dma(12),
+            dma(118),
+            dma(118),
+            dma(4),
+            dma(2),
+            dma(20),
         ],
         compiler_params=params(1),
-    )(x, valid, gain_one, gain_two, seg_q, seg_k, same, taps, mix_own, out_own, feed_own)
+    )(
+        x, valid_lanes, gains, segments, taps, mix_own, out_own, feed_own, down_own, cotangent, teacher
+    )
 
 
 def feed_lanes(hidden):
@@ -947,167 +1098,8 @@
     return silu * up, up * sigmoid * (1.0 + gate * (1.0 - sigmoid)), silu
 
 
-def feed_forward_kernel(
-    valid, count, h2_in, feed_in, x1_in, cotangent_in, teacher_in, down_own,
-    down_out, slopes_out, active_out, act_out, dy_out, dyb_out, dybt_out, h2t_out, squares_out,
-    h2, feed, down, slopes, active, x1, cotangent, teacher, dyb, turned, send, receive, total,
-    send_sems, recv_sems, local_sems, load_sems, out_sems,
-):
-    at = neighbours()
-    sems = (send_sems, recv_sems)
-    rows, shard = x1.shape[0], down_own.shape[0]
-    low = jnp.bfloat16
-    greet(at)
-    ring = RingGather(
-        at, down_own, lambda i, first, size: down.at[pl.ds(pl.multiple_of(i * shard + first, 16), size)],
-        sems, 0, local_sems.at[0],
-    )
-    group = GatherTensor(at, dyb, rows, sems, 31)
-    loads = [
-        pltpu.make_async_copy(source, target, load_sems.at[n])
-        for n, (source, target) in enumerate(
-            ((h2_in, h2), (feed_in, feed), (x1_in, x1), (cotangent_in, cotangent), (teacher_in, teacher))
-        )
-    ]
-    keeps = []
-
-    def keep(source, target):
-        copy = pltpu.make_async_copy(source, target, out_sems.at[len(keeps)])
-        copy.start()
-        keeps.append(copy)
-
-    ring.start()
-    for load in loads:
-        load.start()
-    hidden = active.shape[1]
-    parts, main = feed_lanes(hidden)
-    tail = hidden - main
-    loads[0].wait()
-    loads[1].wait()
-
-    def widen(first, last):
-        @pl.loop(first, last)
-        def _(j):
-            here = pl.ds(pl.multiple_of(j * rows, rows), rows)
-            left = h2[here]
-            for own, gate_lanes, up_lanes in parts:
-                a, by_gate, by_up = gated(nn_dot(left, feed[:, gate_lanes]), nn_dot(left, feed[:, up_lanes]))
-                active[here, own] = a.astype(low)
-                slopes[here, gate_lanes] = by_gate.astype(low)
-                slopes[here, up_lanes] = by_up.astype(low)
-            both = nn_dot(left, feed[:, pl.ds(2 * main, 2 * tail)])
-            a, by_gate, by_up = gated(both[:, :tail], both[:, tail:])
-            active[here, pl.ds(main, tail)] = a.astype(low)
-            slopes[here, pl.ds(2 * main, 2 * tail)] = jnp.concatenate([by_gate, by_up], axis=1).astype(low)
-
-    ring.tick()
-    for k in range(4):
-        widen(k, k + 1)
-        ring.tick()
-    keep(active, active_out)
-    keep(slopes, slopes_out)
-    ring.tick()
-
-    def turn(source, block):
-        here = pl.multiple_of(block * rows, rows)
-        turned[:, pl.ds(here, rows)] = source[pl.ds(here, rows)].T
-
-    @pl.loop(0, 4)
-    def _(j):
-        turn(h2, j)
-
-    keep(turned, h2t_out)
-    ring.finish()
-    keep(down, down_out)
-    for load in loads[2:]:
-        load.wait()
-
-    def part(block):
-        return nt_dot(active[pl.ds(pl.multiple_of(block * rows, rows), rows)], down[...])
-
-    sum_rows(at, part, send, receive, total, sems, 28)
-    weight = (rows * 4 * 8) / count[0:1, 0:1]
-    squares_out[...] = jnp.zeros_like(squares_out)
-
-    @chunks_of(rows, 32)
-    def _(row, size):
-        here = pl.ds(row, size)
-        result = total[here] + x1[here]
-        deviation = result - teacher[here].astype(jnp.float32)
-        kept = valid[here, 0:1] * deviation
-        total[here] = result
-        squares_out[0:1] += jnp.sum(kept * deviation, axis=0, keepdims=True)
-        grad = cotangent[here] + kept * weight
-        x1[here] = grad
-        dyb[pl.ds(pl.multiple_of(at["t"] * rows + row, size), size)] = grad.astype(low)
-
-    group.start()
-    keep(total, act_out)
-    keep(x1, dy_out)
-    keeps[2].wait()
-    turn(dyb, at["t"])
-    group.receives[0].wait_recv()
-    turn(dyb, at["core"])
-    group.relay()
-    turn(dyb, at["cross"])
-    group.receives[2].wait_recv()
-    turn(dyb, at["cross_core"])
-    group.drain()
-    keep(dyb, dyb_out)
-    keep(turned, dybt_out)
-    ring.drain()
-    for n, copy in enumerate(keeps):
-        if n != 2:
-            copy.wait()
-
-
-def feed_forward(valid, count, h2, feed, x1, cotangent, teacher, down_own):
-    rows, width = x1.shape
-    shard, hidden = down_own.shape
-    everyone, depth = 4 * rows, 8 * shard
-    low, wide = jnp.bfloat16, jnp.float32
-    vmem, hbm = specs()
-    return pl.pallas_call(
-        feed_forward_kernel,
-        out_shape=(
-            shape(depth, hidden),
-            shape(everyone, 2 * hidden),
-            shape(everyone, hidden),
-            shape(rows, width, kind=wide),
-            shape(rows, width, kind=wide),
-            shape(everyone, width),
-            shape(width, everyone),
-            shape(width, everyone),
-            shape(8, width, kind=wide),
-        ),
-        in_specs=[vmem] * 2 + [hbm] * 6,
-        out_specs=(hbm,) * 8 + (vmem,),
-        scratch_shapes=[
-            pltpu.VMEM((everyone, width), low),
-            pltpu.VMEM((depth, 2 * hidden), low),
-            pltpu.VMEM((depth, hidden), low),
-            pltpu.VMEM((everyone, 2 * hidden), low),
-            pltpu.VMEM((everyone, hidden), low),
-            pltpu.VMEM((rows, width), wide),
-            pltpu.VMEM((rows, width), wide),
-            pltpu.VMEM((rows, width), low),
-            pltpu.VMEM((everyone, width), low),
-            pltpu.VMEM((width, everyone), low),
-            pltpu.VMEM((3, rows, width), low),
-            pltpu.VMEM((3, rows, width), low),
-            pltpu.VMEM((rows, width), wide),
-            dma(34),
-            dma(34),
-            dma(1),
-            dma(5),
-            dma(8),
-        ],
-        compiler_params=params(2),
-    )(valid, count, h2, feed, x1, cotangent, teacher, down_own)
-
-
 def feed_backward_kernel(
-    gain, dyb_in, dybt_in, h2t_in, down_in, feed_in, active_in, slopes_in, last_in, x1_in, dy_in,
+    gains, dyb_in, dybt_in, h2t_in, down_in, feed_in, active_in, slopes_in, last_in, x1_in, dy_in,
     down_grad, gate_grad, gain_part, dx1_out, dx1t_out, do_out, slopes_out,
     dyb, dybt, h2t, down, feed, active, slopes, last, do, side, total, down_slots, gate_slots,
     down_term, gate_term, send, receive,
@@ -1126,7 +1118,7 @@
             )
         )
     ]
-    for load in loads[:-1]:
+    for load in loads[:2]:
         load.start()
     greet(at)
     hidden = active.shape[1]
@@ -1146,6 +1138,8 @@
 
     loads[0].wait()
     loads[1].wait()
+    for load in loads[2:-1]:
+        load.start()
     first.start()
     for load in loads[2:5]:
         load.wait()
@@ -1189,7 +1183,7 @@
     @chunks_of(rows, 32)
     def _(row, size):
         here = pl.ds(row, size)
-        through, term_gain = norm_back(side[here], total[here], gain[...])
+        through, term_gain = norm_back(side[here], total[here], gains[1:2])
         gain_part[0:1] += term_gain
         total[here] = through
 
@@ -1236,7 +1230,7 @@
         copy.wait()
 
 
-def feed_backward(gain, dyb, dybt, h2t, down, feed, active, slopes, last, x1, dy):
+def feed_backward(gains, dyb, dybt, h2t, down, feed, active, slopes, last, x1, dy):
     rows, width = x1.shape
     depth, hidden = down.shape
     local = last.shape[1]
@@ -1281,11 +1275,11 @@
             dma(4),
         ],
         compiler_params=params(3),
-    )(gain, dyb, dybt, h2t, down, feed, active, slopes, last, x1, dy)
+    )(gains, dyb, dybt, h2t, down, feed, active, slopes, last, x1, dy)
 
 
 def mixer_backward_kernel(
-    x, gain, same, taps, gain_part, squares,
+    x, gains, same, taps, gain_part, squares,
     dx1t_in, o_in, h2t_in, slopes_in, q_in, k_in, v_in, u_in, p_in, do_in, mix_in, h1t_in, dx1_in,
     out_grad, up_grad, mix_grad, input_grad, small_out, conv_out,
     turned, o, h2t, slopes, q, k_pad, v_pad, u, p, do, mix,
@@ -1307,7 +1301,7 @@
             )
         )
     ]
-    for load in loads[:-1]:
+    for load in loads[:4]:
         load.start()
     greet(at, everyone=True)
     local = q.shape[1]
@@ -1323,6 +1317,8 @@
     first.start()
     loads[2].wait()
     loads[3].wait()
+    for load in loads[4:-1]:
+        load.start()
     second.start()
     dk[...] = jnp.zeros_like(dk)
     dv[...] = jnp.zeros_like(dv)
@@ -1338,11 +1334,15 @@
         def _(i):
             attend_back_tile(i, q, k_pad, v_pad, u, p, same, taps, do, dk, dv, conv_sum)
 
-    for k in range(4):
-        attend(k * tiles // 4, (k + 1) * tiles // 4)
+    for k in range(8):
+        attend(k * tiles // 8, (k + 1) * tiles // 8)
         first.tick()
         second.tick()
     conv_all.start()
+
+    first.finish()
+    loads[12].start()
+    second.tick()
 
     @chunks_of(q.shape[0])
     def _(row, size):
@@ -1353,14 +1353,11 @@
         ends = jnp.concatenate([value[:, main:] for value in four], axis=1)
         grads[here, pl.ds(4 * main, 4 * tail)] = ends.astype(low)
 
-    first.finish()
-    loads[12].start()
-    second.tick()
     second.tick()
     loads[12].wait()
+    third.start()
     loads[10].wait()
     loads[11].wait()
-    third.start()
 
     def part(block):
         return nt_dot(grads[pl.ds(pl.multiple_of(block * rows, rows), rows)], mix[...])
@@ -1381,7 +1378,7 @@
     @chunks_of(rows, 32)
     def _(row, size):
         here = pl.ds(row, size)
-        through, term_gain = norm_back(x[here].astype(jnp.float32), total[here], gain[...])
+        through, term_gain = norm_back(x[here].astype(jnp.float32), total[here], gains[0:1])
         small[0, 0:1] += term_gain
         input_grad[here] += through
 
@@ -1402,7 +1399,7 @@
 
 
 def mixer_backward(
-    x, gain, same, taps, gain_part, squares, dx1t, o, h2t, slopes, q, k_pad, v_pad, u, p, do, mix, h1t, dx1
+    x, gains, same, taps, gain_part, squares, dx1t, o, h2t, slopes, q, k_pad, v_pad, u, p, do, mix, h1t, dx1
 ):
     rows, width = x.shape
     everyone, local = o.shape
@@ -1445,42 +1442,71 @@
             dma(13),
         ],
         compiler_params=params(4),
-    )(x, gain, same, taps, gain_part, squares, *arrays, h1t, dx1)
-
-
-def segment_tables(segments):
-    padded = jnp.concatenate([jnp.full((TILE,), -1, jnp.int32), segments])
-    seg_k = jnp.concatenate(
-        [padded[:-TILE].reshape(-1, 1, TILE), padded[TILE:].reshape(-1, 1, TILE)], axis=2
-    )
-    same = [
-        jnp.concatenate(
-            [jnp.zeros((m,), jnp.float32), (segments[m:] == segments[:-m]).astype(jnp.float32)]
-        )
-        for m in range(1, CONV)
-    ]
-    return segments[:, None], seg_k, jnp.stack(same, axis=1)
+    )(x, gains, same, taps, gain_part, squares, *arrays, h1t, dx1)
+
+
+def finish_kernel(
+    count, down_grad, gate_main, up_rest, mix_grad, out_grad, small, conv, act_in, input_in,
+    loss, act, input_grad, query, key, value, mixgate, output, conv_grad, gain_one, gain_two, gate, up, down,
+):
+    act[...] = act_in[...]
+    input_grad[...] = input_in[...]
+    local = query.shape[1]
+    main = local // LANES * LANES
+    tail = local - main
+    for n, target in enumerate((query, key, value, mixgate)):
+        target[:, pl.ds(0, main)] = mix_grad[:, pl.ds(n * main, main)]
+        target[:, pl.ds(main, tail)] = mix_grad[:, pl.ds(4 * main, 4 * tail)][:, n * tail : (n + 1) * tail]
+    cut = gate_main.shape[1]
+    rest = gate.shape[1] - cut
+    ends = up_rest[:, pl.ds(cut, 2 * rest)]
+    gate[:, pl.ds(0, cut)] = gate_main[...]
+    gate[:, pl.ds(cut, rest)] = ends[:, :rest]
+    up[:, pl.ds(0, cut)] = up_rest[:, pl.ds(0, cut)]
+    up[:, pl.ds(cut, rest)] = ends[:, rest:]
+    output[...] = out_grad[...].T
+    down[...] = down_grad[...].T
+    conv_grad[...] = jnp.concatenate([conv[n, 0:CONV] for n in range(conv.shape[0])], axis=1)
+    gain_one[...] = small[0]
+    gain_two[...] = small[1]
+    total = jnp.sum(small[2:3], axis=1, keepdims=True) / (count[0:1, 0:1] * D)
+    loss[...] = jnp.broadcast_to(total, loss.shape)
+
+
+def finish(count, down_grad, gate_main, up_rest, mix_grad, out_grad, small, conv, act, input_grad):
+    vmem, _ = specs()
+    wide = jnp.float32
+    shard, hidden = down_grad.shape
+    local, width = out_grad.shape[1], small.shape[1]
+    square = shape(shard, local, kind=wide)
+    broad = shape(shard, hidden, kind=wide)
+    return pl.pallas_call(
+        finish_kernel,
+        out_shape=(
+            shape(8, LANES, kind=wide),
+            shape(*act.shape, kind=wide),
+            shape(*input_grad.shape, kind=wide),
+            square,
+            square,
+            square,
+            square,
+            shape(local, shard, kind=wide),
+            shape(CONV, width, kind=wide),
+            shape(width, kind=wide),
+            shape(width, kind=wide),
+            broad,
+            broad,
+            shape(hidden, shard, kind=wide),
+        ),
+        in_specs=[vmem] * 10,
+        out_specs=(vmem,) * 14,
+        compiler_params=pltpu.CompilerParams(vmem_limit_bytes=VMEM_LIMIT),
+    )(count, down_grad, gate_main, up_rest, mix_grad, out_grad, small, conv, act, input_grad)
 
 
 def pack(*weights):
     main = weights[0].shape[1] // LANES * LANES
     return jnp.concatenate([w[:, :main] for w in weights] + [w[:, main:] for w in weights], axis=1)
-
-
-def unpack(packed, count):
-    width = packed.shape[1] // count
-    main = width // LANES * LANES
-    tail = width - main
-    return [
-        jnp.concatenate(
-            [
-                packed[:, n * main : (n + 1) * main],
-                packed[:, count * main + n * tail : count * main + (n + 1) * tail],
-            ],
-            axis=1,
-        )
-        for n in range(count)
-    ]
 
 
 def on_rings(
@@ -1503,43 +1529,26 @@
 ):
     local = query_weight.shape[1]
     taps = lax.dynamic_slice_in_dim(conv_weight, lax.axis_index("tensor") * local, local, 1)
-    seg_q, seg_k, same = segment_tables(segments)
-    valid = valid_mask.astype(jnp.float32)
-    mix_own = pack(query_weight, key_weight, value_weight, mixgate_weight)
-    feed_own = pack(gate_weight, up_weight)
-    gain_one, gain_two = gain_mixer[None], gain_feed[None]
-    mix, last, feed, h1t, q, k_pad, v_pad, u, p, o, x1, h2, count = mixer_forward(
-        block_input, valid.reshape(-1, LANES), gain_one, gain_two, seg_q, seg_k, same, taps,
-        mix_own, output_weight.T, feed_own,
-    )
-    down, slopes, active, outputs, dy, dyb, dybt, h2t, squares = feed_forward(
-        valid[:, None], count, h2, feed, x1, cotangent, teacher, down_weight.T
+    gains = jnp.stack([gain_mixer, gain_feed])
+    (
+        mix, last, feed, down, h1t, h2t, dybt, q, k_pad, v_pad, u, p, o, x1, dyb, slopes, active,
+        outputs, dy, count, squares, same,
+    ) = forward(
+        block_input, valid_mask.reshape(-1, LANES), gains, segments.reshape(-1, LANES), taps,
+        pack(query_weight, key_weight, value_weight, mixgate_weight), output_weight.T,
+        pack(gate_weight, up_weight), down_weight.T, cotangent, teacher,
     )
     down_grad, gate_main, gain_part, dx1, dx1t, do, slopes_up = feed_backward(
-        gain_two, dyb, dybt, h2t, down, feed, active, slopes, last, x1, dy
+        gains, dyb, dybt, h2t, down, feed, active, slopes, last, x1, dy
     )
     out_grad, up_rest, mix_grad, input_grad, small, conv = mixer_backward(
-        block_input, gain_one, same, taps, gain_part, squares, dx1t, o, h2t, slopes_up, q, k_pad, v_pad,
+        block_input, gains, same, taps, gain_part, squares, dx1t, o, h2t, slopes_up, q, k_pad, v_pad,
         u, p, do, mix, h1t, dx1,
     )
-    main = gate_main.shape[1]
-    tail = gate_weight.shape[1] - main
-    gate_grad = jnp.concatenate([gate_main, up_rest[:, main : main + tail]], axis=1)
-    up_grad = jnp.concatenate([up_rest[:, :main], up_rest[:, main + tail :]], axis=1)
-    mean_loss = jnp.sum(small[2]) / (count[0, 0] * D)
-    return (
-        mean_loss,
-        outputs,
-        input_grad,
-        *unpack(mix_grad, 4),
-        out_grad.T,
-        conv[:, :CONV].transpose(1, 0, 2).reshape(CONV, -1),
-        small[0],
-        small[1],
-        gate_grad,
-        up_grad,
-        down_grad.T,
-    )
+    loss, *rest = finish(
+        count, down_grad, gate_main, up_rest, mix_grad, out_grad, small, conv, outputs, input_grad
+    )
+    return (loss[0, 0], *rest)
 
 
 def on_any_mesh(

time: 565 us -> 534 us (0.945)
  local copies, waits for them, and re-layouts: 22.4 us -> 10 us
  other arithmetic: 11.7 us -> 0.61 us
    concatenate x8 -> x0, other arithmetic: 6.18 us -> none  [the longest x4 3.26 us: unpack(): jnp.concatenate([packed[:, n * main:(n + 1) * main], packed[:, count * ma...]
where the time goes in v4:
time: 534 us; the launch traced here: 527 us
  Pallas kernels  515 us (96%)
  local copies, waits for them, and re-layouts  10 us (2%)
    pallas_call x1, Pallas kernels, forward(): pl.pallas_call(forward_kernel, out_shape=(shape(depth, 4 * local), shape(...  274 us
    pallas_call x1, Pallas kernels, mixer_backward(): pl.pallas_call(mixer_backward_kernel, out_shape=(shape(shard, local, kind...  140 us
    pallas_call x1, Pallas kernels, feed_backward(): pl.pallas_call(feed_backward_kernel, out_shape=(shape(shard, hidden, kind...  93 us

profile of v4, /device:TPU:0, one launch (start us, length us, event | category | flops | bytes accessed | tf_op | source)
XLA Modules:
  0.0 527.1 jit_solution(6602166864316545528)
XLA Ops:
  0.6 0.0 copy-start
  0.7 0.0 slice-start.10
  0.7 0.0 slice-start.11
  0.7 0.0 slice-start.8
  0.7 0.0 slice-start.9
  0.7 0.0 slice-start.6
  0.7 0.0 slice-start.7
  0.7 0.0 slice-start.4
  0.7 0.0 slice-start.5
  0.8 0.8 stack.9
  1.6 0.7 stack.10
  2.3 0.6 pad_maximum_fusion.gains
  2.9 0.0 copy-done
  2.9 0.7 constant_dynamic-slice_fusion.taps
  3.6 0.0 copy-start.2
  3.6 0.0 slice-done.10
  3.6 0.0 slice-done.11
  3.6 0.0 slice-done.8
  3.6 0.0 slice-done.9
  3.6 0.0 slice-done.6
  3.6 0.0 slice-done.7
  3.6 0.0 slice-done.4
  3.6 0.0 slice-done.5
  3.6 0.0 slice-start
  3.7 0.0 slice-start.1
  3.7 0.0 slice-start.2
  3.7 0.0 slice-start.3
  3.7 1.1 concatenate.6.mix_own
  4.8 0.0 copy-done.2
  4.8 0.8 copy.30
  5.6 0.0 slice-done
  5.6 0.0 slice-done.1
  5.6 0.0 slice-done.2
  5.6 0.0 slice-done.3
  5.6 1.9 concatenate.7.feed_own
  7.5 273.9 %shard_map.263 = (bf16[1792,1792]{1,0:T(8,128)(2,1)}, bf16[1792,448]{1,0:T(8,128)(2,1)}, bf16[1792,2432]{1,0:T(8,128)(2,1)}, bf16[1792,1216]{1,0:T(8,128)(2,1)},...) custom-call(bf16[256,1792]{1,0:T(8,128)(2,1)} %x.3, ...), custom_call_target="tpu_custom_call" | custom-call | tf_op jit(solution)/shard_map/pallas_call | solution.py:1021
  281.5 93.0 %shard_map.264 = (f32[224,1216]{1,0:T(8,128)}, f32[224,1152]{1,0:T(8,128)}, f32[8,1792]{1,0:T(8,128)}, f32[256,1792]{1,0:T(8,128)}, bf16[1792,1024]{1,0:T(8,128)...) custom-call(f32[2,1792]{1,0:T(2,128)} %pad_maximum_fusion.gains, ...), custom_call_target="tpu_custom_call" | custom-call | tf_op jit(solution)/shard_map/pallas_call | solution.py:1241
  374.5 140.4 %shard_map.265 = (f32[224,448]{1,0:T(8,128)}, f32[224,1280]{1,0:T(8,128)}, f32[224,1792]{1,0:T(8,128)}, f32[256,1792]{1,0:T(8,128)}, f32[8,1792]{1,0:T(8,128)}, /*index=5*/f32[4,8,448]{2,1,0:T(8,128)}) custom-call(bf16[256,1792]{1,0:T(8,128)(2,1)} %x.3, f32[2,1792]{1,0:T(2,128)} %pad_maximum_fusion.gains, f32[1024,2]{1,0:T(8,128)} %get-tuple-element.76.same, ...), custom_call_target="tpu_custom_call" | custom-call | tf_op jit(solution)/shard_map/pallas_call | solution.py:1410
  514.8 0.0 copy-start.1
  514.8 7.9 %shard_map.266 = (f32[8,128]{1,0:T(8,128)}, f32[256,1792]{1,0:T(8,128)}, f32[256,1792]{1,0:T(8,128)}, f32[224,448]{1,0:T(8,128)}, f32[224,448]{1,0:T(8,128)}, /*...) custom-call(f32[8,128]{1,0:T(8,128)} %get-tuple-element.63.count, ...), custom_call_target="tpu_custom_call" | custom-call | tf_op jit(solution)/shard_map/pallas_call | solution.py:1483
  522.8 1.2 slice.51
  524.0 2.7 copy.31
  526.7 0.0 copy-done.1
Async XLA Ops:
  0.6 2.3 copy-start
  0.7 2.9 slice-start.10
  0.7 2.9 slice-start.11
  0.7 2.9 slice-start.8
  0.7 2.9 slice-start.9
  0.7 2.9 slice-start.6
  0.7 2.9 slice-start.7
  0.7 2.9 slice-start.4
  0.7 2.9 slice-start.5
  3.6 1.2 copy-start.2
  3.6 2.0 slice-start
  3.7 2.0 slice-start.1
  3.7 1.9 slice-start.2
  3.7 1.9 slice-start.3
  514.8 11.8 %copy-start.1 = (f32[3,1792]{1,0:T(4,128)S(1)}, f32[3,1792]{1,0:T(4,128)}, u32[]{:S(2)}) copy-start(f32[3,1792]{1,0:T(4,128)} %param.26) | copy-start | bytes 64516

commit v5 on v4

--- a/solution.py
+++ b/solution.py
@@ -310,6 +310,7 @@
 
 TILE = 64
 LANES = 128
+PIECES = 4
 
 
 def neighbours():
@@ -545,6 +546,79 @@
     second.wait_recv()
     total[...] += receive[1].astype(jnp.float32)
     for copy in (first, second, third):
+        copy.wait_send()
+
+
+class GatherPieces:
+    def __init__(self, at, full, rows, count, sems, base):
+        size = rows // count
+        to_core, to_cross = (at["d"], at["core"]), (at["d"], at["cross"])
+
+        def place(block, c):
+            return full.at[pl.ds(pl.multiple_of(block * rows + c * size, size), size)]
+
+        def copies(k, block, to):
+            return [
+                remote(place(block, c), place(block, c), sems, base + k * count + c, to)
+                for c in range(count)
+            ]
+
+        self.to_core = copies(0, at["t"], to_core)
+        self.to_cross = copies(1, at["t"], to_cross)
+        self.relay_core = copies(2, at["cross"], to_core)
+        self.receives = [
+            copies(k, block, to_core) for k, block in enumerate((at["core"], at["cross"], at["cross_core"]))
+        ]
+
+    def start(self, c):
+        self.to_cross[c].start()
+        self.to_core[c].start()
+
+    def relay(self):
+        for receive, send in zip(self.receives[1], self.relay_core):
+            receive.wait_recv()
+            send.start()
+
+    def wait(self, k):
+        for receive in self.receives[k]:
+            receive.wait_recv()
+
+    def drain(self):
+        for send in self.to_core + self.to_cross + self.relay_core:
+            send.wait_send()
+
+
+def sum_pieces(at, block_part, send, receive, total, sems, base, count, done):
+    to_core, to_cross = (at["d"], at["core"]), (at["d"], at["cross"])
+    low = jnp.bfloat16
+    size = total.shape[0] // count
+    pieces = [pl.ds(c * size, size) for c in range(count)]
+
+    def copies(k, to):
+        return [
+            remote(send.at[k, piece], receive.at[k, piece], sems, base + k * count + c, to)
+            for c, piece in enumerate(pieces)
+        ]
+
+    first, second, third = copies(0, to_core), copies(1, to_cross), copies(2, to_core)
+    send[0] = block_part(at["cross_core"]).astype(low)
+    for copy in first:
+        copy.start()
+    total[...] = block_part(at["cross"])
+    for c, piece in enumerate(pieces):
+        first[c].wait_recv()
+        send[1, piece] = (total[piece] + receive[0, piece].astype(jnp.float32)).astype(low)
+        second[c].start()
+    send[2] = block_part(at["core"]).astype(low)
+    for copy in third:
+        copy.start()
+    total[...] = block_part(at["t"])
+    for c, piece in enumerate(pieces):
+        third[c].wait_recv()
+        second[c].wait_recv()
+        total[piece] += receive[2, piece].astype(jnp.float32) + receive[1, piece].astype(jnp.float32)
+        done(c)
+    for copy in first + second + third:
         copy.wait_send()
 
 
@@ -710,6 +784,10 @@
         seg_k[2 * n + 1] = values[n : n + 1]
 
 
+def row_of(gain):
+    return gain[...].reshape(1, -1)
+
+
 def norm_rows(values, gain):
     scale = lax.rsqrt(jnp.mean(values * values, axis=1, keepdims=True) + EPS)
     return (values * scale * gain).astype(jnp.bfloat16)
@@ -733,11 +811,11 @@
 
 
 def forward_kernel(
-    x, valid_lanes, gains, segments, taps,
-    mix_own, out_own, feed_own, down_own, cotangent_in, teacher_in,
+    x, valid_lanes, gain_one, gain_two, segments, taps,
+    gate_own, up_own, mix_own, out_own, down_own, cotangent_in, teacher_in,
     mix_out, last_out, feed_out, down_out, h1t_out, h2t_out, dybt_out, q_out, k_out, v_out, u_out, p_out,
     o_out, x1_out, dyb_out, slopes_out, active_out, act_out, dy_out, count_out, squares_out, same,
-    valid, seg_q, seg_k, mix, last, feed, down, h1, turned, h2, q, k_pad, v_pad, u, p, o, slopes, active, x1, side, teacher,
+    valid, seg_q, seg_k, feed_own, mix, last, feed, down, h1, turned, h2, q, k_pad, v_pad, u, p, o, slopes, active, x1, side, teacher,
     send, receive, total, count, count_in,
     send_sems, recv_sems, local_sems, load_sems, out_sems,
 ):
@@ -753,12 +831,14 @@
     mix_ring = RingGather(at, mix_own, slot_of(mix), sems, 0, local_sems.at[0])
     last_ring = RingGather(at, out_own, slot_of(last), sems, 28, local_sems.at[1], count=1)
     feed_ring = RingGather(at, feed_own, slot_of(feed), sems, 42, local_sems.at[2])
-    down_ring = RingGather(at, down_own, slot_of(down), sems, 70, local_sems.at[3])
+    down_ring = RingGather(
+        at, down_own.at[:, pl.ds(0, down.shape[1])], slot_of(down), sems, 70, local_sems.at[3]
+    )
     dyb = h1
     group_one = GatherTensor(at, h1, rows, sems, 98)
     group_two = GatherTensor(at, h2, rows, sems, 101)
-    group_back = GatherTensor(at, dyb, rows, sems, 104)
-    counting = SumAll(at, count, count_in, sems, 113)
+    group_back = GatherPieces(at, dyb, rows, PIECES, sems, 115)
+    counting = SumAll(at, count, count_in, sems, 110)
     local = q.shape[1]
     main = local // LANES * LANES
     tail = local - main
@@ -788,7 +868,7 @@
     @chunks_of(rows)
     def _(row, size):
         h1[pl.ds(pl.multiple_of(at["t"] * rows + row, size), size)] = norm_rows(
-            x[pl.ds(row, size)].astype(jnp.float32), gains[0:1]
+            x[pl.ds(row, size)].astype(jnp.float32), row_of(gain_one)
         )
 
     group_one.start()
@@ -802,36 +882,33 @@
     k_pad[pl.ds(0, TILE)] = jnp.zeros((TILE, local), k_pad.dtype)
     v_pad[pl.ds(0, TILE)] = jnp.zeros((TILE, local), v_pad.dtype)
     make_tables(segments, seg_q, seg_k, same)
+    width = gate_own.shape[1]
+    cut = width // LANES * LANES
+    rest = width - cut
+    feed_own[:, pl.ds(0, cut)] = gate_own[:, pl.ds(0, cut)]
+    feed_own[:, pl.ds(cut, cut)] = up_own[:, pl.ds(0, cut)]
+    ends = [own[:, pl.ds(cut, rest)].astype(jnp.float32) for own in (gate_own, up_own)]
+    feed_own[:, pl.ds(2 * cut, 2 * rest)] = jnp.concatenate(ends, axis=1).astype(low)
     spare = jnp.zeros((8 - flags.shape[0], LANES), jnp.float32)
     columns = jnp.concatenate([flags, spare], axis=0).T
     for n in range(flags.shape[0]):
         valid[pl.ds(n * LANES, LANES)] = columns[:, n : n + 1]
+    for _ in range(6):
+        mix_ring.tick()
+    group_one.relay()
     mix_ring.tick()
     mix_ring.tick()
-    counting.step()
-    mix_ring.tick()
-    mix_ring.tick()
-    counting.step()
-    mix_ring.tick()
-    group_one.relay()
-    mix_ring.tick()
-    counting.step()
-    mix_ring.tick()
-    mix_ring.tick()
-    counting.step()
     group_one.finish()
     mix_ring.tick()
-
-    @pl.loop(0, 4)
-    def _(j):
-        turn(h1, j)
-
+    for k in range(2):
+
+        @pl.loop(2 * k, 2 * k + 2)
+        def _(j):
+            turn(h1, j)
+
+        mix_ring.tick()
     keep_h1t = keep(turned, h1t_out)
-    mix_ring.tick()
-    counting.finish()
-    keep(count.at[5], count_out)
     last_ring.start()
-    mix_ring.tick()
     mix_ring.tick()
     last_ring.tick()
     feed_ring.start()
@@ -864,6 +941,7 @@
 
     projects(0, 2)
     tick()
+    counting.step()
     projects(2, 4)
     for source, target in ((q, q_out), (k_pad, k_out), (v_pad, v_out), (u, u_out)):
         keep(source, target)
@@ -878,13 +956,15 @@
     for k in range(4):
         attend(k * tiles // 4, (k + 1) * tiles // 4)
         tick()
+        if k % 2:
+            counting.step()
     last_ring.finish()
     keep(last, last_out)
     keep(p, p_out)
     keep(o, o_out)
 
     def mixed_part(block):
-        return nt_dot(o[pl.ds(pl.multiple_of(block * rows, rows), rows)], last[...])
+        return nt_dot(o[pl.ds(pl.multiple_of(block * rows, rows), rows)], last[:, pl.ds(0, local)])
 
     def idle(point):
         tick()
@@ -898,25 +978,27 @@
         here = pl.ds(row, size)
         hidden = total[here] + x[here].astype(jnp.float32)
         x1[here] = hidden
-        h2[pl.ds(pl.multiple_of(at["t"] * rows + row, size), size)] = norm_rows(hidden, gains[1:2])
+        h2[pl.ds(pl.multiple_of(at["t"] * rows + row, size), size)] = norm_rows(hidden, row_of(gain_two))
 
     group_two.start()
     keep(x1, x1_out)
     for _ in range(3):
         tick()
+    counting.step()
+    tick()
     group_two.relay()
     tick()
+    counting.finish()
+    keep(count.at[5], count_out)
     group_two.finish()
     while feed_ring.at < len(feed_ring.receives):
         tick()
     feed_ring.finish()
     keep(feed, feed_out)
-    width = active.shape[1]
-    parts, cut = feed_lanes(width)
-    rest = width - cut
+    parts, _ = feed_lanes(width)
 
     def widen(j):
-        here = pl.ds(pl.multiple_of(j * rows, rows), rows)
+        here = pl.ds(pl.multiple_of(j * (rows // 2), rows // 2), rows // 2)
         left = h2[here]
         for own, gate_lanes, up_lanes in parts:
             a, by_gate, by_up = gated(nn_dot(left, feed[:, gate_lanes]), nn_dot(left, feed[:, up_lanes]))
@@ -928,7 +1010,7 @@
         active[here, pl.ds(cut, rest)] = a.astype(low)
         slopes[here, pl.ds(2 * cut, 2 * rest)] = jnp.concatenate([by_gate, by_up], axis=1).astype(low)
 
-    for k in range(4):
+    for k in range(8):
 
         @pl.loop(k, k + 1)
         def _(j):
@@ -938,51 +1020,63 @@
     keep(active, active_out)
     keep(slopes, slopes_out)
     keep_h1t.wait()
-
-    @pl.loop(0, 4)
-    def _(j):
-        turn(h2, j)
-
+    for k in range(4):
+
+        @pl.loop(k, k + 1)
+        def _(j):
+            turn(h2, j)
+
+        tick()
     keep_h2t = keep(turned, h2t_out)
-    tick()
     down_ring.finish()
     keep(down, down_out)
     load_teacher.wait()
     load_cotangent.wait()
 
     def fed_part(block):
-        return nt_dot(active[pl.ds(pl.multiple_of(block * rows, rows), rows)], down[...])
-
-    sum_rows(at, fed_part, send, receive, total, sems, 110)
+        here = pl.ds(pl.multiple_of(block * rows, rows), rows)
+        ends = nt_dot(active[here, pl.ds(cut, rest)], last[:, pl.ds(local, rest)])
+        return ends + nt_dot(active[here, pl.ds(0, cut)], down[...])
+
     weight = (rows * 4 * 8) / count[5, 0:1, 0:1]
     squares_out[...] = jnp.zeros_like(squares_out)
-
-    @chunks_of(rows, 32)
-    def _(row, size):
-        here = pl.ds(row, size)
-        result = total[here] + x1[here]
-        deviation = result - teacher[here].astype(jnp.float32)
-        kept = valid[here, 0:1] * deviation
-        total[here] = result
-        squares_out[0:1] += jnp.sum(kept * deviation, axis=0, keepdims=True)
-        grad = side[here] + kept * weight
-        side[here] = grad
-        dyb[pl.ds(pl.multiple_of(at["t"] * rows + row, size), size)] = grad.astype(low)
-
-    group_back.start()
+    piece, step = rows // PIECES, 32
+
+    def judge(c):
+        @pl.loop(0, piece // step)
+        def _(i):
+            row = pl.multiple_of(c * piece + i * step, step)
+            here = pl.ds(row, step)
+            result = total[here] + x1[here]
+            deviation = result - teacher[here].astype(jnp.float32)
+            kept = valid[here, 0:1] * deviation
+            total[here] = result
+            squares_out[0:1] += jnp.sum(kept * deviation, axis=0, keepdims=True)
+            grad = side[here] + kept * weight
+            side[here] = grad
+            dyb[pl.ds(pl.multiple_of(at["t"] * rows + row, step), step)] = grad.astype(low)
+
+        group_back.start(c)
+
+    sum_pieces(at, fed_part, send, receive, total, sems, 115 + 3 * PIECES, PIECES, judge)
     keep(total, act_out)
     keep(side, dy_out)
     keep_h2t.wait()
-    turn(dyb, at["t"])
-    group_back.receives[0].wait_recv()
-    turn(dyb, at["core"])
+
+    def spread(block):
+        here = pl.ds(pl.multiple_of(block * rows, rows), rows)
+        turn(dyb, block)
+        keep(dyb.at[here], dyb_out.at[here])
+        keep(turned.at[:, here], dybt_out.at[:, here])
+
+    spread(at["t"])
+    group_back.wait(0)
+    spread(at["core"])
     group_back.relay()
-    turn(dyb, at["cross"])
-    group_back.receives[2].wait_recv()
-    turn(dyb, at["cross_core"])
+    spread(at["cross"])
+    group_back.wait(2)
+    spread(at["cross_core"])
     group_back.drain()
-    keep(dyb, dyb_out)
-    keep(turned, dybt_out)
     for ring in (mix_ring, last_ring, feed_ring, down_ring):
         ring.drain()
     for copy in keeps:
@@ -1009,11 +1103,13 @@
 
 
 def forward(
-    x, valid_lanes, gains, segments, taps, mix_own, out_own, feed_own, down_own, cotangent, teacher
+    x, valid_lanes, gain_one, gain_two, segments, taps, mix_own, out_own, gate_own, up_own, down_own, cotangent,
+    teacher,
 ):
     rows, width = x.shape
-    shard, local = out_own.shape
-    hidden = down_own.shape[1]
+    shard = out_own.shape[0]
+    local, hidden = mix_own.shape[1] // 4, gate_own.shape[1]
+    cut = hidden // LANES * LANES
     everyone, depth = 4 * rows, 8 * shard
     low, wide = jnp.bfloat16, jnp.float32
     tiles, heads = everyone // TILE, local // HEAD_DIM
@@ -1022,9 +1118,9 @@
         forward_kernel,
         out_shape=(
             shape(depth, 4 * local),
-            shape(depth, local),
+            shape(depth, out_own.shape[1]),
             shape(depth, 2 * hidden),
-            shape(depth, hidden),
+            shape(depth, cut),
             shape(width, everyone),
             shape(width, everyone),
             shape(width, everyone),
@@ -1044,16 +1140,17 @@
             shape(8, width, kind=wide),
             shape(everyone, CONV - 1, kind=wide),
         ),
-        in_specs=[vmem] * 5 + [hbm] * 6,
+        in_specs=[vmem] * 8 + [hbm] * 5,
         out_specs=(hbm,) * 20 + (vmem,) * 2,
         scratch_shapes=[
             pltpu.VMEM((rows, 1), wide),
             pltpu.VMEM((everyone, 1), jnp.int32),
             pltpu.VMEM((tiles, 1, 2 * TILE), jnp.int32),
+            pltpu.VMEM((shard, 2 * hidden), low),
             pltpu.VMEM((depth, 4 * local), low),
-            pltpu.VMEM((depth, local), low),
+            pltpu.VMEM((depth, out_own.shape[1]), low),
             pltpu.VMEM((depth, 2 * hidden), low),
-            pltpu.VMEM((depth, hidden), low),
+            pltpu.VMEM((depth, cut), low),
             pltpu.VMEM((everyone, width), low),
             pltpu.VMEM((width, everyone), low),
             pltpu.VMEM((everyone, width), low),
@@ -1073,15 +1170,16 @@
             pltpu.VMEM((rows, width), wide),
             pltpu.VMEM((6, 8, LANES), wide),
             pltpu.VMEM((5, 8, LANES), wide),
-            dma(118),
-            dma(118),
+            dma(115 + 6 * PIECES),
+            dma(115 + 6 * PIECES),
             dma(4),
             dma(2),
-            dma(20),
+            dma(26),
         ],
         compiler_params=params(1),
     )(
-        x, valid_lanes, gains, segments, taps, mix_own, out_own, feed_own, down_own, cotangent, teacher
+        x, valid_lanes, gain_one, gain_two, segments, taps, gate_own, up_own, mix_own, out_own, down_own,
+        cotangent, teacher,
     )
 
 
@@ -1099,7 +1197,7 @@
 
 
 def feed_backward_kernel(
-    gains, dyb_in, dybt_in, h2t_in, down_in, feed_in, active_in, slopes_in, last_in, x1_in, dy_in,
+    gain, dyb_in, dybt_in, h2t_in, down_in, feed_in, active_in, slopes_in, last_in, x1_in, dy_in,
     down_grad, gate_grad, gain_part, dx1_out, dx1t_out, do_out, slopes_out,
     dyb, dybt, h2t, down, feed, active, slopes, last, do, side, total, down_slots, gate_slots,
     down_term, gate_term, send, receive,
@@ -1114,7 +1212,7 @@
         for n, (source, target) in enumerate(
             (
                 (dybt_in, dybt), (active_in, active), (dyb_in, dyb), (down_in, down), (slopes_in, slopes),
-                (h2t_in, h2t), (feed_in, feed), (last_in, last), (x1_in, side), (dy_in, side),
+                (last_in, last), (h2t_in, h2t), (feed_in, feed), (x1_in, side), (dy_in, side),
             )
         )
     ]
@@ -1141,7 +1239,7 @@
     for load in loads[2:-1]:
         load.start()
     first.start()
-    for load in loads[2:5]:
+    for load in loads[2:6]:
         load.wait()
 
     def slope_back(first_block, last_block):
@@ -1153,7 +1251,7 @@
                 da = nn_dot(left, down[:, own])
                 slopes[here, gate_lanes] = (da * slopes[here, gate_lanes].astype(jnp.float32)).astype(low)
                 slopes[here, up_lanes] = (da * slopes[here, up_lanes].astype(jnp.float32)).astype(low)
-            da = nn_dot(left, down[:, pl.ds(main, tail)])
+            da = nn_dot(left, last[:, pl.ds(last.shape[1] - tail, tail)])
             ends = pl.ds(2 * main, 2 * tail)
             both = jnp.concatenate([da, da], axis=1) * slopes[here, ends].astype(jnp.float32)
             slopes[here, ends] = both.astype(low)
@@ -1162,9 +1260,9 @@
         slope_back(k, k + 1)
         first.tick()
     keep(slopes.at[:, pl.ds(main, 2 * hidden - main)], slopes_out)
-    loads[5].wait()
+    loads[6].wait()
     second.start()
-    loads[6].wait()
+    loads[7].wait()
     loads[8].wait()
 
     def part(block):
@@ -1183,7 +1281,7 @@
     @chunks_of(rows, 32)
     def _(row, size):
         here = pl.ds(row, size)
-        through, term_gain = norm_back(side[here], total[here], gains[1:2])
+        through, term_gain = norm_back(side[here], total[here], row_of(gain))
         gain_part[0:1] += term_gain
         total[here] = through
 
@@ -1201,12 +1299,11 @@
 
     group.start()
     keep(total, dx1_out)
-    loads[7].wait()
 
     def spread(block):
         here = pl.ds(pl.multiple_of(block * rows, rows), rows)
         dybt[:, here] = dyb[here].T
-        do[here] = nn_dot(dyb[here], last[...]).astype(low)
+        do[here] = nn_dot(dyb[here], last[:, pl.ds(0, do.shape[1])]).astype(low)
 
     while first.at < len(first.sends):
         first.tick()
@@ -1230,11 +1327,11 @@
         copy.wait()
 
 
-def feed_backward(gains, dyb, dybt, h2t, down, feed, active, slopes, last, x1, dy):
+def feed_backward(gain, dyb, dybt, h2t, down, feed, active, slopes, last, x1, dy):
     rows, width = x1.shape
-    depth, hidden = down.shape
-    local = last.shape[1]
-    main = hidden // LANES * LANES
+    depth, main = down.shape
+    hidden = active.shape[1]
+    local = last.shape[1] - (hidden - main)
     everyone, shard = 4 * rows, depth // 8
     low, wide = jnp.bfloat16, jnp.float32
     vmem, hbm = specs()
@@ -1255,11 +1352,11 @@
             pltpu.VMEM((everyone, width), low),
             pltpu.VMEM((width, everyone), low),
             pltpu.VMEM((width, everyone), low),
-            pltpu.VMEM((depth, hidden), low),
+            pltpu.VMEM((depth, main), low),
             pltpu.VMEM((depth, 2 * hidden), low),
             pltpu.VMEM((everyone, hidden), low),
             pltpu.VMEM((everyone, 2 * hidden), low),
-            pltpu.VMEM((depth, local), low),
+            pltpu.VMEM(last.shape, low),
             pltpu.VMEM((everyone, local), low),
             pltpu.VMEM((rows, width), wide),
             pltpu.VMEM((rows, width), wide),
@@ -1275,11 +1372,11 @@
             dma(4),
         ],
         compiler_params=params(3),
-    )(gains, dyb, dybt, h2t, down, feed, active, slopes, last, x1, dy)
+    )(gain, dyb, dybt, h2t, down, feed, active, slopes, last, x1, dy)
 
 
 def mixer_backward_kernel(
-    x, gains, same, taps, gain_part, squares,
+    x, gain, same, taps, gain_part, squares,
     dx1t_in, o_in, h2t_in, slopes_in, q_in, k_in, v_in, u_in, p_in, do_in, mix_in, h1t_in, dx1_in,
     out_grad, up_grad, mix_grad, input_grad, small_out, conv_out,
     turned, o, h2t, slopes, q, k_pad, v_pad, u, p, do, mix,
@@ -1378,28 +1475,27 @@
     @chunks_of(rows, 32)
     def _(row, size):
         here = pl.ds(row, size)
-        through, term_gain = norm_back(x[here].astype(jnp.float32), total[here], gains[0:1])
+        through, term_gain = norm_back(x[here].astype(jnp.float32), total[here], row_of(gain))
         small[0, 0:1] += term_gain
         input_grad[here] += through
 
     small_sum.start()
-    for k in range(4):
-        second.tick()
+    second.finish()
+    for k in range(5):
         third.tick()
-        conv_all.step()
-        second.tick()
+        if k > 0:
+            conv_all.step()
         third.tick()
         small_sum.step()
+    third.finish()
     small_sum.finish()
     conv_all.finish()
-    second.finish()
-    third.finish()
     small_out[...] = small[5]
     conv_out[...] = conv[5]
 
 
 def mixer_backward(
-    x, gains, same, taps, gain_part, squares, dx1t, o, h2t, slopes, q, k_pad, v_pad, u, p, do, mix, h1t, dx1
+    x, gain, same, taps, gain_part, squares, dx1t, o, h2t, slopes, q, k_pad, v_pad, u, p, do, mix, h1t, dx1
 ):
     rows, width = x.shape
     everyone, local = o.shape
@@ -1442,7 +1538,7 @@
             dma(13),
         ],
         compiler_params=params(4),
-    )(x, gains, same, taps, gain_part, squares, *arrays, h1t, dx1)
+    )(x, gain, same, taps, gain_part, squares, *arrays, h1t, dx1)
 
 
 def finish_kernel(
@@ -1465,12 +1561,12 @@
     up[:, pl.ds(0, cut)] = up_rest[:, pl.ds(0, cut)]
     up[:, pl.ds(cut, rest)] = ends[:, rest:]
     output[...] = out_grad[...].T
-    down[...] = down_grad[...].T
+    down[...] = down_grad[...]
     conv_grad[...] = jnp.concatenate([conv[n, 0:CONV] for n in range(conv.shape[0])], axis=1)
     gain_one[...] = small[0]
     gain_two[...] = small[1]
     total = jnp.sum(small[2:3], axis=1, keepdims=True) / (count[0:1, 0:1] * D)
-    loss[...] = jnp.broadcast_to(total, loss.shape)
+    loss[...] = total
 
 
 def finish(count, down_grad, gate_main, up_rest, mix_grad, out_grad, small, conv, act, input_grad):
@@ -1483,7 +1579,7 @@
     return pl.pallas_call(
         finish_kernel,
         out_shape=(
-            shape(8, LANES, kind=wide),
+            shape(1, 1, kind=wide),
             shape(*act.shape, kind=wide),
             shape(*input_grad.shape, kind=wide),
             square,
@@ -1496,7 +1592,7 @@
             shape(width, kind=wide),
             broad,
             broad,
-            shape(hidden, shard, kind=wide),
+            broad,
         ),
         in_specs=[vmem] * 10,
         out_specs=(vmem,) * 14,
@@ -1529,26 +1625,28 @@
 ):
     local = query_weight.shape[1]
     taps = lax.dynamic_slice_in_dim(conv_weight, lax.axis_index("tensor") * local, local, 1)
-    gains = jnp.stack([gain_mixer, gain_feed])
+    cut = down_weight.shape[0] // LANES * LANES
+    down_own = down_weight.T
     (
         mix, last, feed, down, h1t, h2t, dybt, q, k_pad, v_pad, u, p, o, x1, dyb, slopes, active,
         outputs, dy, count, squares, same,
     ) = forward(
-        block_input, valid_mask.reshape(-1, LANES), gains, segments.reshape(-1, LANES), taps,
-        pack(query_weight, key_weight, value_weight, mixgate_weight), output_weight.T,
-        pack(gate_weight, up_weight), down_weight.T, cotangent, teacher,
+        block_input, valid_mask.reshape(-1, LANES), gain_mixer, gain_feed, segments.reshape(-1, LANES), taps,
+        pack(query_weight, key_weight, value_weight, mixgate_weight),
+        jnp.concatenate([output_weight.T, down_own[:, cut:]], axis=1), gate_weight, up_weight, down_own,
+        cotangent, teacher,
     )
     down_grad, gate_main, gain_part, dx1, dx1t, do, slopes_up = feed_backward(
-        gains, dyb, dybt, h2t, down, feed, active, slopes, last, x1, dy
+        gain_feed, dyb, dybt, h2t, down, feed, active, slopes, last, x1, dy
     )
     out_grad, up_rest, mix_grad, input_grad, small, conv = mixer_backward(
-        block_input, gains, same, taps, gain_part, squares, dx1t, o, h2t, slopes_up, q, k_pad, v_pad,
+        block_input, gain_mixer, same, taps, gain_part, squares, dx1t, o, h2t, slopes_up, q, k_pad, v_pad,
         u, p, do, mix, h1t, dx1,
     )
-    loss, *rest = finish(
+    loss, *rest, down_turned = finish(
         count, down_grad, gate_main, up_rest, mix_grad, out_grad, small, conv, outputs, input_grad
     )
-    return (loss[0, 0], *rest)
+    return (loss.reshape(()), *rest, down_turned.T)
 
 
 def on_any_mesh(

time: 534 us -> 512 us (0.959)
  Pallas kernels: 515 us -> 500 us
  local copies, waits for them, and re-layouts: 10 us -> 3.46 us
    pallas_call x1, Pallas kernels: 274 us -> 261 us  [forward(): pl.pallas_call(forward_kernel, out_shape=(shape(depth, 4 * local), shape(...]
where the time goes in v5:
time: 512 us; the launch traced here: 505 us
  Pallas kernels  500 us (98%)
    pallas_call x1, Pallas kernels, forward(): pl.pallas_call(forward_kernel, out_shape=(shape(depth, 4 * local), shape(...  261 us
    pallas_call x1, Pallas kernels, mixer_backward(): pl.pallas_call(mixer_backward_kernel, out_shape=(shape(shard, local, kind...  139 us
    pallas_call x1, Pallas kernels, feed_backward(): pl.pallas_call(feed_backward_kernel, out_shape=(shape(shard, hidden, kind...  92.9 us

profile of v5, /device:TPU:0, one launch (start us, length us, event | category | flops | bytes accessed | tf_op | source)
XLA Modules:
  0.0 505.2 jit_solution(213426363491793951)
XLA Ops:
  0.6 0.0 copy-start
  0.7 0.0 slice-start.6
  0.7 0.0 slice-start.7
  0.7 0.0 slice-start.4
  0.7 0.0 slice-start.5
  0.7 0.0 slice-start.2
  0.7 0.0 slice-start.3
  0.7 0.0 slice-start
  0.7 0.0 slice-start.1
  0.8 0.7 copy-done
  1.4 0.7 constant_dynamic-slice_fusion.taps
  2.1 0.0 copy-start.2
  2.1 0.9 slice.36
  2.9 0.0 slice-done.6
  2.9 0.0 slice-done.7
  2.9 0.0 slice-done.4
  3.0 0.0 slice-done.5
  3.0 0.0 slice-done.2
  3.0 0.0 slice-done.3
  3.0 0.0 slice-done
  3.0 0.0 slice-done.1
  3.0 1.1 concatenate.6.mix_own
  4.1 0.0 copy-done.2
  4.1 0.1 copy.30
  4.2 0.8 pad_maximum_fusion.out_own
  5.0 260.6 %shard_map.263 = (bf16[1792,1792]{1,0:T(8,128)(2,1)}, bf16[1792,512]{1,0:T(8,128)(2,1)}, bf16[1792,2432]{1,0:T(8,128)(2,1)}, bf16[1792,1152]{1,0:T(8,128)(2,1)},...) custom-call(bf16[256,1792]{1,0:T(8,128)(2,1)} %x.3, ...), custom_call_target="tpu_custom_call" | custom-call | tf_op jit(solution)/shard_map/pallas_call | solution.py:1117
  265.7 92.9 %shard_map.264 = (f32[224,1216]{1,0:T(8,128)}, f32[224,1152]{1,0:T(8,128)}, f32[8,1792]{1,0:T(8,128)}, f32[256,1792]{1,0:T(8,128)}, bf16[1792,1024]{1,0:T(8,128)...) custom-call(f32[1792]{0:T(1024)} %gain.2, bf16[1024,1792]{1,0:T(8,128)(2,1)} %get-tuple-element.64.dyb_in, ...), custom_call_target="tpu_custom_call" | custom-call | tf_op jit(solution)/shard_map/pallas_call | solution.py:1338
  358.6 138.8 %shard_map.265 = (f32[224,448]{1,0:T(8,128)}, f32[224,1280]{1,0:T(8,128)}, f32[224,1792]{1,0:T(8,128)}, f32[256,1792]{1,0:T(8,128)}, f32[8,1792]{1,0:T(8,128)}, /*index=5*/f32[4,8,448]{2,1,0:T(8,128)}) custom-call(bf16[256,1792]{1,0:T(8,128)(2,1)} %x.3, f32[1792]{0:T(1024)} %gain.3, f32[1024,2]{1,0:T(8,128)} %get-tuple-element.76.same, ...), custom_call_target="tpu_custom_call" | custom-call | tf_op jit(solution)/shard_map/pallas_call | solution.py:1506
  497.4 0.0 copy-start.1
  497.4 7.6 %shard_map.266 = (f32[1,1]{1,0:T(1,128)}, f32[256,1792]{1,0:T(8,128)}, f32[256,1792]{1,0:T(8,128)}, f32[224,448]{1,0:T(8,128)}, f32[224,448]{1,0:T(8,128)}, /*in...) custom-call(f32[8,128]{1,0:T(8,128)} %get-tuple-element.63.count, ...), custom_call_target="tpu_custom_call" | custom-call | tf_op jit(solution)/shard_map/pallas_call | solution.py:1579
  504.9 0.0 copy-done.1
Async XLA Ops:
  0.6 0.8 copy-start
  0.7 2.3 slice-start.6
  0.7 2.3 slice-start.7
  0.7 2.3 slice-start.4
  0.7 2.3 slice-start.5
  0.7 2.3 slice-start.2
  0.7 2.3 slice-start.3
  0.7 2.3 slice-start
  0.7 2.3 slice-start.1
  2.1 2.0 copy-start.2
  497.4 7.6 %copy-start.1 = (f32[3,1792]{1,0:T(4,128)S(1)}, f32[3,1792]{1,0:T(4,128)}, u32[]{:S(2)}) copy-start(f32[3,1792]{1,0:T(4,128)} %param.26) | copy-start | bytes 64516

commit v6 on v5

--- a/solution.py
+++ b/solution.py
@@ -311,6 +311,7 @@
 TILE = 64
 LANES = 128
 PIECES = 4
+SHARE = 2
 
 
 def neighbours():
@@ -337,15 +338,20 @@
     )
 
 
-def greet(at, everyone=False):
+def hail(at, everyone=False):
     d, t = at["d"], at["t"]
     devices = [(at["ring"](1), t), (at["ring"](-1), t), (d, at["core"]), (d, at["cross"])]
     if everyone:
         devices += [(at["mate"], t), (at["z_pair"], t), (at["z_mirror"], t)]
-    barrier = pltpu.get_barrier_semaphore()
     for device in devices:
-        pl.semaphore_signal(barrier, inc=1, device_id=device, device_id_type=MESH)
-    pl.semaphore_wait(barrier, len(devices))
+        pl.semaphore_signal(
+            pltpu.get_barrier_semaphore(), inc=1, device_id=device, device_id_type=MESH
+        )
+    return len(devices)
+
+
+def meet(number):
+    pl.semaphore_wait(pltpu.get_barrier_semaphore(), number)
 
 
 def remote(source, target, sems, index, device):
@@ -413,8 +419,8 @@
 
 
 class RingScatter:
-    def __init__(self, at, left, right, slots, term, out, sems, base, count=2):
-        self.ring, self.left, self.right = at["ring"], left, right
+    def __init__(self, at, left, right, slots, term, out, sems, base, count=2, side=None):
+        self.ring, self.left, self.right, self.side = at["ring"], left, right, side
         self.slots, self.term, self.out = slots, term, out
         self.half, self.columns = slots.shape[2], slots.shape[3]
         self.pieces = pieces_of(self.half, count)
@@ -437,6 +443,15 @@
         half = self.half
         first = pl.multiple_of(self.ring(-away) * 2 * half, half)
         second = pl.multiple_of(self.ring(away) * 2 * half + half, half)
+        if self.side is not None:
+            left, beside = [
+                jnp.concatenate([ref[pl.ds(first, half)], ref[pl.ds(second, half)]], axis=0)
+                for ref in (self.left, self.side)
+            ]
+            self.term[...] = jnp.concatenate(
+                [nn_dot(left, self.right[...]), beside.astype(jnp.float32)], axis=1
+            )
+            return
         width = 512
         whole = self.columns // width * width
 
@@ -453,14 +468,19 @@
         if whole < self.columns:
             block(pl.ds(whole, self.columns - whole))
 
+    def prepare(self):
+        self.compute(1)
+        for way in range(2):
+            self.slots[way, 0] = self.term[pl.ds(way * self.half, self.half)].astype(jnp.bfloat16)
+
+    def launch(self):
+        for k in range(len(self.pieces)):
+            for way in range(2):
+                self.sends[k][way].start()
+
     def start(self):
-        self.compute(1)
-        for k, (first, size) in enumerate(self.pieces):
-            for way in range(2):
-                self.slots[way, 0, pl.ds(first, size)] = self.term[
-                    pl.ds(way * self.half + first, size)
-                ].astype(jnp.bfloat16)
-                self.sends[k][way].start()
+        self.prepare()
+        self.launch()
         self.compute(2)
 
     def tick(self):
@@ -588,7 +608,9 @@
             send.wait_send()
 
 
-def sum_pieces(at, block_part, send, receive, total, sems, base, count, done):
+def sum_pieces(
+    at, block_part, send, receive, total, sems, base, count, done, idle=lambda: None
+):
     to_core, to_cross = (at["d"], at["core"]), (at["d"], at["cross"])
     low = jnp.bfloat16
     size = total.shape[0] // count
@@ -609,11 +631,13 @@
         first[c].wait_recv()
         send[1, piece] = (total[piece] + receive[0, piece].astype(jnp.float32)).astype(low)
         second[c].start()
+    idle()
     send[2] = block_part(at["core"]).astype(low)
     for copy in third:
         copy.start()
     total[...] = block_part(at["t"])
     for c, piece in enumerate(pieces):
+        idle()
         third[c].wait_recv()
         second[c].wait_recv()
         total[piece] += receive[2, piece].astype(jnp.float32) + receive[1, piece].astype(jnp.float32)
@@ -623,13 +647,15 @@
 
 
 class SumAll:
-    def __init__(self, at, value, received, sems, base):
+    def __init__(self, at, value, received, sems, base, over=("core", "cross", "mate", "z_pair", "z_mirror")):
         d, t = at["d"], at["t"]
-        partners = ((d, at["core"]), (d, at["cross"]), (at["mate"], t), (at["z_pair"], t), (at["z_mirror"], t))
         self.value, self.received, self.s = value, received, 0
         self.copies = [
-            remote(value.at[k], received.at[k], sems, base + k, partner)
-            for k, partner in enumerate(partners)
+            remote(
+                value.at[k], received.at[k], sems, base + k,
+                (d, at[name]) if name in ("core", "cross") else (at[name], t),
+            )
+            for k, name in enumerate(over)
         ]
 
     def start(self):
@@ -637,14 +663,16 @@
 
     def step(self):
         s = self.s
+        if s == len(self.copies):
+            return
         self.copies[s].wait_recv()
         self.value[s + 1] = self.value[s] + self.received[s]
-        if s < 4:
+        if s + 1 < len(self.copies):
             self.copies[s + 1].start()
         self.s += 1
 
     def finish(self):
-        while self.s < 5:
+        while self.s < len(self.copies):
             self.step()
         for copy in self.copies:
             copy.wait_send()
@@ -750,7 +778,7 @@
         back = tn_dot(chance_low, grad_heads)
         zero = jnp.zeros_like(grad_conv)
         for m, same_m in enumerate((None, same_one, same_two)):
-            conv_sum[m : m + 1, lanes] += jnp.sum(grad_conv * rows[m], axis=0, keepdims=True)
+            conv_sum[m, :, lanes] += jnp.sum(grad_conv * rows[m], axis=0, keepdims=True)
             term = taps[m : m + 1, lanes] * grad_conv
             term = term if m == 0 else term * same_m
             term = jnp.concatenate([zero, term], axis=0)
@@ -812,10 +840,10 @@
 
 def forward_kernel(
     x, valid_lanes, gain_one, gain_two, segments, taps,
-    gate_own, up_own, mix_own, out_own, down_own, cotangent_in, teacher_in,
+    gate_own, up_own, out_turned, down_own, mix_own, cotangent_in, teacher_in,
     mix_out, last_out, feed_out, down_out, h1t_out, h2t_out, dybt_out, q_out, k_out, v_out, u_out, p_out,
     o_out, x1_out, dyb_out, slopes_out, active_out, act_out, dy_out, count_out, squares_out, same,
-    valid, seg_q, seg_k, feed_own, mix, last, feed, down, h1, turned, h2, q, k_pad, v_pad, u, p, o, slopes, active, x1, side, teacher,
+    valid, seg_q, seg_k, feed_own, out_own, mix, last, feed, down, h1, turned, h2, q, k_pad, v_pad, u, p, o, slopes, active, x1, side, teacher,
     send, receive, total, count, count_in,
     send_sems, recv_sems, local_sems, load_sems, out_sems,
 ):
@@ -823,7 +851,7 @@
     sems = (send_sems, recv_sems)
     rows, shard = x.shape[0], mix_own.shape[0]
     low = jnp.bfloat16
-    greet(at, everyone=True)
+    meet(hail(at, everyone=True))
 
     def slot_of(full):
         return lambda i, first, size: full.at[pl.ds(pl.multiple_of(i * shard + first, 16), size)]
@@ -889,6 +917,8 @@
     feed_own[:, pl.ds(cut, cut)] = up_own[:, pl.ds(0, cut)]
     ends = [own[:, pl.ds(cut, rest)].astype(jnp.float32) for own in (gate_own, up_own)]
     feed_own[:, pl.ds(2 * cut, 2 * rest)] = jnp.concatenate(ends, axis=1).astype(low)
+    ends = [out_turned[...].astype(jnp.float32).T, down_own[:, pl.ds(cut, rest)].astype(jnp.float32)]
+    out_own[...] = jnp.concatenate(ends, axis=1).astype(low)
     spare = jnp.zeros((8 - flags.shape[0], LANES), jnp.float32)
     columns = jnp.concatenate([flags, spare], axis=0).T
     for n in range(flags.shape[0]):
@@ -1103,13 +1133,14 @@
 
 
 def forward(
-    x, valid_lanes, gain_one, gain_two, segments, taps, mix_own, out_own, gate_own, up_own, down_own, cotangent,
-    teacher,
+    x, valid_lanes, gain_one, gain_two, segments, taps, mix_own, output_weight, gate_own, up_own, down_own,
+    cotangent, teacher,
 ):
     rows, width = x.shape
-    shard = out_own.shape[0]
+    shard = mix_own.shape[0]
     local, hidden = mix_own.shape[1] // 4, gate_own.shape[1]
     cut = hidden // LANES * LANES
+    both = local + hidden - cut
     everyone, depth = 4 * rows, 8 * shard
     low, wide = jnp.bfloat16, jnp.float32
     tiles, heads = everyone // TILE, local // HEAD_DIM
@@ -1118,7 +1149,7 @@
         forward_kernel,
         out_shape=(
             shape(depth, 4 * local),
-            shape(depth, out_own.shape[1]),
+            shape(depth, both),
             shape(depth, 2 * hidden),
             shape(depth, cut),
             shape(width, everyone),
@@ -1140,15 +1171,16 @@
             shape(8, width, kind=wide),
             shape(everyone, CONV - 1, kind=wide),
         ),
-        in_specs=[vmem] * 8 + [hbm] * 5,
+        in_specs=[vmem] * 10 + [hbm] * 3,
         out_specs=(hbm,) * 20 + (vmem,) * 2,
         scratch_shapes=[
             pltpu.VMEM((rows, 1), wide),
             pltpu.VMEM((everyone, 1), jnp.int32),
             pltpu.VMEM((tiles, 1, 2 * TILE), jnp.int32),
             pltpu.VMEM((shard, 2 * hidden), low),
+            pltpu.VMEM((shard, both), low),
             pltpu.VMEM((depth, 4 * local), low),
-            pltpu.VMEM((depth, out_own.shape[1]), low),
+            pltpu.VMEM((depth, both), low),
             pltpu.VMEM((depth, 2 * hidden), low),
             pltpu.VMEM((depth, cut), low),
             pltpu.VMEM((everyone, width), low),
@@ -1178,7 +1210,7 @@
         ],
         compiler_params=params(1),
     )(
-        x, valid_lanes, gain_one, gain_two, segments, taps, gate_own, up_own, mix_own, out_own, down_own,
+        x, valid_lanes, gain_one, gain_two, segments, taps, gate_own, up_own, output_weight, down_own, mix_own,
         cotangent, teacher,
     )
 
@@ -1198,9 +1230,9 @@
 
 def feed_backward_kernel(
     gain, dyb_in, dybt_in, h2t_in, down_in, feed_in, active_in, slopes_in, last_in, x1_in, dy_in,
-    down_grad, gate_grad, gain_part, dx1_out, dx1t_out, do_out, slopes_out,
-    dyb, dybt, h2t, down, feed, active, slopes, last, do, side, total, down_slots, gate_slots,
-    down_term, gate_term, send, receive,
+    down_grad, gate_grad, gain_part, dx1_out, dx1t_out, do_out, slopes_out, ends_out,
+    dyb, dybt, h2t, down, feed, active, slopes, last, do, x1, dy, total, down_slots, gate_slots,
+    down_term, gate_term, ends, send, receive,
     send_sems, recv_sems, load_sems, out_sems,
 ):
     at = neighbours()
@@ -1212,21 +1244,23 @@
         for n, (source, target) in enumerate(
             (
                 (dybt_in, dybt), (active_in, active), (dyb_in, dyb), (down_in, down), (slopes_in, slopes),
-                (last_in, last), (h2t_in, h2t), (feed_in, feed), (x1_in, side), (dy_in, side),
+                (last_in, last), (h2t_in, h2t), (feed_in, feed), (x1_in, x1), (dy_in, dy),
             )
         )
     ]
     for load in loads[:2]:
         load.start()
-    greet(at)
+    number = hail(at)
     hidden = active.shape[1]
     parts, main = feed_lanes(hidden)
-    tail = hidden - main
-    first = RingScatter(at, dybt, active, down_slots, down_term, down_grad, sems, 0)
+    tail, share = hidden - main, gate_slots.shape[3]
+    first = RingScatter(
+        at, dybt, active.at[:, pl.ds(0, main)], down_slots, down_term, down_grad, sems, 0
+    )
     second = RingScatter(
-        at, h2t, slopes.at[:, pl.ds(0, main)], gate_slots, gate_term, gate_grad, sems, 28
-    )
-    group = GatherTensor(at, dyb, rows, sems, 59)
+        at, h2t, slopes.at[:, pl.ds(0, share)], gate_slots, gate_term, gate_grad, sems, 28
+    )
+    group = GatherPieces(at, dyb, rows, PIECES, sems, 56)
     keeps = []
 
     def keep(source, target):
@@ -1236,68 +1270,75 @@
 
     loads[0].wait()
     loads[1].wait()
-    for load in loads[2:-1]:
+    for load in loads[2:]:
         load.start()
-    first.start()
+    first.prepare()
+    meet(number)
+    first.launch()
+    first.compute(2)
     for load in loads[2:6]:
         load.wait()
 
     def slope_back(first_block, last_block):
         @pl.loop(first_block, last_block)
         def _(j):
-            here = pl.ds(pl.multiple_of(j * rows, rows), rows)
+            here = pl.ds(pl.multiple_of(j * (rows // 2), rows // 2), rows // 2)
             left = dyb[here]
             for own, gate_lanes, up_lanes in parts:
                 da = nn_dot(left, down[:, own])
                 slopes[here, gate_lanes] = (da * slopes[here, gate_lanes].astype(jnp.float32)).astype(low)
                 slopes[here, up_lanes] = (da * slopes[here, up_lanes].astype(jnp.float32)).astype(low)
             da = nn_dot(left, last[:, pl.ds(last.shape[1] - tail, tail)])
-            ends = pl.ds(2 * main, 2 * tail)
-            both = jnp.concatenate([da, da], axis=1) * slopes[here, ends].astype(jnp.float32)
-            slopes[here, ends] = both.astype(low)
-
-    for k in range(4):
+            last_lanes = pl.ds(2 * main, 2 * tail)
+            both = jnp.concatenate([da, da], axis=1) * slopes[here, last_lanes].astype(jnp.float32)
+            slopes[here, last_lanes] = both.astype(low)
+
+    for k in range(8):
         slope_back(k, k + 1)
-        first.tick()
-    keep(slopes.at[:, pl.ds(main, 2 * hidden - main)], slopes_out)
+        if k % 2 or k > 3:
+            first.tick()
     loads[6].wait()
     second.start()
+    first.tick()
+    keep(slopes.at[:, pl.ds(share, 2 * hidden - share)], slopes_out)
+
+    @pl.loop(0, dybt.shape[0] // rows)
+    def _(j):
+        here = pl.ds(pl.multiple_of(j * rows, rows), rows)
+        ends[here] = nn_dot(dybt[here], active[:, pl.ds(main, tail)]).astype(low)
+
+    keep(ends, ends_out)
+    first.tick()
     loads[7].wait()
     loads[8].wait()
 
     def part(block):
         return nt_dot(slopes[pl.ds(pl.multiple_of(block * rows, rows), rows)], feed[...])
 
-    def idle(point):
+    def idle():
         first.tick()
         second.tick()
-        if point == 2:
-            first.tick()
-            second.tick()
-
-    sum_rows(at, part, send, receive, total, sems, 56, idle=idle)
+
     gain_part[...] = jnp.zeros_like(gain_part)
-
-    @chunks_of(rows, 32)
-    def _(row, size):
-        here = pl.ds(row, size)
-        through, term_gain = norm_back(side[here], total[here], row_of(gain))
-        gain_part[0:1] += term_gain
-        total[here] = through
-
-    loads[9].start()
-    first.tick()
-    second.tick()
     loads[9].wait()
-
-    @chunks_of(rows, 32)
-    def _(row, size):
-        here = pl.ds(row, size)
-        grad = total[here] + side[here]
-        total[here] = grad
-        dyb[pl.ds(pl.multiple_of(at["t"] * rows + row, size), size)] = grad.astype(low)
-
-    group.start()
+    piece, step = rows // PIECES, 32
+
+    def through_norm(c):
+        @pl.loop(0, piece // step)
+        def _(i):
+            row = pl.multiple_of(c * piece + i * step, step)
+            here = pl.ds(row, step)
+            through, term_gain = norm_back(x1[here], total[here], row_of(gain))
+            gain_part[0:1] += term_gain
+            grad = dy[here] + through
+            total[here] = grad
+            dyb[pl.ds(pl.multiple_of(at["t"] * rows + row, step), step)] = grad.astype(low)
+
+        group.start(c)
+
+    sum_pieces(
+        at, part, send, receive, total, sems, 56 + 3 * PIECES, PIECES, through_norm, idle=idle
+    )
     keep(total, dx1_out)
 
     def spread(block):
@@ -1310,13 +1351,13 @@
         second.tick()
     spread(at["t"])
     second.tick()
-    group.receives[0].wait_recv()
+    group.wait(0)
     spread(at["core"])
     second.tick()
     group.relay()
     second.tick()
     spread(at["cross"])
-    group.receives[2].wait_recv()
+    group.wait(2)
     spread(at["cross_core"])
     group.drain()
     keep(dybt, dx1t_out)
@@ -1331,6 +1372,7 @@
     rows, width = x1.shape
     depth, main = down.shape
     hidden = active.shape[1]
+    share = main + SHARE * LANES
     local = last.shape[1] - (hidden - main)
     everyone, shard = 4 * rows, depth // 8
     low, wide = jnp.bfloat16, jnp.float32
@@ -1338,16 +1380,17 @@
     return pl.pallas_call(
         feed_backward_kernel,
         out_shape=(
-            shape(shard, hidden, kind=wide),
             shape(shard, main, kind=wide),
+            shape(shard, share, kind=wide),
             shape(8, width, kind=wide),
             shape(rows, width, kind=wide),
             shape(width, everyone),
             shape(everyone, local),
-            shape(everyone, 2 * hidden - main),
+            shape(everyone, 2 * hidden - share),
+            shape(width, hidden - main),
         ),
         in_specs=[vmem] + [hbm] * 10,
-        out_specs=(vmem,) * 3 + (hbm,) * 4,
+        out_specs=(vmem,) * 3 + (hbm,) * 5,
         scratch_shapes=[
             pltpu.VMEM((everyone, width), low),
             pltpu.VMEM((width, everyone), low),
@@ -1360,16 +1403,18 @@
             pltpu.VMEM((everyone, local), low),
             pltpu.VMEM((rows, width), wide),
             pltpu.VMEM((rows, width), wide),
-            pltpu.VMEM((2, 8, shard // 2, hidden), low),
+            pltpu.VMEM((rows, width), wide),
             pltpu.VMEM((2, 8, shard // 2, main), low),
-            pltpu.VMEM((shard, hidden), wide),
+            pltpu.VMEM((2, 8, shard // 2, share), low),
             pltpu.VMEM((shard, main), wide),
+            pltpu.VMEM((shard, share), wide),
+            pltpu.VMEM((width, hidden - main), low),
             pltpu.VMEM((3, rows, width), low),
             pltpu.VMEM((3, rows, width), low),
-            dma(62),
-            dma(62),
+            dma(56 + 6 * PIECES),
+            dma(56 + 6 * PIECES),
             dma(10),
-            dma(4),
+            dma(5),
         ],
         compiler_params=params(3),
     )(gain, dyb, dybt, h2t, down, feed, active, slopes, last, x1, dy)
@@ -1377,11 +1422,11 @@
 
 def mixer_backward_kernel(
     x, gain, same, taps, gain_part, squares,
-    dx1t_in, o_in, h2t_in, slopes_in, q_in, k_in, v_in, u_in, p_in, do_in, mix_in, h1t_in, dx1_in,
+    dx1t_in, o_in, h2t_in, slopes_in, ends_in, q_in, k_in, v_in, u_in, p_in, do_in, mix_in, h1t_in, dx1_in,
     out_grad, up_grad, mix_grad, input_grad, small_out, conv_out,
-    turned, o, h2t, slopes, q, k_pad, v_pad, u, p, do, mix,
+    turned, o, h2t, slopes, ends, q, k_pad, v_pad, u, p, do, mix,
     dk, dv, grads, out_slots, up_slots, mix_slots, out_term, up_term, mix_term, send, receive, total,
-    small, small_in, conv, conv_in,
+    small, small_in, conv, conv_in, conv_all,
     send_sems, recv_sems, load_sems,
 ):
     at = neighbours()
@@ -1392,53 +1437,61 @@
         pltpu.make_async_copy(source, target, load_sems.at[n])
         for n, (source, target) in enumerate(
             (
-                (dx1t_in, turned), (o_in, o), (h2t_in, h2t), (slopes_in, slopes), (q_in, q), (k_in, k_pad),
+                (dx1t_in, turned), (o_in, o), (h2t_in, h2t), (slopes_in, slopes), (ends_in, ends), (q_in, q), (k_in, k_pad),
                 (v_in, v_pad), (u_in, u), (p_in, p), (do_in, do), (mix_in, mix), (dx1_in, input_grad),
                 (h1t_in, turned),
             )
         )
     ]
-    for load in loads[:4]:
+    for load in loads[:5]:
         load.start()
-    greet(at, everyone=True)
+    number = hail(at, everyone=True)
     local = q.shape[1]
     main = local // LANES * LANES
     tail = local - main
-    first = RingScatter(at, turned, o, out_slots, out_term, out_grad, sems, 0, count=1)
+    first = RingScatter(
+        at, turned, o, out_slots, out_term, out_grad, sems, 0, count=1, side=ends
+    )
     second = RingScatter(at, h2t, slopes, up_slots, up_term, up_grad, sems, 14)
     third = RingScatter(at, turned, grads, mix_slots, mix_term, mix_grad, sems, 42)
     small_sum = SumAll(at, small, small_in, sems, 73)
-    conv_all = SumAll(at, conv, conv_in, sems, 78)
+    conv_sum = SumAll(at, conv, conv_in, sems, 78, over=("mate", "z_pair", "z_mirror"))
+    conv_group = GatherTensor(at, conv_all, 1, sems, 81)
     loads[0].wait()
     loads[1].wait()
-    first.start()
+    loads[4].wait()
+    first.prepare()
+    meet(number)
+    first.launch()
     loads[2].wait()
     loads[3].wait()
-    for load in loads[4:-1]:
+    for load in loads[5:-1]:
         load.start()
-    second.start()
+    second.prepare()
+    second.launch()
+    first.compute(2)
+    second.compute(2)
     dk[...] = jnp.zeros_like(dk)
     dv[...] = jnp.zeros_like(dv)
     conv[0] = jnp.zeros(conv.shape[1:], jnp.float32)
     first.tick()
-    for load in loads[4:10]:
+    for load in loads[5:11]:
         load.wait()
     tiles = q.shape[0] // TILE
-    conv_sum = conv.at[0, at["t"]]
 
     def attend(a, b):
         @pl.loop(a, b)
         def _(i):
-            attend_back_tile(i, q, k_pad, v_pad, u, p, same, taps, do, dk, dv, conv_sum)
+            attend_back_tile(i, q, k_pad, v_pad, u, p, same, taps, do, dk, dv, conv.at[0])
 
     for k in range(8):
         attend(k * tiles // 8, (k + 1) * tiles // 8)
         first.tick()
         second.tick()
-    conv_all.start()
+    conv_sum.start()
 
     first.finish()
-    loads[12].start()
+    loads[13].start()
     second.tick()
 
     @chunks_of(q.shape[0])
@@ -1447,14 +1500,14 @@
         four = [q[here].astype(jnp.float32), dk[there], dv[there], do[here].astype(jnp.float32)]
         for n, value in enumerate(four):
             grads[here, pl.ds(n * main, main)] = value[:, :main].astype(low)
-        ends = jnp.concatenate([value[:, main:] for value in four], axis=1)
-        grads[here, pl.ds(4 * main, 4 * tail)] = ends.astype(low)
+        lasts = jnp.concatenate([value[:, main:] for value in four], axis=1)
+        grads[here, pl.ds(4 * main, 4 * tail)] = lasts.astype(low)
 
     second.tick()
+    loads[13].wait()
+    third.start()
+    loads[11].wait()
     loads[12].wait()
-    third.start()
-    loads[10].wait()
-    loads[11].wait()
 
     def part(block):
         return nt_dot(grads[pl.ds(pl.multiple_of(block * rows, rows), rows)], mix[...])
@@ -1464,78 +1517,82 @@
         third.tick()
         if point == 2:
             second.tick()
-            conv_all.step()
+        conv_sum.step()
 
     sum_rows(at, part, send, receive, total, sems, 70, idle=idle)
-    small[0, 0:1] = jnp.zeros((1, small.shape[2]), jnp.float32)
-    small[0, 1:2] = gain_part[0:1]
-    small[0, 2:3] = squares[0:1]
-    small[0, 3:8] = jnp.zeros((5, small.shape[2]), jnp.float32)
+    conv_sum.finish()
+    conv_all[at["t"]] = conv[3]
+    conv_group.start()
+    small[0, 0] = jnp.zeros((1, small.shape[3]), jnp.float32)
+    small[0, 1] = gain_part[0:1]
+    small[0, 2] = squares[0:1]
 
     @chunks_of(rows, 32)
     def _(row, size):
         here = pl.ds(row, size)
         through, term_gain = norm_back(x[here].astype(jnp.float32), total[here], row_of(gain))
-        small[0, 0:1] += term_gain
+        small[0, 0] += term_gain
         input_grad[here] += through
 
     small_sum.start()
     second.finish()
     for k in range(5):
         third.tick()
-        if k > 0:
-            conv_all.step()
         third.tick()
         small_sum.step()
+        if k == 1:
+            conv_group.relay()
+    conv_group.finish()
     third.finish()
     small_sum.finish()
-    conv_all.finish()
     small_out[...] = small[5]
-    conv_out[...] = conv[5]
+    conv_out[...] = conv_all[...]
 
 
 def mixer_backward(
-    x, gain, same, taps, gain_part, squares, dx1t, o, h2t, slopes, q, k_pad, v_pad, u, p, do, mix, h1t, dx1
+    x, gain, same, taps, gain_part, squares, dx1t, o, h2t, slopes, ends, q, k_pad, v_pad, u, p, do, mix, h1t, dx1
 ):
     rows, width = x.shape
     everyone, local = o.shape
     shard, ups = width // 8, slopes.shape[1]
+    both = local + ends.shape[1]
     low, wide = jnp.bfloat16, jnp.float32
     vmem, hbm = specs()
-    arrays = (dx1t, o, h2t, slopes, q, k_pad, v_pad, u, p, do, mix)
+    arrays = (dx1t, o, h2t, slopes, ends, q, k_pad, v_pad, u, p, do, mix)
     return pl.pallas_call(
         mixer_backward_kernel,
         out_shape=(
-            shape(shard, local, kind=wide),
+            shape(shard, both, kind=wide),
             shape(shard, ups, kind=wide),
             shape(shard, 4 * local, kind=wide),
             shape(rows, width, kind=wide),
-            shape(8, width, kind=wide),
-            shape(4, 8, local, kind=wide),
+            shape(CONV, 1, width, kind=wide),
+            shape(4, CONV, 1, local, kind=wide),
         ),
-        in_specs=[vmem] * 6 + [hbm] * 13,
+        in_specs=[vmem] * 6 + [hbm] * 14,
         out_specs=(vmem,) * 6,
         scratch_shapes=[pltpu.VMEM(array.shape, array.dtype) for array in arrays]
         + [
             pltpu.VMEM((everyone + TILE, local), wide),
             pltpu.VMEM((everyone + TILE, local), wide),
             pltpu.VMEM((everyone, 4 * local), low),
-            pltpu.VMEM((2, 8, shard // 2, local), low),
+            pltpu.VMEM((2, 8, shard // 2, both), low),
             pltpu.VMEM((2, 8, shard // 2, ups), low),
             pltpu.VMEM((2, 8, shard // 2, 4 * local), low),
-            pltpu.VMEM((shard, local), wide),
+            pltpu.VMEM((shard, both), wide),
             pltpu.VMEM((shard, ups), wide),
             pltpu.VMEM((shard, 4 * local), wide),
             pltpu.VMEM((3, rows, width), low),
             pltpu.VMEM((3, rows, width), low),
             pltpu.VMEM((rows, width), wide),
-            pltpu.VMEM((6, 8, width), wide),
-            pltpu.VMEM((5, 8, width), wide),
-            pltpu.VMEM((6, 4, 8, local), wide),
-            pltpu.VMEM((5, 4, 8, local), wide),
-            dma(83),
-            dma(83),
-            dma(13),
+            pltpu.VMEM((6, 3, 1, width), wide),
+            pltpu.VMEM((5, 3, 1, width), wide),
+            pltpu.VMEM((4, CONV, 1, local), wide),
+            pltpu.VMEM((3, CONV, 1, local), wide),
+            pltpu.VMEM((4, CONV, 1, local), wide),
+            dma(84),
+            dma(84),
+            dma(14),
         ],
         compiler_params=params(4),
     )(x, gain, same, taps, gain_part, squares, *arrays, h1t, dx1)
@@ -1553,27 +1610,31 @@
     for n, target in enumerate((query, key, value, mixgate)):
         target[:, pl.ds(0, main)] = mix_grad[:, pl.ds(n * main, main)]
         target[:, pl.ds(main, tail)] = mix_grad[:, pl.ds(4 * main, 4 * tail)][:, n * tail : (n + 1) * tail]
-    cut = gate_main.shape[1]
-    rest = gate.shape[1] - cut
-    ends = up_rest[:, pl.ds(cut, 2 * rest)]
-    gate[:, pl.ds(0, cut)] = gate_main[...]
+    cut = gate.shape[1] // LANES * LANES
+    rest, early = gate.shape[1] - cut, gate_main.shape[1] - cut
+    late = cut - early
+    ends = up_rest[:, pl.ds(late, 2 * rest)]
+    gate[:, pl.ds(0, cut)] = gate_main[:, pl.ds(0, cut)]
     gate[:, pl.ds(cut, rest)] = ends[:, :rest]
-    up[:, pl.ds(0, cut)] = up_rest[:, pl.ds(0, cut)]
+    up[:, pl.ds(0, early)] = gate_main[:, pl.ds(cut, early)]
+    up[:, pl.ds(early, late)] = up_rest[:, pl.ds(0, late)]
     up[:, pl.ds(cut, rest)] = ends[:, rest:]
-    output[...] = out_grad[...].T
-    down[...] = down_grad[...]
-    conv_grad[...] = jnp.concatenate([conv[n, 0:CONV] for n in range(conv.shape[0])], axis=1)
-    gain_one[...] = small[0]
-    gain_two[...] = small[1]
-    total = jnp.sum(small[2:3], axis=1, keepdims=True) / (count[0:1, 0:1] * D)
+    output[...] = out_grad[:, pl.ds(0, local)].T
+    down[:, pl.ds(0, cut)] = down_grad[...]
+    down[:, pl.ds(cut, rest)] = out_grad[:, pl.ds(local, rest)]
+    for m in range(CONV):
+        conv_grad[m : m + 1] = jnp.concatenate([conv[n, m] for n in range(conv.shape[0])], axis=1)
+    gain_one[...] = small[0, 0]
+    gain_two[...] = small[1, 0]
+    total = jnp.sum(small[2], axis=1, keepdims=True) / (count[0:1, 0:1] * D)
     loss[...] = total
 
 
 def finish(count, down_grad, gate_main, up_rest, mix_grad, out_grad, small, conv, act, input_grad):
     vmem, _ = specs()
     wide = jnp.float32
-    shard, hidden = down_grad.shape
-    local, width = out_grad.shape[1], small.shape[1]
+    shard, width = gate_main.shape[0], small.shape[2]
+    hidden, local = (gate_main.shape[1] + up_rest.shape[1]) // 2, mix_grad.shape[1] // 4
     square = shape(shard, local, kind=wide)
     broad = shape(shard, hidden, kind=wide)
     return pl.pallas_call(
@@ -1625,22 +1686,19 @@
 ):
     local = query_weight.shape[1]
     taps = lax.dynamic_slice_in_dim(conv_weight, lax.axis_index("tensor") * local, local, 1)
-    cut = down_weight.shape[0] // LANES * LANES
-    down_own = down_weight.T
     (
         mix, last, feed, down, h1t, h2t, dybt, q, k_pad, v_pad, u, p, o, x1, dyb, slopes, active,
         outputs, dy, count, squares, same,
     ) = forward(
         block_input, valid_mask.reshape(-1, LANES), gain_mixer, gain_feed, segments.reshape(-1, LANES), taps,
         pack(query_weight, key_weight, value_weight, mixgate_weight),
-        jnp.concatenate([output_weight.T, down_own[:, cut:]], axis=1), gate_weight, up_weight, down_own,
-        cotangent, teacher,
-    )
-    down_grad, gate_main, gain_part, dx1, dx1t, do, slopes_up = feed_backward(
+        output_weight, gate_weight, up_weight, down_weight.T, cotangent, teacher,
+    )
+    down_grad, gate_main, gain_part, dx1, dx1t, do, slopes_up, ends = feed_backward(
         gain_feed, dyb, dybt, h2t, down, feed, active, slopes, last, x1, dy
     )
     out_grad, up_rest, mix_grad, input_grad, small, conv = mixer_backward(
-        block_input, gain_mixer, same, taps, gain_part, squares, dx1t, o, h2t, slopes_up, q, k_pad, v_pad,
+        block_input, gain_mixer, same, taps, gain_part, squares, dx1t, o, h2t, slopes_up, ends, q, k_pad, v_pad,
         u, p, do, mix, h1t, dx1,
     )
     loss, *rest, down_turned = finish(

time: 512 us -> 505 us (0.986)
    pallas_call x2, Pallas kernels: 232 us -> 226 us  [the longest x1 129 us: mixer_backward(): pl.pallas_call(mixer_backward_kernel, out_shape=(shape(shard, both, kind=...]
where the time goes in v6:
time: 505 us; the launch traced here: 499 us
  Pallas kernels  495 us (98%)
    pallas_call x1, Pallas kernels, forward(): pl.pallas_call(forward_kernel, out_shape=(shape(depth, 4 * local), shape(...  261 us
    pallas_call x1, Pallas kernels, mixer_backward(): pl.pallas_call(mixer_backward_kernel, out_shape=(shape(shard, both, kind=...  129 us
    pallas_call x1, Pallas kernels, feed_backward(): pl.pallas_call(feed_backward_kernel, out_shape=(shape(shard, main, kind=w...  96.9 us

profile of v6, /device:TPU:0, one launch (start us, length us, event | category | flops | bytes accessed | tf_op | source)
XLA Modules:
  0.0 498.6 jit_solution(14711981654777393418)
XLA Ops:
  0.6 0.0 copy-start
  0.7 0.0 slice-start.6
  0.7 0.0 slice-start.7
  0.7 0.0 slice-start.4
  0.7 0.0 slice-start.5
  0.7 0.0 slice-start.2
  0.7 0.0 slice-start.3
  0.7 0.0 slice-start
  0.7 0.0 slice-start.1
  0.8 0.7 copy-done
  1.4 0.7 constant_dynamic-slice_fusion.taps
  2.1 0.0 slice-done.6
  2.1 0.0 slice-done.7
  2.1 0.0 slice-done.4
  2.1 0.0 slice-done.5
  2.1 0.0 slice-done.2
  2.1 0.0 slice-done.3
  2.1 0.0 slice-done
  2.1 0.0 slice-done.1
  2.1 1.1 concatenate.3.mix_own
  3.2 260.9 %shard_map.263 = (bf16[1792,1792]{1,0:T(8,128)(2,1)}, bf16[1792,512]{1,0:T(8,128)(2,1)}, bf16[1792,2432]{1,0:T(8,128)(2,1)}, bf16[1792,1152]{1,0:T(8,128)(2,1)},...) custom-call(bf16[256,1792]{1,0:T(8,128)(2,1)} %x.3, ...), custom_call_target="tpu_custom_call" | custom-call | tf_op jit(solution)/shard_map/pallas_call | solution.py:1148
  264.1 96.9 %shard_map.264 = (f32[224,1152]{1,0:T(8,128)}, f32[224,1408]{1,0:T(8,128)}, f32[8,1792]{1,0:T(8,128)}, f32[256,1792]{1,0:T(8,128)}, bf16[1792,1024]{1,0:T(8,128)...) custom-call(f32[1792]{0:T(1024)} %gain.2, ...), custom_call_target="tpu_custom_call" | custom-call | tf_op jit(solution)/shard_map/pallas_call | solution.py:1380
  361.0 129.5 %shard_map.265 = (f32[224,512]{1,0:T(8,128)}, f32[224,1024]{1,0:T(8,128)}, f32[224,1792]{1,0:T(8,128)}, f32[256,1792]{1,0:T(8,128)}, f32[3,1,1792]{2,1,0:T(1,128)}, /*index=5*/f32[4,3,1,448]{3,2,1,0:T(1,128)}) custom-call(bf16[256,1792]{1,0:T(8,128)(2,1)} %x.3, f32[1792]{0:T(1024)} %gain.3, f32[1024,2]{1,0:T(8,128)} %get-tuple-element.77.same, ...), custom_call_target="tpu_custom_call" | custom-call | tf_op jit(solution)/shard_map/pallas_call | solution.py:1562
  490.5 0.0 copy-start.1
  490.5 7.6 %shard_map.266 = (f32[1,1]{1,0:T(1,128)}, f32[256,1792]{1,0:T(8,128)}, f32[256,1792]{1,0:T(8,128)}, f32[224,448]{1,0:T(8,128)}, f32[224,448]{1,0:T(8,128)}, /*in...) custom-call(f32[8,128]{1,0:T(8,128)} %get-tuple-element.64.count, ...), custom_call_target="tpu_custom_call" | custom-call | tf_op jit(solution)/shard_map/pallas_call | solution.py:1640
  498.1 0.0 copy-done.1
Async XLA Ops:
  0.6 0.8 copy-start
  0.7 1.4 slice-start.6
  0.7 1.4 slice-start.7
  0.7 1.4 slice-start.4
  0.7 1.4 slice-start.5
  0.7 1.4 slice-start.2
  0.7 1.4 slice-start.3
  0.7 1.4 slice-start
  0.7 1.4 slice-start.1
  490.5 7.6 %copy-start.1 = (f32[3,1792]{1,0:T(4,128)S(1)}, f32[3,1792]{1,0:T(4,128)}, u32[]{:S(2)}) copy-start(f32[3,1792]{1,0:T(4,128)} %param.26) | copy-start | bytes 64516

commit v7 on v6

--- a/solution.py
+++ b/solution.py
@@ -840,10 +840,10 @@
 
 def forward_kernel(
     x, valid_lanes, gain_one, gain_two, segments, taps,
-    gate_own, up_own, out_turned, down_own, mix_own, cotangent_in, teacher_in,
+    gate_in, up_in, out_in, down_in, mix_own, cotangent_in, teacher_in,
     mix_out, last_out, feed_out, down_out, h1t_out, h2t_out, dybt_out, q_out, k_out, v_out, u_out, p_out,
     o_out, x1_out, dyb_out, slopes_out, active_out, act_out, dy_out, count_out, squares_out, same,
-    valid, seg_q, seg_k, feed_own, out_own, mix, last, feed, down, h1, turned, h2, q, k_pad, v_pad, u, p, o, slopes, active, x1, side, teacher,
+    valid, seg_q, seg_k, gate_own, up_own, out_turned, down_own, feed_own, out_own, mix, last, feed, down, h1, turned, h2, q, k_pad, v_pad, u, p, o, slopes, active, x1, side, teacher,
     send, receive, total, count, count_in,
     send_sems, recv_sems, local_sems, load_sems, out_sems,
 ):
@@ -905,14 +905,22 @@
     counting.start()
     load_teacher = pltpu.make_async_copy(teacher_in, teacher, load_sems.at[0])
     load_cotangent = pltpu.make_async_copy(cotangent_in, side, load_sems.at[1])
-    load_teacher.start()
-    load_cotangent.start()
+    raw = [
+        pltpu.make_async_copy(source, target, load_sems.at[2 + n])
+        for n, (source, target) in enumerate(
+            ((gate_in, gate_own), (up_in, up_own), (out_in, out_turned), (down_in, down_own))
+        )
+    ]
+    for load in raw + [load_teacher, load_cotangent]:
+        load.start()
     k_pad[pl.ds(0, TILE)] = jnp.zeros((TILE, local), k_pad.dtype)
     v_pad[pl.ds(0, TILE)] = jnp.zeros((TILE, local), v_pad.dtype)
     make_tables(segments, seg_q, seg_k, same)
     width = gate_own.shape[1]
     cut = width // LANES * LANES
     rest = width - cut
+    for load in raw:
+        load.wait()
     feed_own[:, pl.ds(0, cut)] = gate_own[:, pl.ds(0, cut)]
     feed_own[:, pl.ds(cut, cut)] = up_own[:, pl.ds(0, cut)]
     ends = [own[:, pl.ds(cut, rest)].astype(jnp.float32) for own in (gate_own, up_own)]
@@ -999,6 +1007,7 @@
     def idle(point):
         tick()
         if point == 2:
+            tick()
             tick()
 
     sum_rows(at, mixed_part, send, receive, total, sems, 107, idle=idle)
@@ -1171,12 +1180,16 @@
             shape(8, width, kind=wide),
             shape(everyone, CONV - 1, kind=wide),
         ),
-        in_specs=[vmem] * 10 + [hbm] * 3,
+        in_specs=[vmem] * 6 + [hbm] * 7,
         out_specs=(hbm,) * 20 + (vmem,) * 2,
         scratch_shapes=[
             pltpu.VMEM((rows, 1), wide),
             pltpu.VMEM((everyone, 1), jnp.int32),
             pltpu.VMEM((tiles, 1, 2 * TILE), jnp.int32),
+            pltpu.VMEM((shard, hidden), low),
+            pltpu.VMEM((shard, hidden), low),
+            pltpu.VMEM(output_weight.shape, low),
+            pltpu.VMEM((shard, hidden), low),
             pltpu.VMEM((shard, 2 * hidden), low),
             pltpu.VMEM((shard, both), low),
             pltpu.VMEM((depth, 4 * local), low),
@@ -1205,7 +1218,7 @@
             dma(115 + 6 * PIECES),
             dma(115 + 6 * PIECES),
             dma(4),
-            dma(2),
+            dma(6),
             dma(26),
         ],
         compiler_params=params(1),
@@ -1516,7 +1529,9 @@
         second.tick()
         third.tick()
         if point == 2:
-            second.tick()
+            for _ in range(3):
+                second.tick()
+                third.tick()
         conv_sum.step()
 
     sum_rows(at, part, send, receive, total, sems, 70, idle=idle)
@@ -1538,7 +1553,8 @@
     second.finish()
     for k in range(5):
         third.tick()
-        third.tick()
+        if k < 3:
+            third.tick()
         small_sum.step()
         if k == 1:
             conv_group.relay()

time: 505 us -> 504 us (level)
  no operation moved by 1% of the time
where the time goes in v7:
time: 504 us; the launch traced here: 497 us
  Pallas kernels  493 us (98%)
    pallas_call x1, Pallas kernels, forward(): pl.pallas_call(forward_kernel, out_shape=(shape(depth, 4 * local), shape(...  260 us
    pallas_call x1, Pallas kernels, mixer_backward(): pl.pallas_call(mixer_backward_kernel, out_shape=(shape(shard, both, kind=...  130 us
    pallas_call x1, Pallas kernels, feed_backward(): pl.pallas_call(feed_backward_kernel, out_shape=(shape(shard, main, kind=w...  96.5 us

profile of v7, /device:TPU:0, one launch (start us, length us, event | category | flops | bytes accessed | tf_op | source)
XLA Modules:
  0.0 497.2 jit_solution(1513679036833635720)
XLA Ops:
  0.6 0.0 copy-start
  0.7 0.0 slice-start.6
  0.7 0.0 slice-start.7
  0.7 0.0 slice-start.4
  0.7 0.0 slice-start.5
  0.7 0.0 slice-start.2
  0.7 0.0 slice-start.3
  0.7 0.0 slice-start
  0.7 0.0 slice-start.1
  0.8 0.7 copy-done
  1.4 0.7 constant_dynamic-slice_fusion.taps
  2.1 0.0 slice-done.6
  2.1 0.0 slice-done.7
  2.1 0.0 slice-done.4
  2.1 0.0 slice-done.5
  2.1 0.0 slice-done.2
  2.1 0.0 slice-done.3
  2.1 0.0 slice-done
  2.1 0.0 slice-done.1
  2.1 1.1 concatenate.3.mix_own
  3.2 259.6 %shard_map.263 = (bf16[1792,1792]{1,0:T(8,128)(2,1)}, bf16[1792,512]{1,0:T(8,128)(2,1)}, bf16[1792,2432]{1,0:T(8,128)(2,1)}, bf16[1792,1152]{1,0:T(8,128)(2,1)},...) custom-call(bf16[256,1792]{1,0:T(8,128)(2,1)} %x.3, ...), custom_call_target="tpu_custom_call" | custom-call | tf_op jit(solution)/shard_map/pallas_call | solution.py:1157
  262.8 96.5 %shard_map.264 = (f32[224,1152]{1,0:T(8,128)}, f32[224,1408]{1,0:T(8,128)}, f32[8,1792]{1,0:T(8,128)}, f32[256,1792]{1,0:T(8,128)}, bf16[1792,1024]{1,0:T(8,128)...) custom-call(f32[1792]{0:T(1024)} %gain.2, ...), custom_call_target="tpu_custom_call" | custom-call | tf_op jit(solution)/shard_map/pallas_call | solution.py:1393
  359.4 129.7 %shard_map.265 = (f32[224,512]{1,0:T(8,128)}, f32[224,1024]{1,0:T(8,128)}, f32[224,1792]{1,0:T(8,128)}, f32[256,1792]{1,0:T(8,128)}, f32[3,1,1792]{2,1,0:T(1,128)}, /*index=5*/f32[4,3,1,448]{3,2,1,0:T(1,128)}) custom-call(bf16[256,1792]{1,0:T(8,128)(2,1)} %x.3, f32[1792]{0:T(1024)} %gain.3, f32[1024,2]{1,0:T(8,128)} %get-tuple-element.77.same, ...), custom_call_target="tpu_custom_call" | custom-call | tf_op jit(solution)/shard_map/pallas_call | solution.py:1578
  489.1 0.0 copy-start.1
  489.1 7.6 %shard_map.266 = (f32[1,1]{1,0:T(1,128)}, f32[256,1792]{1,0:T(8,128)}, f32[256,1792]{1,0:T(8,128)}, f32[224,448]{1,0:T(8,128)}, f32[224,448]{1,0:T(8,128)}, /*in...) custom-call(f32[8,128]{1,0:T(8,128)} %get-tuple-element.64.count, ...), custom_call_target="tpu_custom_call" | custom-call | tf_op jit(solution)/shard_map/pallas_call | solution.py:1656
  496.7 0.0 copy-done.1
Async XLA Ops:
  0.6 0.8 copy-start
  0.7 1.4 slice-start.6
  0.7 1.4 slice-start.7
  0.7 1.4 slice-start.4
  0.7 1.4 slice-start.5
  0.7 1.4 slice-start.2
  0.7 1.4 slice-start.3
  0.7 1.4 slice-start
  0.7 1.4 slice-start.1
  489.1 7.6 %copy-start.1 = (f32[3,1792]{1,0:T(4,128)S(1)}, f32[3,1792]{1,0:T(4,128)}, u32[]{:S(2)}) copy-start(f32[3,1792]{1,0:T(4,128)} %param.26) | copy-start | bytes 64516
